TPU v7x, 256 devices: a whole 4x4x8 slice. The times are simulated.
256 devices in a mesh: dp: 16 (over x, y_hi, core), blk: 16 (over y_lo, z).
Axes of the slice: x: 4, y: 4 (y_hi: 2, y_lo: 2; y = y_hi * 2 + y_lo), z: 8, core: 2. Of those that a mesh axis runs over, the one named last changes fastest.
Arguments:
- queries: bfloat16 [16, 2048, 4096], P('dp', 'blk'), may hold values from -24 to 24
- response_key_rows: bfloat16 [16, 2048, 512], P('dp', 'blk'), may hold values from -6 to 6
- response_value_rows: bfloat16 [16, 2048, 512], P('dp', 'blk'), may hold values from -6 to 6
- prompt_keys: bfloat16 [16, 1024, 512], P('dp', 'blk'), may hold values from -24 to 24
- prompt_value_rows: bfloat16 [16, 1024, 512], P('dp', 'blk'), may hold values from -6 to 6
- output_gradient: bfloat16 [16, 2048, 4096], P('dp', 'blk'), may hold values from -256 to 256
- prompt_owner: int32 [16], replicated, may hold values from 0 to 15, each once
- response_prompt: int32 [16], replicated, may hold values from 0 to 15
- lengths: int32 [16], replicated, may hold values from 1 to 2048, 17408 in all
- half_blocks: int32 [32], replicated, may hold values from 0 to 31, each once
Outputs:
- attn_out: bfloat16 [16, 2048, 4096], P('dp', 'blk')
- prompt_key_grad: float32 [16, 1024, 512], P('dp', 'blk')
- prompt_value_grad: float32 [16, 1024, 512], P('dp', 'blk')
Inputs may be any that keep to these rules, and one draw needn't show every extreme that they name: `prompt_owner`: A permutation of the owner rows. `response_prompt`: several responses may share a prompt; some prompts have none. `lengths`: some response has the full length 2048. `half_blocks`: A permutation of the 2 * 16 position blocks.
All inputs are finite; a program needn't handle non-finite values.
Results may differ from a plain program's by a relative error of at most 0.006.
Values may be sent and summed in bfloat16 or wider, within the bound.
A program may use at most 192 MiB of HBM per device.

v0:
```python
import jax
import jax.numpy as jnp
from jax import lax
from jax.sharding import PartitionSpec as P

QUERY_HEADS = 32
KEY_VALUE_HEADS = 4
HEAD_WIDTH = 128


NEGATIVE_LIMIT = -1e30
EXACT = lax.Precision.HIGHEST


def block_positions(half_blocks, first_part, item_count, half_rows):
    index = first_part + jnp.arange(item_count, dtype=jnp.int32)
    which = index // half_rows
    table = jnp.arange(half_blocks.shape[0], dtype=jnp.int32)
    picked = jnp.sum(jnp.where(which[:, None] == table[None, :], half_blocks[None, :], 0), axis=1)
    return picked * half_rows + index % half_rows


def absorb(state, query_rows, key_rows, value_rows, visible):
    peak, total, mixed = state
    scale = HEAD_WIDTH ** (-0.5)
    scores = (
        jnp.einsum(
            "rhgd,khd->hgrk",
            query_rows,
            key_rows.reshape(key_rows.shape[0], KEY_VALUE_HEADS, HEAD_WIDTH),
            preferred_element_type=jnp.float32,
        )
        * scale
    )
    masked = jnp.where(visible[None, None], scores, NEGATIVE_LIMIT)
    fresh = jnp.maximum(peak, jnp.max(masked, -1))
    weights = jnp.where(visible[None, None], jnp.exp(scores - fresh[..., None]), 0.0)
    factor = jnp.exp(peak - fresh)
    total = total * factor + jnp.sum(weights, -1)
    narrow = weights.astype(jnp.bfloat16)
    mixed = mixed * factor[..., None] + jnp.einsum(
        "hgrk,khd->hgrd",
        narrow,
        value_rows.reshape(value_rows.shape[0], KEY_VALUE_HEADS, HEAD_WIDTH),
        preferred_element_type=jnp.float32,
    )
    return (fresh, total, mixed)


def on_device(
    queries,
    response_key_rows,
    response_value_rows,
    prompt_keys,
    prompt_value_rows,
    output_gradient,
    prompt_owner,
    response_prompt,
    lengths,
    half_blocks,
):
    rank_here = lax.axis_index("dp")
    block_here = lax.axis_index("blk")
    count_of_rows = queries.shape[1]
    half_rows = count_of_rows // 2
    head_group = QUERY_HEADS // KEY_VALUE_HEADS
    slice_width = KEY_VALUE_HEADS * HEAD_WIDTH
    scale = HEAD_WIDTH ** (-0.5)
    owned_row_index = prompt_owner[response_prompt[rank_here]]
    length = lengths[rank_here]
    query_rows = queries[0].reshape(count_of_rows, KEY_VALUE_HEADS, head_group, HEAD_WIDTH)
    query_wide = query_rows.astype(jnp.float32)
    query_pos = block_positions(half_blocks, block_here * count_of_rows, count_of_rows, half_rows)
    blank = jnp.zeros(prompt_keys.shape[1:], jnp.bfloat16)
    chosen = (blank, blank)
    pieces = (
        lax.all_gather(prompt_keys, "dp", axis=0, tiled=True),
        lax.all_gather(prompt_value_rows, "dp", axis=0, tiled=True),
    )
    start = jnp.int32(0)
    item_count = pieces[0].shape[0]
    offset = jnp.clip(owned_row_index, 0, item_count - 1)
    inside = (owned_row_index >= start) & (owned_row_index < start + item_count)
    own_keys, own_values = tuple(
        (
            jnp.where(inside, lax.dynamic_index_in_dim(piece, offset, 0, keepdims=False), older)
            for piece, older in zip(pieces, chosen)
        )
    )
    combined_keys, combined_values = (
        lax.all_gather(own_keys, "blk", axis=0, tiled=True),
        lax.all_gather(own_values, "blk", axis=0, tiled=True),
    )
    prompt_len = combined_keys.shape[0]
    state = (
        jnp.full((KEY_VALUE_HEADS, head_group, count_of_rows), NEGATIVE_LIMIT, jnp.float32),
        jnp.zeros((KEY_VALUE_HEADS, head_group, count_of_rows), jnp.float32),
        jnp.zeros((KEY_VALUE_HEADS, head_group, count_of_rows, HEAD_WIDTH), jnp.float32),
    )
    state = absorb(
        state,
        query_rows,
        combined_keys,
        combined_values,
        jnp.ones((count_of_rows, prompt_len), jnp.bool_),
    )
    pieces = (
        lax.all_gather(response_key_rows, "blk", axis=1, tiled=True),
        lax.all_gather(response_value_rows, "blk", axis=1, tiled=True),
    )
    key_rows = pieces[0][0]
    value_rows = pieces[1][0]
    item_count = key_rows.shape[0]
    key_pos = block_positions(half_blocks, jnp.int32(0), item_count, half_rows)
    visible = (key_pos[None, :] <= query_pos[:, None]) & (key_pos[None, :] < length)
    peak, total, mixed = absorb(state, query_rows, key_rows, value_rows, visible)
    output = mixed / total[..., None]
    log_total = peak + jnp.log(total)
    output_cotangent = output_gradient[0].reshape(
        count_of_rows, KEY_VALUE_HEADS, head_group, HEAD_WIDTH
    )
    delta = jnp.sum(jnp.transpose(output_cotangent, (1, 2, 0, 3)).astype(jnp.float32) * output, -1)
    attn_out = (
        jnp.transpose(output, (2, 0, 1, 3))
        .reshape(1, count_of_rows, QUERY_HEADS * HEAD_WIDTH)
        .astype(jnp.bfloat16)
    )
    item_count = lax.axis_size("blk") * own_keys.shape[0]
    key_rows = combined_keys.reshape(item_count, KEY_VALUE_HEADS, HEAD_WIDTH)
    value_rows = combined_values.reshape(item_count, KEY_VALUE_HEADS, HEAD_WIDTH)
    scores = (
        jnp.einsum("rhgd,khd->hgrk", query_rows, key_rows, preferred_element_type=jnp.float32)
        * scale
    )
    probs = jnp.exp(scores - log_total[..., None])
    value_gradient = jnp.einsum(
        "hgrk,rhgd->khd",
        probs.astype(jnp.bfloat16),
        output_cotangent,
        preferred_element_type=jnp.float32,
    )
    back = jnp.einsum(
        "rhgd,khd->hgrk", output_cotangent, value_rows, preferred_element_type=jnp.float32
    )
    slopes = probs * (back - delta[..., None])
    key_gradient = (
        jnp.einsum(
            "hgrk,rhgd->khd",
            slopes,
            query_wide,
            precision=EXACT,
            preferred_element_type=jnp.float32,
        )
        * scale
    )
    share = lax.psum_scatter(
        jnp.stack(
            [
                key_gradient.reshape(item_count, slice_width),
                value_gradient.reshape(item_count, slice_width),
            ],
            axis=1,
        ),
        "blk",
        scatter_dimension=0,
        tiled=True,
    )
    zero_index = jnp.zeros((), jnp.int32)
    slots = jnp.zeros((lax.axis_size("dp"),) + share.shape, jnp.float32)
    slots = lax.dynamic_update_slice(
        slots, share[None], (owned_row_index, zero_index, zero_index, zero_index)
    )
    summed = lax.psum_scatter(slots, "dp", scatter_dimension=0, tiled=True)
    return (attn_out, summed[:, :, 0, :], summed[:, :, 1, :])


def solution(mesh):
    placed = (
        P("dp", "blk", None),
        P("dp", "blk", None),
        P("dp", "blk", None),
        P("dp", "blk", None),
        P("dp", "blk", None),
        P("dp", "blk", None),
        P(),
        P(),
        P(),
        P(),
    )
    return jax.shard_map(
        on_device,
        mesh=mesh,
        in_specs=placed,
        out_specs=(P("dp", "blk", None), P("dp", "blk", None), P("dp", "blk", None)),
        check_vma=False,
    )
```

profile of v0, /device:TPU:1, one launch (start us, length us, event | category | flops | bytes accessed | tf_op | source)
XLA Modules:
  0.0 625.8 jit_solution(8382402992058754606)
XLA Ops:
  7.2 0.0 all-gather.9.cloned.1.call-start
  7.2 0.7 all-gather.9.cloned.1.call-update
  7.9 0.0 all-gather.11.cloned.1.call-start
  7.9 0.7 all-gather.11.cloned.1.call-update
  8.6 0.0 all-gather.17.cloned.1.call-start
  8.7 1.2 dynamic_slice.16
  11.9 1.3 dynamic_slice.17
  15.0 50.0 %all-gather.9.cloned.1.call-done = bf16[16,64,512]{2,1,0:T(8,128)(2,1)} async-done(((bf16[1,64,512]{2,1,0:T(8,128)(2,1)}), bf16[16,64,512]{2,1,0:T(8,128)(2,1)}) %all-gather.9.cloned.1.call-update) | async-done | bytes 1048592 | tf_op jit(solution)/shard_map/all_gather | solution.py:77
  65.0 1.5 dynamic-slice_select_fusion.1
  66.5 0.0 all-gather.17.cloned.1.call-update
  66.5 0.0 all-gather.13.cloned.1.call-start
  66.6 1.7 copy.67
  68.2 0.0 all-gather.13.cloned.1.call-update
  68.3 0.0 all-gather.19.cloned.1.call-start
  68.3 48.3 %all-gather.11.cloned.1.call-done = bf16[16,64,512]{2,1,0:T(8,128)(2,1)} async-done(((bf16[1,64,512]{2,1,0:T(8,128)(2,1)}), bf16[16,64,512]{2,1,0:T(8,128)(2,1)}) %all-gather.11.cloned.1.call-update) | async-done | bytes 1048592 | tf_op jit(solution)/shard_map/all_gather | solution.py:78
  116.7 1.5 dynamic-slice_select_fusion
  118.1 0.0 all-gather.19.cloned.1.call-update
  118.2 0.0 all-gather.15.cloned.1.call-start
  118.2 0.5 all-gather.15.cloned.1.call-update
  118.7 0.0 reduce-scatter.3.cloned.1.call-start
  118.8 1.6 copy.99
  120.4 1.3 dynamic_slice.20
  121.7 0.8 select_reduce_fusion
  122.5 0.6 broadcast_compare_fusion
  123.1 0.7 select_reduce_fusion.1
  123.9 1.6 copy.72
  125.5 1.5 compare_and_fusion
  127.0 49.3 %all-gather.17.cloned.1.call-done = bf16[1,1024,512]{2,1,0:T(8,128)(2,1)} async-done(((bf16[1,64,512]{2,1,0:T(8,128)(2,1)}), bf16[1,1024,512]{2,1,0:T(8,128)(2,1)}) %all-gather.17.cloned.1.call-update) | async-done | bytes 1048592 | tf_op jit(solution)/shard_map/all_gather | solution.py:91
  176.3 1.5 copy.62
  177.8 8.1 %bitcast_reduce_fusion = (f32[4,8,128]{2,1,0:T(8,128)S(1)}, f32[4,1024,128,8]{2,1,3,0:T(8,128)}) fusion(bf16[1024,4,128,1]{0,2,3,1:T(8,128)(2,1)S(1)} %bitcast.150, bf16[128,4,8,128]{0,3,2,1:T(8,128)(2,1)S(1)} %bitcast.143), kind=kOutput, calls=%fused_computation.12 | convolution fusion | flops 1082126336 | bytes 18890752 | tf_op jit(solution)/shard_map/rhgd,khd->hgrk/dot_general | solution.py:27
  185.9 62.7 %all-gather.13.cloned.1.call-done = bf16[1,2048,512]{1,2,0:T(8,128)(2,1)} async-done(((bf16[1,128,512]{1,2,0:T(8,128)(2,1)}), bf16[1,2048,512]{1,2,0:T(8,128)(2,1)}) %all-gather.13.cloned.1.call-update) | async-done | bytes 2097168 | tf_op jit(solution)/shard_map/all_gather | solution.py:108
  248.6 15.0 %fusion = (f32[4,8,128]{2,1,0:T(8,128)S(1)}, f32[4,2048,128,8]{2,1,3,0:T(8,128)}) fusion(pred[128,2048]{0,1:T(8,128)(4,1)S(1)} %compare_and_fusion, bf16[2048,4,128,1]{0,2,3,1:T(8,128)(2,1)} %bitcast.151, bf16[128,4,8,128]{0,3,2,1:T(8,128)(2,1)S(1)} %bitcast.144), kind=kOutput, calls=%fused_computation.2 | convolution fusion | flops 2172645376 | bytes 36978688 | tf_op jit(solution)/shard_map/rhgd,khd->hgrk/dot_general | solution.py:27
  263.6 14.2 %fusion.3 = f32[4,8,128]{2,1,0:T(8,128)S(1)} fusion(f32[4,2048,128,8]{2,1,3,0:T(8,128)} %get-tuple-element.29, f32[4,8,128]{2,1,0:T(8,128)S(1)} %get-tuple-element.16, pred[128,2048]{0,1:T(8,128)(4,1)S(1)} %compare_and_fusion), kind=kLoop, calls=%fused_computation.5 | loop fusion | flops 33550336 | bytes 33849344 | tf_op jit(solution)/shard_map/reduce_sum | solution.py:39
  277.8 41.5 %all-gather.19.cloned.1.call-done = bf16[1,1024,512]{2,1,0:T(8,128)(2,1)} async-done(((bf16[1,64,512]{2,1,0:T(8,128)(2,1)}), bf16[1,1024,512]{2,1,0:T(8,128)(2,1)}) %all-gather.19.cloned.1.call-update) | async-done | bytes 1048592 | tf_op jit(solution)/shard_map/all_gather | solution.py:92
  319.2 1.7 copy.65
  320.9 8.6 %fusion.15 = f32[4,8,128]{2,1,0:T(8,128)S(1)} fusion(f32[4,1024,128,8]{2,1,3,0:T(8,128)} %get-tuple-element.27, f32[4,8,128]{2,1,0:T(8,128)S(1)} %get-tuple-element.25), kind=kLoop, calls=%fused_computation.18 | loop fusion | flops 12578816 | bytes 16809984 | tf_op jit(solution)/shard_map/reduce_sum | solution.py:39
  329.5 0.6 fusion.35
  330.2 8.1 %fusion.55 = f32[4,1024,128,8]{2,1,3,0:T(8,128)} fusion(bf16[1024,4,128,1]{0,2,3,1:T(8,128)(2,1)S(1)} %bitcast.146, bf16[128,4,8,128]{0,3,2,1:T(8,128)(2,1)S(1)} %bitcast.140), kind=kOutput, calls=%fused_computation.88 | convolution fusion | flops 1073741824 | bytes 18874368 | tf_op jit(solution)/shard_map/rhgd,khd->hgrk/dot_general | solution.py:142
  338.3 10.2 %fusion.18 = f32[4,8,128,128]{2,3,1,0:T(8,128)} fusion(bf16[1024,4,128,1]{0,2,3,1:T(8,128)(2,1)S(1)} %bitcast.147, f32[4,1024,128,8]{2,1,3,0:T(8,128)} %get-tuple-element.27, f32[4,8,128]{2,1,0:T(8,128)S(1)} %get-tuple-element.25), kind=kOutput, calls=%fused_computation.21 | convolution fusion | flops 1086324736 | bytes 19939328 | tf_op jit(solution)/shard_map/hgrk,khd->hgrd/dot_general | solution.py:41
  348.5 0.0 copy-start
  348.5 0.0 copy-start.1
  348.5 0.0 copy-start.2
  348.5 10.4 %fusion.20 = f32[4,1024,128,1]{1,2,3,0:T(8,128)} fusion(bf16[128,4,8,128]{0,3,2,1:T(8,128)(2,1)S(1)} %bitcast.141, f32[4,1024,128,8]{2,1,3,0:T(8,128)} %get-tuple-element.27, f32[4,8,128]{2,1,0:T(8,128)S(1)} %get-tuple-element.17), kind=kOutput, calls=%fused_computation.22 | convolution fusion | flops 1086324736 | bytes 19939328 | tf_op jit(solution)/shard_map/hgrk,rhgd->khd/dot_general | solution.py:136
  358.9 31.7 %all-gather.15.cloned.1.call-done = bf16[1,2048,512]{2,1,0:T(8,128)(2,1)} async-done(((bf16[1,128,512]{2,1,0:T(8,128)(2,1)}), bf16[1,2048,512]{2,1,0:T(8,128)(2,1)}) %all-gather.15.cloned.1.call-update) | async-done | bytes 2097168 | tf_op jit(solution)/shard_map/all_gather | solution.py:109
  390.6 4.0 copy.70
  394.6 0.0 copy-done
  394.6 0.0 copy-done.1
  394.6 0.0 copy-done.2
  394.6 16.5 %fusion.31 = (bf16[128,4,8,128]{0,3,2,1:T(8,128)(2,1)S(1)}, f32[4,8,128,128]{2,3,1,0:T(8,128)}) fusion(f32[4,8,128,128]{2,3,1,0:T(8,128)} %fusion.18, f32[128,4,8]{0,2,1:T(8,128)S(1)} %copy-done.1, f32[128,4,8]{0,2,1:T(8,128)S(1)} %copy-done, f32[128,4,8]{0,2,1:T(8,128)S(1)} %copy-done.2, bf16[2048,4,128,1]{0,2,3,1:T(8,128)(2,1)} %bitcast.152, ...), kind=kOutput, calls=%fused_computation.36 | convolution fusion | flops 2183659520 | bytes 41222144 | tf_op jit(solution)/shard_map/hgrk,khd->hgrd/dot_general | solution.py:41
  411.1 3.1 fusion.29
  414.1 19.5 %bitcast_multiply_fusion = f32[4,1024,128]{1,2,0:T(8,128)} fusion(bf16[128,4,8,128]{0,3,2,1:T(8,128)(2,1)S(1)} %bitcast.145, f32[4,1024,128,8]{2,1,3,0:T(8,128)} %fusion.55, f32[4,1024,128,8]{2,1,3,0:T(8,128)} %get-tuple-element.27, f32[4,8,128]{2,1,0:T(8,128)S(1)} %fusion.29, f32[4,8,128]{2,1,0:T(8,128)S(1)} %get-tuple-element.17), kind=kOutput, calls=%fused_computation.31 | convolution fusion | flops 6459752448 | bytes 36732928 | tf_op jit(solution)/shard_map/hgrk,rhgd->khd/dot_general | solution.py:147
  433.7 1.9 copy.78
  435.6 2.9 copy.79
  438.5 4.0 pad_maximum_fusion
  442.5 0.0 reduce-scatter.3.cloned.1.call-update
  442.5 0.0 reduce-scatter.5.cloned.1.call-start
  444.4 75.7 %reduce-scatter.3.cloned.1.call-done = f32[64,2,512]{2,0,1:T(8,128)} async-done(((f32[1024,2,512]{2,0,1:T(8,128)}), f32[64,2,512]{2,0,1:T(8,128)}) %reduce-scatter.3.cloned.1.call-update) | async-done | bytes 262160 | tf_op jit(solution)/shard_map/reduce_scatter | solution.py:156
  520.1 2.5 broadcast_in_dim.103
  522.6 1.7 bitcast_dynamic-update-slice_fusion
  524.3 0.0 reduce-scatter.5.cloned.1.call-update
  524.3 1.3 copy.80
  525.6 91.7 %reduce-scatter.5.cloned.1.call-done = f32[1,64,2,512]{3,1,2,0:T(8,128)} async-done(((f32[16,64,2,512]{3,1,2,0:T(8,128)}), f32[1,64,2,512]{3,1,2,0:T(8,128)}) %reduce-scatter.5.cloned.1.call-update) | async-done | bytes 262160 | tf_op jit(solution)/shard_map/reduce_scatter | solution.py:173
  617.3 1.7 slice_bitcast_fusion
  (6 shorter events, 0.1 us)
Async XLA Ops:
  7.2 57.9 %all-gather.9.cloned.1.call-start = ((), (), s32[]{:S(2)}) async-start(), calls=%async_computation.2 | async-start | bytes 1114112 | tf_op jit(solution)/shard_map/all_gather | solution.py:77
  7.9 108.8 %all-gather.11.cloned.1.call-start = ((), (), s32[]{:S(2)}) async-start(), calls=%async_computation.3 | async-start | bytes 1114112 | tf_op jit(solution)/shard_map/all_gather | solution.py:78
  8.6 167.7 %all-gather.17.cloned.1.call-start = ((), (), s32[]{:S(2)}) async-start(), calls=%async_computation.8 | async-start | bytes 1114112 | tf_op jit(solution)/shard_map/all_gather | solution.py:91
  66.5 182.1 %all-gather.13.cloned.1.call-start = ((), (), s32[]{:S(2)}) async-start(), calls=%async_computation.4 | async-start | bytes 2228224 | tf_op jit(solution)/shard_map/all_gather | solution.py:108
  68.3 251.0 %all-gather.19.cloned.1.call-start = ((), (), s32[]{:S(2)}) async-start(), calls=%async_computation.9 | async-start | bytes 1114112 | tf_op jit(solution)/shard_map/all_gather | solution.py:92
  118.2 272.4 %all-gather.15.cloned.1.call-start = ((), (), s32[]{:S(2)}) async-start(), calls=%async_computation.5 | async-start | bytes 2228224 | tf_op jit(solution)/shard_map/all_gather | solution.py:109
  118.7 401.4 %reduce-scatter.3.cloned.1.call-start = ((), (), s32[]{:S(2)}) async-start(), calls=%async_computation.6 | async-start | bytes 4456448 | tf_op jit(solution)/shard_map/reduce_scatter | solution.py:156
  348.5 46.1 %copy-start = (f32[128,4,8]{0,2,1:T(8,128)S(1)}, f32[128,4,8]{0,2,1:T(8,128)}, u32[]{:S(2)}) copy-start(f32[128,4,8]{0,2,1:T(8,128)} %get-tuple-element.21) | copy-start | bytes 49156
  348.5 46.1 %copy-start.1 = (f32[128,4,8]{0,2,1:T(8,128)S(1)}, f32[128,4,8]{0,2,1:T(8,128)}, u32[]{:S(2)}) copy-start(f32[128,4,8]{0,2,1:T(8,128)} %get-tuple-element.22) | copy-start | bytes 49156
  348.5 46.1 %copy-start.2 = (f32[128,4,8]{0,2,1:T(8,128)S(1)}, f32[128,4,8]{0,2,1:T(8,128)}, u32[]{:S(2)}) copy-start(f32[128,4,8]{0,2,1:T(8,128)} %get-tuple-element.24) | copy-start | bytes 49156
  442.5 174.8 %reduce-scatter.5.cloned.1.call-start = ((), (), s32[]{:S(2)}) async-start(), calls=%async_computation.7 | async-start | bytes 4456448 | tf_op jit(solution)/shard_map/reduce_scatter | solution.py:173
Sparse Core Ops, SparseCore 0:
  10.7 54.2 all-gather.8
  67.7 48.8 all-gather.10
  119.0 57.2 all-gather.16
  178.4 70.0 all-gather.12
  250.8 68.3 all-gather.18
  320.9 69.6 all-gather.14
  442.7 77.4 reduce-scatter.2
  524.5 92.7 reduce-scatter.4
where the time goes:
time: 627 us; the launch traced here: 626 us
  waiting for transfers between devices  453 us (72%)
  matrix products  87.8 us (14%)
  other arithmetic  37.1 us (6%)
  local copies, waits for them, and re-layouts  27.8 us (4%)
  between operations  19.9 us (3%)
    reduce_scatter x1, waiting for transfers between devices, on_device(): summed = lax.psum_scatter(slots, 'dp', scatter_dimension=0, tiled=True)  91.7 us
    reduce_scatter x1, waiting for transfers between devices, on_device(): lax.psum_scatter(jnp.stack([key_gradient.reshape(item_count, slice_width)...  75.7 us
    all_gather x1, waiting for transfers between devices, on_device(): lax.all_gather(response_key_rows, 'blk', axis=1, tiled=True)  62.7 us
    all_gather x1, waiting for transfers between devices, on_device(): lax.all_gather(prompt_keys, 'dp', axis=0, tiled=True)  50 us
    all_gather x1, waiting for transfers between devices, on_device(): lax.all_gather(own_keys, 'blk', axis=0, tiled=True)  49.3 us
    all_gather x1, waiting for transfers between devices, on_device(): lax.all_gather(prompt_value_rows, 'dp', axis=0, tiled=True)  48.3 us
    all_gather x1, waiting for transfers between devices, on_device(): lax.all_gather(own_values, 'blk', axis=0, tiled=True)  41.5 us
    all_gather x1, waiting for transfers between devices, on_device(): lax.all_gather(response_value_rows, 'blk', axis=1, tiled=True)  31.7 us
  transfers between devices with their start and end apart: 8, of which 8 were waited for; matrix products, arithmetic and copies ran while one was open for 15% of the time, Pallas kernels for 0%

commit v1 on v0

v1 whole, which is shorter than its diff:
```python
import jax
import jax.numpy as jnp
from jax import lax
from jax.experimental import pallas as pl
from jax.experimental.pallas import tpu as pltpu
from jax.sharding import PartitionSpec as P

MESH = pl.DeviceIdType.MESH
HEAD_WIDTH = 128
SCALE = HEAD_WIDTH ** (-0.5)
LOG2E = 1.4426950408889634
SCORE_SCALE = SCALE * LOG2E
MASKED = -1e30
LOWEST = -1e20
BF = jnp.bfloat16
F32 = jnp.float32

X, YH, CORES, YL, Z = 4, 2, 2, 2, 8
GROUP = 8
ROWS = 128
PROWS = 64
HALF_KV = 256
HALF_Q = 2048


def nt(a, b):
    return lax.dot_general(a, b, (((1,), (1,)), ((), ())), preferred_element_type=F32)


def nn(a, b):
    return lax.dot_general(a, b, (((1,), (0,)), ((), ())), preferred_element_type=F32)


def tn(a, b):
    return lax.dot_general(a, b, (((0,), (0,)), ((), ())), preferred_element_type=F32)


def kernel(
    q_ref, rk_ref, rv_ref, pk_ref, pv_ref, do_ref, owner_ref, prompt_ref, length_ref, half_ref,
    out_ref, gk_ref, gv_ref,
    q_far, do_far, out_far, resp, xbuf, hp_out, hp_in, prompt,
    m_ref, l_ref, acc_ref, lse_ref, delta_ref, gacc,
    zs_out, zs_in, share, yh_in, core_in, xs_out, xs_in, y_out, y_in, xsum,
    send_sem, recv_sem,
):
    dp = lax.axis_index("dp")
    blk = lax.axis_index("blk")
    x, yh, c = dp // 4, (dp // 2) % 2, dp % 2
    yl, z = blk // Z, blk % Z
    other = 1 - yl
    y_id = (dp, other * Z + z)
    z_right, z_left = (dp, yl * Z + (z + 1) % Z), (dp, yl * Z + (z + Z - 1) % Z)
    x_right = (((x + 1) % X) * 4 + yh * 2 + c, blk)
    x_left = (((x + X - 1) % X) * 4 + yh * 2 + c, blk)
    core_id = (x * 4 + yh * 2 + (1 - c), blk)
    yh_id = (x * 4 + (1 - yh) * 2 + c, blk)

    barrier = pltpu.get_barrier_semaphore()
    peers = (y_id, z_right, z_left, x_right, x_left, core_id, yh_id)
    for peer in peers:
        pl.semaphore_signal(barrier, inc=1, device_id=peer, device_id_type=MESH)
    pl.semaphore_wait(barrier, len(peers))

    started = []

    def send(src, dst, peer):
        index = len(started)
        copy = pltpu.make_async_remote_copy(
            src_ref=src, dst_ref=dst, send_sem=send_sem.at[index], recv_sem=recv_sem.at[index],
            device_id=peer, device_id_type=MESH,
        )
        copy.start()
        started.append(copy)
        return copy

    def arrive(copies):
        for copy in copies:
            copy.wait_recv()

    def lanes(which, width):
        return pl.ds(pl.multiple_of(which * width, width), width)

    mine_kv, far_kv = lanes(yl, HALF_KV), lanes(other, HALF_KV)
    mine_q, far_q = lanes(yl, HALF_Q), lanes(other, HALF_Q)

    y_prompt = [
        send(ref.at[0, :, far_kv], xbuf.at[x, c, kv, yl], y_id)
        for kv, ref in enumerate((pk_ref, pv_ref))
    ]
    y_resp = [
        send(ref.at[0, :, far_kv], resp.at[z, kv, yl], y_id)
        for kv, ref in enumerate((rk_ref, rv_ref))
    ]
    y_q = send(q_ref.at[0, :, far_q], q_far, y_id)
    for kv, ref in enumerate((pk_ref, pv_ref)):
        xbuf[x, c, kv, yl] = ref[0, :, mine_kv]
    for kv, ref in enumerate((rk_ref, rv_ref)):
        resp[z, kv, yl] = ref[0, :, mine_kv]

    def gather_step(slot, pos, n, step, right, left):
        halves_right, halves_left = ((0, 1), (0, 1)) if step < n // 2 - 1 else ((0,), (1,))
        from_slot = (pos + n - step) % n
        copies = [send(slot(from_slot, h), slot(from_slot, h), right) for h in halves_right]
        from_slot = (pos + step) % n
        copies += [send(slot(from_slot, h), slot(from_slot, h), left) for h in halves_left]
        return copies

    def x_slot(i, h):
        return xbuf.at[i, c, h]

    def core_send(i):
        return send(xbuf.at[i, c], xbuf.at[i, c], core_id)

    def resp_slot(i, h):
        return resp.at[i, h]

    def prompt_slot(i, h):
        return prompt.at[i, h]

    lane = lax.broadcasted_iota(jnp.int32, (1, 2 * ROWS), 1)
    last = length_ref[dp] - 1
    limit = jnp.zeros((1, 2 * ROWS), jnp.int32)
    for part, holder in enumerate((blk, other * Z + z)):
        for e in range(2):
            block = part * 2 + e
            inside = (lane >= block * 64) & (lane < block * 64 + 64)
            limit = jnp.where(inside, half_ref[2 * holder + e] * 64 + lane - block * 64, limit)
    limit = jnp.minimum(limit, last)
    down = lax.broadcasted_iota(jnp.int32, (64, 2 * ROWS), 0)

    def head_of(ref, far, h):
        near = ref[0, :, pl.ds(pl.multiple_of(yl * HALF_Q + h * 128, 128), 128)]
        return jnp.concatenate([near, far[:, pl.ds(pl.multiple_of(h * 128, 128), 128)]], axis=0)

    def keys_of(buf, slots, kv, a, rows):
        return jnp.concatenate(
            [buf[i, kv, :, :, a * 128 : (a + 1) * 128].reshape(2 * rows, 128) for i in slots], axis=0
        )

    def absorb(buf, slots, rows, masked):
        bounds = []
        if masked:
            for i in slots:
                for y in range(2):
                    for e in range(2):
                        bounds.append(limit - half_ref[2 * (y * Z + i) + e] * 64)

        def body(g, carry):
            for a in range(2):
                h = a * GROUP + g
                query = head_of(q_ref, q_far, h)
                scores = nt(keys_of(buf, slots, 0, a, rows), query) * SCORE_SCALE
                if masked:
                    scores = jnp.concatenate(
                        [
                            jnp.where(down <= bound, scores[64 * n : 64 * n + 64], MASKED)
                            for n, bound in enumerate(bounds)
                        ],
                        axis=0,
                    )
                old = m_ref[h]
                peak = jnp.maximum(old, jnp.max(scores, axis=0, keepdims=True))
                weights = jnp.exp2(scores - peak)
                factor = jnp.exp2(old - peak)
                m_ref[h] = peak
                l_ref[h] = l_ref[h] * factor + jnp.sum(weights, axis=0, keepdims=True)
                acc_ref[h] = acc_ref[h] * factor + tn(
                    keys_of(buf, slots, 1, a, rows), weights.astype(BF)
                )
            return carry

        lax.fori_loop(0, GROUP, body, 0)

    m_ref[...] = jnp.full(m_ref.shape, LOWEST, F32)
    l_ref[...] = jnp.zeros(l_ref.shape, F32)
    acc_ref[...] = jnp.zeros(acc_ref.shape, F32)

    arrive(y_prompt)
    x0 = gather_step(x_slot, x, X, 0, x_right, x_left)
    cores = [core_send(x)]
    arrive(y_resp)
    r0 = gather_step(resp_slot, z, Z, 0, z_right, z_left)
    arrive(x0)
    x1 = gather_step(x_slot, x, X, 1, x_right, x_left)
    cores += [core_send((x + 1) % X), core_send((x + X - 1) % X)]
    arrive(x1)
    cores += [core_send((x + 2) % X)]
    arrive(cores)
    theirs = owner_ref[prompt_ref[x * 4 + (1 - yh) * 2 + c]]
    mine = owner_ref[prompt_ref[dp]]
    hp_out[...] = xbuf[theirs // 4, theirs % 2]
    yh_copy = send(hp_out, hp_in, yh_id)
    arrive(r0)
    r1 = gather_step(resp_slot, z, Z, 1, z_right, z_left)
    arrive([yh_copy])
    prompt[z] = jnp.where((mine // 2) % 2 == yh, xbuf[mine // 4, mine % 2], hp_in[...])
    p0 = gather_step(prompt_slot, z, Z, 0, z_right, z_left)
    y_do = send(do_ref.at[0, :, far_q], do_far, y_id)
    arrive([y_q])

    def pair(step):
        return [(z + step) % Z, (z + Z - step) % Z]

    absorb(resp, [z], ROWS, True)
    arrive(r1)
    r2 = gather_step(resp_slot, z, Z, 2, z_right, z_left)
    absorb(resp, pair(1), ROWS, True)
    arrive(p0)
    p1 = gather_step(prompt_slot, z, Z, 1, z_right, z_left)
    arrive(r2)
    r3 = gather_step(resp_slot, z, Z, 3, z_right, z_left)
    absorb(resp, pair(2), ROWS, True)
    arrive(p1)
    p2 = gather_step(prompt_slot, z, Z, 2, z_right, z_left)
    absorb(resp, pair(3), ROWS, True)
    arrive(r3)
    arrive(p2)
    p3 = gather_step(prompt_slot, z, Z, 3, z_right, z_left)
    absorb(resp, [(z + 4) % Z], ROWS, True)
    absorb(prompt, [z] + pair(1), PROWS, False)
    absorb(prompt, pair(2) + pair(3), PROWS, False)
    arrive(p3)
    absorb(prompt, [(z + 4) % Z], PROWS, False)

    arrive([y_do])

    def finish(h, carry):
        total = l_ref[h]
        mixed = acc_ref[h] / total
        lse_ref[h] = m_ref[h] + jnp.log(total) * LOG2E
        cotangent = head_of(do_ref, do_far, h).astype(F32)
        delta_ref[h] = jnp.sum(cotangent.T * mixed, axis=0, keepdims=True)
        rows = mixed.T.astype(BF)
        out_ref[0, :, pl.ds(pl.multiple_of(yl * HALF_Q + h * 128, 128), 128)] = rows[:ROWS]
        out_far[:, pl.ds(pl.multiple_of(h * 128, 128), 128)] = rows[ROWS:]
        return carry

    lax.fori_loop(0, 2 * GROUP, finish, 0)
    y_result = send(out_far, out_ref.at[0, :, mine_q], y_id)

    def gradients(slots):
        count = len(slots)
        gacc[...] = jnp.zeros(gacc.shape, F32)

        def body(g, carry):
            for a in range(2):
                h = a * GROUP + g
                query = head_of(q_ref, q_far, h)
                cotangent = head_of(do_ref, do_far, h)
                probs = jnp.exp2(
                    nt(keys_of(prompt, slots, 0, a, PROWS), query) * SCORE_SCALE - lse_ref[h]
                )
                back = nt(keys_of(prompt, slots, 1, a, PROWS), cotangent)
                slopes = probs * (back - delta_ref[h])
                key_part = nn(slopes.astype(BF), query)
                value_part = nn(probs.astype(BF), cotangent)
                for n in range(count):
                    rows = slice(n * 128, n * 128 + 128)
                    columns = slice(a * 128, a * 128 + 128)
                    gacc[n, 0, :, columns] += key_part[rows]
                    gacc[n, 1, :, columns] += value_part[rows]
            return carry

        lax.fori_loop(0, GROUP, body, 0)

    def own_part(n, h):
        part = gacc[n, h].reshape(2, PROWS, HALF_KV)
        return part * SCALE if h == 0 else part

    def scatter_step(own, outgoing, incoming, step, n, right, left):
        halves = ((0,), (1,)) if step == 0 else ((0, 1), (0, 1))
        before = ((0,), (1,)) if step == 1 else ((0, 1), (0, 1))
        copies = []
        for way, peer in enumerate((right, left)):
            for h in halves[way]:
                part = own(way, h)
                if step > 0 and h in before[way]:
                    part = part + incoming[way, step - 1, h].astype(F32)
                outgoing[way, step, h] = part.astype(BF)
                copies.append(send(outgoing.at[way, step, h], incoming.at[way, step, h], peer))
        return copies

    gradients([(z + 4) % Z])
    s0 = scatter_step(lambda way, h: own_part(0, h), zs_out, zs_in, 0, Z, z_right, z_left)
    previous = s0
    for step in range(1, 4):
        gradients(pair(4 - step))
        arrive(previous)
        previous = scatter_step(own_part, zs_out, zs_in, step, Z, z_right, z_left)
    gradients([z])
    arrive(previous)
    for h in range(2):
        share[0, h] = (
            own_part(0, h) + zs_in[0, 3, h].astype(F32) + zs_in[1, 3, h].astype(F32)
        ).astype(BF)

    arrive([send(share.at[0], share.at[1], yh_id)])
    arrive([send(share, core_in, core_id)])
    owners = []
    for source_core in (c, 1 - c):
        for source_half in (yh, 1 - yh):
            owners.append(owner_ref[prompt_ref[x * 4 + source_half * 2 + source_core]])

    def destined(target, h):
        total = jnp.zeros((2, PROWS, HALF_KV), F32)
        for n, owner in enumerate(owners):
            part = (share if n < 2 else core_in)[n % 2, h].astype(F32)
            total = total + jnp.where(owner == target * 4 + yh * 2 + c, part, 0.0)
        return total

    def toward(distance):
        return lambda way, h: destined((x + distance) % X if way == 0 else (x + X - distance) % X, h)

    previous = scatter_step(toward(2), xs_out, xs_in, 0, X, x_right, x_left)
    arrive(previous)
    previous = scatter_step(toward(1), xs_out, xs_in, 1, X, x_right, x_left)
    arrive(previous)
    for h, ref in enumerate((gk_ref, gv_ref)):
        xsum[h] = destined(x, h) + xs_in[0, 1, h].astype(F32) + xs_in[1, 1, h].astype(F32)
        y_out[h] = xsum[h, other].astype(BF)
    last_copy = send(y_out, y_in, y_id)
    for h, ref in enumerate((gk_ref, gv_ref)):
        ref[0, :, mine_kv] = xsum[h, yl]
    arrive([last_copy])
    for h, ref in enumerate((gk_ref, gv_ref)):
        ref[0, :, far_kv] = y_in[h].astype(F32)
    arrive([y_result])
    for copy in started:
        copy.wait_send()


COPIES = 96


def on_device(*arguments):
    block = (2, 2, PROWS, HALF_KV)
    vmem = pl.BlockSpec(memory_space=pltpu.VMEM)
    smem = pl.BlockSpec(memory_space=pltpu.SMEM)
    return pl.pallas_call(
        kernel,
        out_shape=(
            jax.ShapeDtypeStruct((1, ROWS, 4096), BF),
            jax.ShapeDtypeStruct((1, PROWS, 512), F32),
            jax.ShapeDtypeStruct((1, PROWS, 512), F32),
        ),
        in_specs=[vmem] * 6 + [smem] * 4,
        out_specs=(vmem, vmem, vmem),
        scratch_shapes=[
            pltpu.VMEM((ROWS, HALF_Q), BF),
            pltpu.VMEM((ROWS, HALF_Q), BF),
            pltpu.VMEM((ROWS, HALF_Q), BF),
            pltpu.VMEM((Z, 2, 2, ROWS, HALF_KV), BF),
            pltpu.VMEM((X, 2) + block, BF),
            pltpu.VMEM(block, BF),
            pltpu.VMEM(block, BF),
            pltpu.VMEM((Z,) + block, BF),
            pltpu.VMEM((16, 1, 256), F32),
            pltpu.VMEM((16, 1, 256), F32),
            pltpu.VMEM((16, 128, 256), F32),
            pltpu.VMEM((16, 1, 256), F32),
            pltpu.VMEM((16, 1, 256), F32),
            pltpu.VMEM((2, 2, 128, HALF_KV), F32),
            pltpu.VMEM((2, 4) + block, BF),
            pltpu.VMEM((2, 4) + block, BF),
            pltpu.VMEM((2,) + block, BF),
            pltpu.VMEM(block, BF),
            pltpu.VMEM((2,) + block, BF),
            pltpu.VMEM((2, 2) + block, BF),
            pltpu.VMEM((2, 2) + block, BF),
            pltpu.VMEM((2, PROWS, HALF_KV), BF),
            pltpu.VMEM((2, PROWS, HALF_KV), BF),
            pltpu.VMEM(block, F32),
            pltpu.SemaphoreType.DMA((COPIES,)),
            pltpu.SemaphoreType.DMA((COPIES,)),
        ],
        compiler_params=pltpu.CompilerParams(
            collective_id=0, has_side_effects=True, vmem_limit_bytes=48 * 1024 * 1024
        ),
        cost_estimate=pl.CostEstimate(
            flops=10_000_000_000, bytes_accessed=8 * 1024 * 1024, transcendentals=17_000_000
        ),
    )(*arguments)


def solution(mesh):
    split = P("dp", "blk", None)
    return jax.shard_map(
        on_device,
        mesh=mesh,
        in_specs=(split,) * 6 + (P(),) * 4,
        out_specs=(split, split, split),
        check_vma=False,
    )
```

time: 627 us -> 142 us (0.23)
  waiting for transfers between devices: 453 us -> 0 us
  Pallas kernels: 0 us -> 130 us
  matrix products: 87.8 us -> 0 us
  other arithmetic: 37.1 us -> 0 us
  between operations: 19.9 us -> 0.66 us
  local copies, waits for them, and re-layouts: 27.8 us -> 10.8 us
    all_gather x6 -> x0, waiting for transfers between devices: 283 us -> none  [the longest x1 62.7 us: on_device(): lax.all_gather(response_key_rows, 'blk', axis=1, tiled=True)]
    reduce_scatter x2 -> x0, waiting for transfers between devices: 167 us -> none  [the longest x1 91.7 us: on_device(): summed = lax.psum_scatter(slots, 'dp', scatter_dimension=0, tiled=True)]
    pallas_call x0 -> x1, Pallas kernels: none -> 130 us  [on_device(): pl.pallas_call(kernel, out_shape=(jax.ShapeDtypeStruct((1, ROWS, 4096), B...]
    dot_general x7 -> x0, matrix products: 87.8 us -> none  [the longest x2 26.7 us: absorb(): jnp.einsum('hgrk,khd->hgrd', narrow, value_rows.reshape(value_rows.shape[...]
    reduce_sum x5 -> x0, other arithmetic: 27.4 us -> none  [the longest x2 22.8 us: absorb(): total = total * factor + jnp.sum(weights, -1)]
    all_gather x3 -> x0, local copies, waits for them, and re-layouts: 7.1 us -> none  [the longest x1 3.96 us: on_device(): lax.all_gather(response_value_rows, 'blk', axis=1, tiled=True)]
    another operation x3 -> x0, local copies, waits for them, and re-layouts: 6.46 us -> none  [the longest x2 4.85 us: on_device(): jnp.stack([key_gradient.reshape(item_count, slice_width), value_gradient....]
  transfers between devices with their start and end apart: 8 -> 0, of which waited for: 8 -> 0; matrix products, arithmetic and copies ran while one was open for 15% -> 0% of each run, Pallas kernels for 0% -> 0%
where the time goes in v1:
time: 142 us; the launch traced here: 141 us
  Pallas kernels  130 us (92%)
  local copies, waits for them, and re-layouts  10.8 us (8%)
    pallas_call x1, Pallas kernels, on_device(): pl.pallas_call(kernel, out_shape=(jax.ShapeDtypeStruct((1, ROWS, 4096), B...  130 us
    unnamed x23, local copies, waits for them, and re-layouts  10.8 us

profile of v1, /device:TPU:1, one launch (start us, length us, event | category | flops | bytes accessed | tf_op | source)
XLA Modules:
  0.0 141.3 jit_solution(827789758594637158)
XLA Ops:
  0.6 0.0 copy-start
  0.6 1.2 copy-done
  1.9 0.0 copy-start.1
  1.9 1.2 copy-done.1
  3.1 0.0 copy-start.2
  3.1 0.9 copy-done.2
  4.0 0.0 copy-start.3
  4.0 0.9 copy-done.3
  4.9 0.0 copy-start.4
  4.9 0.8 copy-done.4
  5.7 0.0 copy-start.5
  5.7 0.8 copy-done.5
  6.6 0.0 copy-start.6
  6.6 0.7 copy-done.6
  7.2 0.0 copy-start.7
  7.2 0.7 copy-done.7
  7.9 0.0 copy-start.8
  7.9 0.7 copy-done.8
  8.5 0.0 copy-start.9
  8.5 0.7 copy-done.9
  9.2 129.8 %shard_map.121 = (bf16[1,128,4096]{2,1,0:T(8,128)(2,1)S(1)}, f32[1,64,512]{2,1,0:T(8,128)S(1)}, f32[1,64,512]{2,1,0:T(8,128)S(1)}) custom-call(bf16[1,128,4096]{2,1,0:T(8,128)(2,1)S(1)} %copy-done, bf16[1,128,512]{2,1,0:T(8,128)(2,1)S(1)} %copy-done.2, bf16[1,128,512]{2,1,0:T(8,128)(2,1)S(1)} %copy-done.3, bf16[1,64,512]{2,1,0:T(8,128)(2,1)S(1)} %copy-done.4, ...), custom_call_target="tpu_custom_call" | custom-call | flops 10000000000 | bytes 8388608 | tf_op jit(solution)/shard_map/pallas_call | solution.py:339
  139.0 1.0 copy.16
  140.0 0.7 copy.17
  140.7 0.7 copy.18
Async XLA Ops:
  0.6 1.2 copy-start
  1.9 1.2 copy-start.1
  3.1 0.9 copy-start.2
  4.0 0.9 copy-start.3
  4.9 0.8 copy-start.4
  5.7 0.8 copy-start.5
  6.6 0.7 copy-start.6
  7.2 0.7 copy-start.7
  7.9 0.7 copy-start.8
  8.5 0.7 copy-start.9

commit v2 on v1

--- a/solution.py
+++ b/solution.py
@@ -36,12 +36,14 @@
 
 
 def kernel(
-    q_ref, rk_ref, rv_ref, pk_ref, pv_ref, do_ref, owner_ref, prompt_ref, length_ref, half_ref,
+    q_ref, rk_ref, rv_ref, pk_ref, pv_ref, do_ref, owner_hbm, prompt_hbm, length_hbm, half_hbm,
     out_ref, gk_ref, gv_ref,
-    q_far, do_far, out_far, resp, xbuf, hp_out, hp_in, prompt,
+    q_near, q_far, do_near, do_far, out_near, out_far, q_rows, q_turned, do_rows, do_turned,
+    resp, xbuf, hp_out, hp_in, prompt, v_turned,
     m_ref, l_ref, acc_ref, lse_ref, delta_ref, gacc,
-    zs_out, zs_in, share, yh_in, core_in, xs_out, xs_in, y_out, y_in, xsum,
-    send_sem, recv_sem,
+    zs_out, zs_in, share, core_in, xs_out, xs_in, y_out, y_in, xsum,
+    owner_ref, prompt_ref, length_ref, half_ref,
+    send_sem, recv_sem, local_sem,
 ):
     dp = lax.axis_index("dp")
     blk = lax.axis_index("blk")
@@ -55,6 +57,39 @@
     core_id = (x * 4 + yh * 2 + (1 - c), blk)
     yh_id = (x * 4 + (1 - yh) * 2 + c, blk)
 
+    def lanes(which, width):
+        return pl.ds(pl.multiple_of(which * width, width), width)
+
+    mine_kv, far_kv = lanes(yl, HALF_KV), lanes(other, HALF_KV)
+    mine_q, far_q = lanes(yl, HALF_Q), lanes(other, HALF_Q)
+
+    fetched = []
+
+    def fetch(src, dst):
+        copy = pltpu.make_async_copy(src, dst, local_sem.at[len(fetched)])
+        copy.start()
+        fetched.append(copy)
+        return copy
+
+    def present(copies):
+        for copy in copies:
+            copy.wait()
+
+    own_prompt = [
+        fetch(ref.at[0, :, mine_kv], xbuf.at[x, c, kv, yl])
+        for kv, ref in enumerate((pk_ref, pv_ref))
+    ]
+    own_resp = [
+        fetch(ref.at[0, :, mine_kv], resp.at[z, kv, yl])
+        for kv, ref in enumerate((rk_ref, rv_ref))
+    ]
+    tables = [
+        fetch(owner_hbm, owner_ref), fetch(prompt_hbm, prompt_ref),
+        fetch(length_hbm, length_ref), fetch(half_hbm, half_ref),
+    ]
+    own_q = fetch(q_ref.at[0, :, mine_q], q_near)
+    own_do = fetch(do_ref.at[0, :, mine_q], do_near)
+
     barrier = pltpu.get_barrier_semaphore()
     peers = (y_id, z_right, z_left, x_right, x_left, core_id, yh_id)
     for peer in peers:
@@ -77,12 +112,6 @@
         for copy in copies:
             copy.wait_recv()
 
-    def lanes(which, width):
-        return pl.ds(pl.multiple_of(which * width, width), width)
-
-    mine_kv, far_kv = lanes(yl, HALF_KV), lanes(other, HALF_KV)
-    mine_q, far_q = lanes(yl, HALF_Q), lanes(other, HALF_Q)
-
     y_prompt = [
         send(ref.at[0, :, far_kv], xbuf.at[x, c, kv, yl], y_id)
         for kv, ref in enumerate((pk_ref, pv_ref))
@@ -92,11 +121,6 @@
         for kv, ref in enumerate((rk_ref, rv_ref))
     ]
     y_q = send(q_ref.at[0, :, far_q], q_far, y_id)
-    for kv, ref in enumerate((pk_ref, pv_ref)):
-        xbuf[x, c, kv, yl] = ref[0, :, mine_kv]
-    for kv, ref in enumerate((rk_ref, rv_ref)):
-        resp[z, kv, yl] = ref[0, :, mine_kv]
-
     def gather_step(slot, pos, n, step, right, left):
         halves_right, halves_left = ((0, 1), (0, 1)) if step < n // 2 - 1 else ((0,), (1,))
         from_slot = (pos + n - step) % n
@@ -117,6 +141,16 @@
     def prompt_slot(i, h):
         return prompt.at[i, h]
 
+    def prepare(source, part, rows, turned):
+        def body(h, carry):
+            tile = source[:, pl.ds(pl.multiple_of(h * 128, 128), 128)]
+            rows[h, part * ROWS : (part + 1) * ROWS] = tile
+            turned[h, :, part * ROWS : (part + 1) * ROWS] = tile.T
+            return carry
+
+        lax.fori_loop(0, 2 * GROUP, body, 0, unroll=4)
+
+    present(tables)
     lane = lax.broadcasted_iota(jnp.int32, (1, 2 * ROWS), 1)
     last = length_ref[dp] - 1
     limit = jnp.zeros((1, 2 * ROWS), jnp.int32)
@@ -128,58 +162,73 @@
     limit = jnp.minimum(limit, last)
     down = lax.broadcasted_iota(jnp.int32, (64, 2 * ROWS), 0)
 
-    def head_of(ref, far, h):
-        near = ref[0, :, pl.ds(pl.multiple_of(yl * HALF_Q + h * 128, 128), 128)]
-        return jnp.concatenate([near, far[:, pl.ds(pl.multiple_of(h * 128, 128), 128)]], axis=0)
-
     def keys_of(buf, slots, kv, a, rows):
-        return jnp.concatenate(
-            [buf[i, kv, :, :, a * 128 : (a + 1) * 128].reshape(2 * rows, 128) for i in slots], axis=0
-        )
-
-    def absorb(buf, slots, rows, masked):
+        columns = pl.ds(pl.multiple_of(a * 128, 128), 128)
+        return [buf[i, kv, :, :, columns].reshape(2 * rows, 128) for i in slots]
+
+    def absorb(*chunks):
         bounds = []
-        if masked:
+        for buf, slots, rows, masked in chunks:
             for i in slots:
-                for y in range(2):
-                    for e in range(2):
-                        bounds.append(limit - half_ref[2 * (y * Z + i) + e] * 64)
-
-        def body(g, carry):
-            for a in range(2):
-                h = a * GROUP + g
-                query = head_of(q_ref, q_far, h)
-                scores = nt(keys_of(buf, slots, 0, a, rows), query) * SCORE_SCALE
-                if masked:
-                    scores = jnp.concatenate(
-                        [
-                            jnp.where(down <= bound, scores[64 * n : 64 * n + 64], MASKED)
-                            for n, bound in enumerate(bounds)
-                        ],
-                        axis=0,
-                    )
-                old = m_ref[h]
-                peak = jnp.maximum(old, jnp.max(scores, axis=0, keepdims=True))
-                weights = jnp.exp2(scores - peak)
-                factor = jnp.exp2(old - peak)
-                m_ref[h] = peak
-                l_ref[h] = l_ref[h] * factor + jnp.sum(weights, axis=0, keepdims=True)
-                acc_ref[h] = acc_ref[h] * factor + tn(
-                    keys_of(buf, slots, 1, a, rows), weights.astype(BF)
-                )
+                for n in range(2 * rows // 64):
+                    if masked:
+                        bounds.append(limit - half_ref[2 * ((n // 2) * Z + i) + n % 2] * 64)
+                    else:
+                        bounds.append(None)
+        count = 64 * len(bounds)
+
+        def all_keys(kv, a):
+            parts = []
+            for buf, slots, rows, masked in chunks:
+                parts += keys_of(buf, slots, kv, a, rows)
+            return jnp.concatenate(parts, axis=0) if len(parts) > 1 else parts[0]
+
+        for a in range(2):
+            v_turned[a, :, :count] = all_keys(1, a).T
+
+        def hide(scores):
+            pieces = []
+            for n, bound in enumerate(bounds):
+                piece = scores[64 * n : 64 * n + 64]
+                pieces.append(piece if bound is None else jnp.where(down <= bound, piece, MASKED))
+            return jnp.concatenate(pieces, axis=0)
+
+        def body(t, carry):
+            a = t // 2
+            heads = pl.ds(t * 4, 4)
+            keys, values = all_keys(0, a), v_turned[a, :, :count]
+            old, old_total, old_mixed = m_ref[heads], l_ref[heads], acc_ref[heads]
+            scores = [hide(nn(keys, q_turned[t * 4 + j]) * SCORE_SCALE) for j in range(4)]
+            peaks, totals, mixes = [], [], []
+            for j in range(4):
+                peak = jnp.maximum(old[j], jnp.max(scores[j], axis=0, keepdims=True))
+                weights = jnp.exp2(scores[j] - peak)
+                factor = jnp.exp2(old[j] - peak)
+                peaks.append(peak)
+                totals.append(old_total[j] * factor + jnp.sum(weights, axis=0, keepdims=True))
+                mixes.append(old_mixed[j] * factor + nn(values, weights.astype(BF)))
+            for j in range(4):
+                m_ref[t * 4 + j] = peaks[j]
+                l_ref[t * 4 + j] = totals[j]
+                acc_ref[t * 4 + j] = mixes[j]
             return carry
 
-        lax.fori_loop(0, GROUP, body, 0)
+        lax.fori_loop(0, 4, body, 0)
 
     m_ref[...] = jnp.full(m_ref.shape, LOWEST, F32)
     l_ref[...] = jnp.zeros(l_ref.shape, F32)
     acc_ref[...] = jnp.zeros(acc_ref.shape, F32)
 
+    present(own_prompt)
     arrive(y_prompt)
     x0 = gather_step(x_slot, x, X, 0, x_right, x_left)
     cores = [core_send(x)]
+    present(own_resp)
     arrive(y_resp)
     r0 = gather_step(resp_slot, z, Z, 0, z_right, z_left)
+    present([own_q, own_do])
+    prepare(q_near, 0, q_rows, q_turned)
+    prepare(do_near, 0, do_rows, do_turned)
     arrive(x0)
     x1 = gather_step(x_slot, x, X, 1, x_right, x_left)
     cores += [core_send((x + 1) % X), core_send((x + X - 1) % X)]
@@ -197,71 +246,77 @@
     p0 = gather_step(prompt_slot, z, Z, 0, z_right, z_left)
     y_do = send(do_ref.at[0, :, far_q], do_far, y_id)
     arrive([y_q])
+    prepare(q_far, 1, q_rows, q_turned)
 
     def pair(step):
         return [(z + step) % Z, (z + Z - step) % Z]
 
-    absorb(resp, [z], ROWS, True)
+    absorb((resp, [z] + pair(1), ROWS, True))
     arrive(r1)
     r2 = gather_step(resp_slot, z, Z, 2, z_right, z_left)
-    absorb(resp, pair(1), ROWS, True)
     arrive(p0)
     p1 = gather_step(prompt_slot, z, Z, 1, z_right, z_left)
+    absorb((resp, pair(2), ROWS, True))
     arrive(r2)
     r3 = gather_step(resp_slot, z, Z, 3, z_right, z_left)
-    absorb(resp, pair(2), ROWS, True)
     arrive(p1)
     p2 = gather_step(prompt_slot, z, Z, 2, z_right, z_left)
-    absorb(resp, pair(3), ROWS, True)
-    arrive(r3)
+    absorb((resp, pair(3), ROWS, True))
+    arrive([y_do])
+    prepare(do_far, 1, do_rows, do_turned)
     arrive(p2)
     p3 = gather_step(prompt_slot, z, Z, 3, z_right, z_left)
-    absorb(resp, [(z + 4) % Z], ROWS, True)
-    absorb(prompt, [z] + pair(1), PROWS, False)
-    absorb(prompt, pair(2) + pair(3), PROWS, False)
+    arrive(r3)
+    absorb((resp, [(z + 4) % Z], ROWS, True), (prompt, [z] + pair(1) + pair(2), PROWS, False))
     arrive(p3)
-    absorb(prompt, [(z + 4) % Z], PROWS, False)
-
-    arrive([y_do])
-
-    def finish(h, carry):
-        total = l_ref[h]
-        mixed = acc_ref[h] / total
-        lse_ref[h] = m_ref[h] + jnp.log(total) * LOG2E
-        cotangent = head_of(do_ref, do_far, h).astype(F32)
-        delta_ref[h] = jnp.sum(cotangent.T * mixed, axis=0, keepdims=True)
-        rows = mixed.T.astype(BF)
-        out_ref[0, :, pl.ds(pl.multiple_of(yl * HALF_Q + h * 128, 128), 128)] = rows[:ROWS]
-        out_far[:, pl.ds(pl.multiple_of(h * 128, 128), 128)] = rows[ROWS:]
+    absorb((prompt, pair(3) + [(z + 4) % Z], PROWS, False))
+
+    def finish(t, carry):
+        heads = pl.ds(t * 4, 4)
+        peak, total, mixed = m_ref[heads], l_ref[heads], acc_ref[heads]
+        turned = do_turned[heads]
+        outs, sums, deltas = [], [], []
+        for j in range(4):
+            result = mixed[j] / total[j]
+            sums.append(peak[j] + jnp.log(total[j]) * LOG2E)
+            deltas.append(jnp.sum(turned[j].astype(F32) * result, axis=0, keepdims=True))
+            outs.append(result.T.astype(BF))
+        for j in range(4):
+            h = t * 4 + j
+            lse_ref[h] = sums[j]
+            delta_ref[h] = deltas[j]
+            columns = pl.ds(pl.multiple_of(h * 128, 128), 128)
+            out_near[:, columns] = outs[j][:ROWS]
+            out_far[:, columns] = outs[j][ROWS:]
         return carry
 
-    lax.fori_loop(0, 2 * GROUP, finish, 0)
+    lax.fori_loop(0, 4, finish, 0)
     y_result = send(out_far, out_ref.at[0, :, mine_q], y_id)
+    own_result = fetch(out_near, out_ref.at[0, :, mine_q])
 
     def gradients(slots):
-        count = len(slots)
-        gacc[...] = jnp.zeros(gacc.shape, F32)
-
-        def body(g, carry):
-            for a in range(2):
-                h = a * GROUP + g
-                query = head_of(q_ref, q_far, h)
-                cotangent = head_of(do_ref, do_far, h)
-                probs = jnp.exp2(
-                    nt(keys_of(prompt, slots, 0, a, PROWS), query) * SCORE_SCALE - lse_ref[h]
-                )
-                back = nt(keys_of(prompt, slots, 1, a, PROWS), cotangent)
-                slopes = probs * (back - delta_ref[h])
-                key_part = nn(slopes.astype(BF), query)
-                value_part = nn(probs.astype(BF), cotangent)
-                for n in range(count):
-                    rows = slice(n * 128, n * 128 + 128)
-                    columns = slice(a * 128, a * 128 + 128)
-                    gacc[n, 0, :, columns] += key_part[rows]
-                    gacc[n, 1, :, columns] += value_part[rows]
+        def body(a, carry):
+            keys = jnp.concatenate(keys_of(prompt, slots, 0, a, PROWS), axis=0)
+            values = jnp.concatenate(keys_of(prompt, slots, 1, a, PROWS), axis=0)
+            all_probs, all_slopes = [], []
+            for j in range(GROUP):
+                h = a * GROUP + j
+                probs = jnp.exp2(nn(keys, q_turned[h]) * SCORE_SCALE - lse_ref[h])
+                slopes = probs * (nn(values, do_turned[h]) - delta_ref[h])
+                all_probs.append(probs.astype(BF))
+                all_slopes.append(slopes.astype(BF))
+            heads = pl.ds(a * GROUP, GROUP)
+            queries = q_rows[heads].reshape(GROUP * 2 * ROWS, 128)
+            cotangents = do_rows[heads].reshape(GROUP * 2 * ROWS, 128)
+            key_part = nn(jnp.concatenate(all_slopes, axis=1), queries)
+            value_part = nn(jnp.concatenate(all_probs, axis=1), cotangents)
+            columns = pl.ds(pl.multiple_of(a * 128, 128), 128)
+            for n in range(len(slots)):
+                gacc[n, 0, :, columns] = key_part[n * 128 : n * 128 + 128]
+                gacc[n, 1, :, columns] = value_part[n * 128 : n * 128 + 128]
             return carry
 
-        lax.fori_loop(0, GROUP, body, 0)
+        lax.fori_loop(0, 2, body, 0)
 
     def own_part(n, h):
         part = gacc[n, h].reshape(2, PROWS, HALF_KV)
@@ -325,6 +380,7 @@
     for h, ref in enumerate((gk_ref, gv_ref)):
         ref[0, :, far_kv] = y_in[h].astype(F32)
     arrive([y_result])
+    present([own_result])
     for copy in started:
         copy.wait_send()
 
@@ -335,7 +391,7 @@
 def on_device(*arguments):
     block = (2, 2, PROWS, HALF_KV)
     vmem = pl.BlockSpec(memory_space=pltpu.VMEM)
-    smem = pl.BlockSpec(memory_space=pltpu.SMEM)
+    hbm = pl.BlockSpec(memory_space=pltpu.HBM)
     return pl.pallas_call(
         kernel,
         out_shape=(
@@ -343,17 +399,25 @@
             jax.ShapeDtypeStruct((1, PROWS, 512), F32),
             jax.ShapeDtypeStruct((1, PROWS, 512), F32),
         ),
-        in_specs=[vmem] * 6 + [smem] * 4,
-        out_specs=(vmem, vmem, vmem),
+        in_specs=[hbm] * 10,
+        out_specs=(hbm, vmem, vmem),
         scratch_shapes=[
             pltpu.VMEM((ROWS, HALF_Q), BF),
             pltpu.VMEM((ROWS, HALF_Q), BF),
             pltpu.VMEM((ROWS, HALF_Q), BF),
+            pltpu.VMEM((ROWS, HALF_Q), BF),
+            pltpu.VMEM((ROWS, HALF_Q), BF),
+            pltpu.VMEM((ROWS, HALF_Q), BF),
+            pltpu.VMEM((16, 256, 128), BF),
+            pltpu.VMEM((16, 128, 256), BF),
+            pltpu.VMEM((16, 256, 128), BF),
+            pltpu.VMEM((16, 128, 256), BF),
             pltpu.VMEM((Z, 2, 2, ROWS, HALF_KV), BF),
             pltpu.VMEM((X, 2) + block, BF),
             pltpu.VMEM(block, BF),
             pltpu.VMEM(block, BF),
             pltpu.VMEM((Z,) + block, BF),
+            pltpu.VMEM((2, 128, 1024), BF),
             pltpu.VMEM((16, 1, 256), F32),
             pltpu.VMEM((16, 1, 256), F32),
             pltpu.VMEM((16, 128, 256), F32),
@@ -363,18 +427,22 @@
             pltpu.VMEM((2, 4) + block, BF),
             pltpu.VMEM((2, 4) + block, BF),
             pltpu.VMEM((2,) + block, BF),
-            pltpu.VMEM(block, BF),
             pltpu.VMEM((2,) + block, BF),
             pltpu.VMEM((2, 2) + block, BF),
             pltpu.VMEM((2, 2) + block, BF),
             pltpu.VMEM((2, PROWS, HALF_KV), BF),
             pltpu.VMEM((2, PROWS, HALF_KV), BF),
             pltpu.VMEM(block, F32),
+            pltpu.SMEM((16,), jnp.int32),
+            pltpu.SMEM((16,), jnp.int32),
+            pltpu.SMEM((16,), jnp.int32),
+            pltpu.SMEM((32,), jnp.int32),
             pltpu.SemaphoreType.DMA((COPIES,)),
             pltpu.SemaphoreType.DMA((COPIES,)),
+            pltpu.SemaphoreType.DMA((16,)),
         ],
         compiler_params=pltpu.CompilerParams(
-            collective_id=0, has_side_effects=True, vmem_limit_bytes=48 * 1024 * 1024
+            collective_id=0, has_side_effects=True, vmem_limit_bytes=60 * 1024 * 1024
         ),
         cost_estimate=pl.CostEstimate(
             flops=10_000_000_000, bytes_accessed=8 * 1024 * 1024, transcendentals=17_000_000

time: 142 us -> 109 us (0.77)
  Pallas kernels: 130 us -> 104 us
  local copies, waits for them, and re-layouts: 10.8 us -> 3.93 us
    pallas_call x1, Pallas kernels: 130 us -> 104 us  [on_device(): pl.pallas_call(kernel, out_shape=(jax.ShapeDtypeStruct((1, ROWS, 4096), B...]
    unnamed x23 -> x7, local copies, waits for them, and re-layouts: 10.8 us -> 3.93 us
where the time goes in v2:
time: 109 us
  Pallas kernels  104 us (95%)
  local copies, waits for them, and re-layouts  3.93 us (4%)
    pallas_call x1, Pallas kernels, on_device(): pl.pallas_call(kernel, out_shape=(jax.ShapeDtypeStruct((1, ROWS, 4096), B...  104 us
    unnamed x7, local copies, waits for them, and re-layouts  3.93 us

profile of v2, /device:TPU:1, one launch (start us, length us, event | category | flops | bytes accessed | tf_op | source)
XLA Modules:
  0.0 108.6 jit_solution(5949120009718238741)
XLA Ops:
  0.6 104.0 %shard_map.121 = (bf16[1,128,4096]{2,1,0:T(8,128)(2,1)}, f32[1,64,512]{2,1,0:T(8,128)}, f32[1,64,512]{2,1,0:T(8,128)}) custom-call(bf16[1,128,4096]{2,1,0:T(8,128)(2,1)} %q_ref.1, bf16[1,128,512]{2,1,0:T(8,128)(2,1)} %rk_ref.1, bf16[1,128,512]{2,1,0:T(8,128)(2,1)} %rv_ref.1, bf16[1,64,512]{2,1,0:T(8,128)(2,1)} %pk_ref.1, bf16[1,64,512]{2,1,0:T(8,128)(2,1)} %pv_ref.1, ...), custom_call_target="tpu_custom_call" | custom-call | flops 10000000000 | bytes 8388608 | tf_op jit(solution)/shard_map/pallas_call | solution.py:395
  104.7 0.0 copy-start.1
  104.7 2.3 %copy.16 = bf16[1,128,4096]{2,1,0:T(8,128)(2,1)} copy(bf16[1,128,4096]{2,1,0:T(8,128)(2,1)} %get-tuple-element.6) | data formatting | bytes 2097152
  107.0 0.0 copy-done.1
  107.0 0.0 copy-start
  107.0 0.7 copy.17
  107.7 0.3 copy-done
  108.0 0.7 copy.18
Async XLA Ops:
  104.7 2.3 %copy-start.1 = (f32[1,64,512]{2,1,0:T(8,128)S(1)}, f32[1,64,512]{2,1,0:T(8,128)}, u32[]{:S(2)}) copy-start(f32[1,64,512]{2,1,0:T(8,128)} %get-tuple-element.7) | copy-start | bytes 393220
  107.0 1.0 copy-start

commit v3 on v2

v3 whole, which is shorter than its diff:
```python
import jax
import jax.numpy as jnp
from jax import lax
from jax.experimental import pallas as pl
from jax.experimental.pallas import tpu as pltpu
from jax.sharding import PartitionSpec as P

MESH = pl.DeviceIdType.MESH
HEAD_WIDTH = 128
SCALE = HEAD_WIDTH ** (-0.5)
LOG2E = 1.4426950408889634
SCORE_SCALE = SCALE * LOG2E
MASKED = -1e30
LOWEST = -1e20
BF = jnp.bfloat16
F32 = jnp.float32

X, YH, CORES, YL, Z = 4, 2, 2, 2, 8
GROUP = 8
ROWS = 128
PROWS = 64
HALF_KV = 256
HALF_Q = 2048


def nt(a, b):
    return lax.dot_general(a, b, (((1,), (1,)), ((), ())), preferred_element_type=F32)


def nn(a, b):
    return lax.dot_general(a, b, (((1,), (0,)), ((), ())), preferred_element_type=F32)


def tn(a, b):
    return lax.dot_general(a, b, (((0,), (0,)), ((), ())), preferred_element_type=F32)


def kernel(
    q_ref, rk_ref, rv_ref, pk_ref, pv_ref, do_ref, owner_hbm, prompt_hbm, length_hbm, half_hbm,
    out_ref, gk_ref, gv_ref,
    q_near, q_far, do_near, do_far, out_near, out_far, q_rows, q_turned, do_rows, do_turned,
    resp, xbuf, chosen_out, chosen_in, prompt, v_turned,
    m_ref, acc_ref, lse_ref, delta_ref, gacc,
    zs_out, zs_in, share_out, share, core_in, xs_out, xs_in,
    owner_ref, prompt_ref, length_ref, half_ref,
    send_sem, recv_sem, local_sem,
):
    dp = lax.axis_index("dp")
    blk = lax.axis_index("blk")
    x, yh, c = dp // 4, (dp // 2) % 2, dp % 2
    yl, z = blk // Z, blk % Z
    other = 1 - yl
    y_id = (dp, other * Z + z)
    z_right, z_left = (dp, yl * Z + (z + 1) % Z), (dp, yl * Z + (z + Z - 1) % Z)
    x_right = (((x + 1) % X) * 4 + yh * 2 + c, blk)
    x_left = (((x + X - 1) % X) * 4 + yh * 2 + c, blk)
    core_id = (x * 4 + yh * 2 + (1 - c), blk)
    yh_id = (x * 4 + (1 - yh) * 2 + c, blk)
    diagonal_id = (x * 4 + (1 - yh) * 2 + c, other * Z + z)

    def lanes(which, width):
        return pl.ds(pl.multiple_of(which * width, width), width)

    def head_lanes(half, a):
        return pl.ds(pl.multiple_of(half * HALF_KV + a * 128, 128), 128)

    def group_lanes(half, a):
        return pl.ds(pl.multiple_of(half * HALF_Q + a * 1024, 1024), 1024)

    mine_kv, far_kv = lanes(yl, HALF_KV), lanes(other, HALF_KV)
    mine_q = lanes(yl, HALF_Q)

    fetched = []

    def fetch(src, dst):
        copy = pltpu.make_async_copy(src, dst, local_sem.at[len(fetched)])
        copy.start()
        fetched.append(copy)
        return copy

    def present(copies):
        for copy in copies:
            copy.wait()

    own_prompt = [
        fetch(ref.at[0], xbuf.at[x, c, kv]) for kv, ref in enumerate((pk_ref, pv_ref))
    ]
    own_resp = [
        fetch(ref.at[0, :, mine_kv], resp.at[z, kv, yl])
        for kv, ref in enumerate((rk_ref, rv_ref))
    ]
    tables = [
        fetch(owner_hbm, owner_ref), fetch(prompt_hbm, prompt_ref),
        fetch(length_hbm, length_ref), fetch(half_hbm, half_ref),
    ]
    own_q = fetch(q_ref.at[0, :, mine_q], q_near)
    own_do = fetch(do_ref.at[0, :, mine_q], do_near)

    barrier = pltpu.get_barrier_semaphore()
    peers = (y_id, z_right, z_left, x_right, x_left, core_id, yh_id, diagonal_id)
    for peer in peers:
        pl.semaphore_signal(barrier, inc=1, device_id=peer, device_id_type=MESH)
    pl.semaphore_wait(barrier, len(peers))

    started = []

    def send(src, dst, peer):
        index = len(started)
        copy = pltpu.make_async_remote_copy(
            src_ref=src, dst_ref=dst, send_sem=send_sem.at[index], recv_sem=recv_sem.at[index],
            device_id=peer, device_id_type=MESH,
        )
        copy.start()
        started.append(copy)
        return copy

    def arrive(copies):
        for copy in copies:
            copy.wait_recv()

    x0 = [
        send(ref.at[0], xbuf.at[x, c, kv], peer)
        for peer in (x_right, x_left)
        for kv, ref in enumerate((pk_ref, pv_ref))
    ]
    y_resp = [
        send(ref.at[0, :, far_kv], resp.at[z, kv, yl], y_id)
        for kv, ref in enumerate((rk_ref, rv_ref))
    ]
    cores = [
        send(ref.at[0], xbuf.at[x, c, kv], core_id) for kv, ref in enumerate((pk_ref, pv_ref))
    ]
    y_q = [
        send(q_ref.at[0, :, group_lanes(other, a)], q_far.at[:, a * 1024 : a * 1024 + 1024], y_id)
        for a in range(2)
    ]

    def gather_step(slot, pos, n, step, right, left, halves=(0, 1)):
        final = step == n // 2 - 1
        copies = []
        for h in halves:
            for way, peer in enumerate((right, left)):
                if not final or h == way:
                    at = slot((pos + n - step) % n if way == 0 else (pos + step) % n, h)
                    copies.append(send(at, at, peer))
        return copies

    def resp_gather(step, h):
        return gather_step(lambda i, h: resp.at[i, h], z, Z, step, z_right, z_left, (h,))

    def prompt_gather(a, step):
        return gather_step(lambda i, h: prompt.at[a, i, h], z, Z, step, z_right, z_left)

    def core_send(i):
        return send(xbuf.at[i, c], xbuf.at[i, c], core_id)

    def prepare(source, part, a, rows, turned):
        def body(g, carry):
            h = a * GROUP + g
            tile = source[:, pl.ds(pl.multiple_of(h * 128, 128), 128)]
            rows[h, part * ROWS : (part + 1) * ROWS] = tile
            turned[h, :, part * ROWS : (part + 1) * ROWS] = tile.T
            return carry

        lax.fori_loop(0, GROUP, body, 0, unroll=4)

    present(tables)
    lane = lax.broadcasted_iota(jnp.int32, (1, 2 * ROWS), 1)
    last = length_ref[dp] - 1
    limit = jnp.zeros((1, 2 * ROWS), jnp.int32)
    for part, holder in enumerate((blk, other * Z + z)):
        for e in range(2):
            block = part * 2 + e
            inside = (lane >= block * 64) & (lane < block * 64 + 64)
            limit = jnp.where(inside, half_ref[2 * holder + e] * 64 + lane - block * 64, limit)
    limit = jnp.minimum(limit, last)
    down = lax.broadcasted_iota(jnp.int32, (64, 2 * ROWS), 0)

    def resp_rows(slots, kv, a):
        return [
            resp[i, kv, :, :, a * 128 : (a + 1) * 128].reshape(2 * ROWS, 128) for i in slots
        ]

    def prompt_rows(slots, kv, a):
        return [prompt[a, i, kv].reshape(2 * PROWS, 128) for i in slots]

    def absorb(a, resp_slots, prompt_slots):
        bounds = []
        for i in resp_slots:
            for n in range(4):
                bounds.append(limit - half_ref[2 * ((n // 2) * Z + i) + n % 2] * 64)
        bounds += [None] * (2 * len(prompt_slots))
        count = 64 * len(bounds)

        def all_rows(kv):
            parts = resp_rows(resp_slots, kv, a) + prompt_rows(prompt_slots, kv, a)
            return jnp.concatenate(parts, axis=0) if len(parts) > 1 else parts[0]

        v_turned[:128, :count] = all_rows(1).T

        def hide(scores):
            pieces = []
            for n, bound in enumerate(bounds):
                piece = scores[64 * n : 64 * n + 64]
                pieces.append(piece if bound is None else jnp.where(down <= bound, piece, MASKED))
            return jnp.concatenate(pieces, axis=0)

        def body(t, carry):
            first = a * GROUP + t * 4
            heads = pl.ds(first, 4)
            keys, values = all_rows(0), v_turned[:, :count]
            old, old_mixed = m_ref[heads], acc_ref[heads]
            scores = [hide(nn(keys, q_turned[first + j]) * SCORE_SCALE) for j in range(4)]
            peaks, mixes = [], []
            for j in range(4):
                peak = jnp.maximum(old[j], jnp.max(scores[j], axis=0, keepdims=True))
                weights = jnp.exp2(scores[j] - peak).astype(BF)
                peaks.append(peak)
                mixes.append(old_mixed[j] * jnp.exp2(old[j] - peak) + nn(values, weights))
            for j in range(4):
                m_ref[first + j] = peaks[j]
                acc_ref[first + j] = mixes[j]
            return carry

        lax.fori_loop(0, 2, body, 0)

    def finish(a):
        def body(t, carry):
            first = a * GROUP + t * 4
            heads = pl.ds(first, 4)
            peak, mixed, turned = m_ref[heads], acc_ref[heads], do_turned[heads]
            outs, sums, deltas = [], [], []
            for j in range(4):
                total = mixed[j, 128:129]
                result = mixed[j, :128] / total
                sums.append(peak[j] + jnp.log(total) * LOG2E)
                deltas.append(jnp.sum(turned[j].astype(F32) * result, axis=0, keepdims=True))
                outs.append(result.T.astype(BF))
            for j in range(4):
                h = first + j
                lse_ref[h] = sums[j]
                delta_ref[h] = deltas[j]
                columns = pl.ds(pl.multiple_of(h * 128, 128), 128)
                out_near[:, columns] = outs[j][:ROWS]
                out_far[:, columns] = outs[j][ROWS:]
            return carry

        lax.fori_loop(0, 2, body, 0)
        return send(
            out_far.at[:, a * 1024 : a * 1024 + 1024], out_ref.at[0, :, group_lanes(yl, a)], y_id
        )

    def gradients(a, slots):
        keys = jnp.concatenate(prompt_rows(slots, 0, a), axis=0)
        values = jnp.concatenate(prompt_rows(slots, 1, a), axis=0)
        all_probs, all_slopes = [], []
        for h in range(a * GROUP, a * GROUP + GROUP):
            probs = jnp.exp2(nn(keys, q_turned[h]) * SCORE_SCALE - lse_ref[h])
            slopes = probs * (nn(values, do_turned[h]) - delta_ref[h])
            all_probs.append(probs.astype(BF))
            all_slopes.append(slopes.astype(BF))
        heads = slice(a * GROUP, a * GROUP + GROUP)
        queries = q_rows[heads].reshape(GROUP * 2 * ROWS, 128)
        cotangents = do_rows[heads].reshape(GROUP * 2 * ROWS, 128)
        key_part = nn(jnp.concatenate(all_slopes, axis=1), queries) * SCALE
        value_part = nn(jnp.concatenate(all_probs, axis=1), cotangents)
        for n in range(len(slots)):
            gacc[n, 0] = key_part[n * 128 : n * 128 + 128].reshape(2, PROWS, 128)
            gacc[n, 1] = value_part[n * 128 : n * 128 + 128].reshape(2, PROWS, 128)

    def scatter_step(own, outgoing, incoming, step, right, left):
        halves = ((0,), (1,)) if step == 0 else ((0, 1), (0, 1))
        before = ((0,), (1,)) if step == 1 else ((0, 1), (0, 1))
        copies = []
        for way, peer in enumerate((right, left)):
            for h in halves[way]:
                part = own(way, h)
                if step > 0 and h in before[way]:
                    part = part + incoming[way, step - 1, h].astype(F32)
                outgoing[way, step, h] = part.astype(BF)
                copies.append(send(outgoing.at[way, step, h], incoming.at[way, step, h], peer))
        return copies

    def z_scatter(a, step):
        own = (lambda way, h: gacc[0, h]) if step == 0 else (lambda way, h: gacc[way, h])
        return scatter_step(own, zs_out.at[a], zs_in.at[a], step, z_right, z_left)

    def to_y_ring(a):
        for h in range(2):
            for n, where in enumerate((yl, other)):
                total = gacc[0, h, where]
                for way in range(2):
                    total = total + zs_in[a, way, 3, h, where].astype(F32)
                (share.at[a, 0, 0] if n == 0 else share_out.at[a])[h] = total.astype(BF)
        return [
            send(share_out.at[a], share.at[a, 0, 1], y_id),
            send(share.at[a, 0, 0], share.at[a, 1, 0], yh_id),
            send(share_out.at[a], share.at[a, 1, 1], diagonal_id),
        ]

    def to_core(a):
        return [send(share.at[a], core_in.at[a], core_id)]

    owners = []
    for source_core in (c, 1 - c):
        for source_half in (yh, 1 - yh):
            owners.append(owner_ref[prompt_ref[x * 4 + source_half * 2 + source_core]])

    def destined(a, target, h):
        total = jnp.zeros((2, PROWS, 128), F32)
        for n, owner in enumerate(owners):
            part = (share if n < 2 else core_in)[a, n % 2, :, h].astype(F32)
            total = total + jnp.where(owner == target * 4 + yh * 2 + c, part, 0.0)
        return total

    def x_scatter(a, step):
        distance = 2 - step
        targets = ((x + distance) % X, (x + X - distance) % X)
        return scatter_step(
            lambda way, h: destined(a, targets[way], h),
            xs_out.at[a], xs_in.at[a], step, x_right, x_left,
        )

    def store(a):
        for h, ref in enumerate((gk_ref, gv_ref)):
            total = destined(a, x, h)
            for way in range(2):
                total = total + xs_in[a, way, 1, h].astype(F32)
            ref[0, :, head_lanes(yl, a)] = total[0]
            ref[0, :, head_lanes(other, a)] = total[1]

    drained = []

    def drain():
        for copy in started[len(drained) :]:
            copy.wait_send()
            drained.append(copy)

    m_ref[...] = jnp.full(m_ref.shape, LOWEST, F32)
    acc_ref[...] = jnp.zeros(acc_ref.shape, F32)
    v_turned[128:] = jnp.ones((16, v_turned.shape[1]), BF)

    def pair(step):
        return [(z + step) % Z, (z + Z - step) % Z]

    opposite = [(z + 4) % Z]
    p, r = [None, None], [None, None]

    def pass_on(step):
        for a in range(2):
            arrive(p[a])
            p[a] = prompt_gather(a, step)

    def pass_on_resp(step):
        for h in range(2):
            arrive(r[h])
            r[h] = resp_gather(step, h)

    present([own_q])
    for a in range(2):
        prepare(q_near, 0, a, q_rows, q_turned)
    arrive(x0)
    x1 = gather_step(lambda i, h: xbuf.at[i, c, h], x, X, 1, x_right, x_left)
    cores += [core_send((x + 1) % X), core_send((x + X - 1) % X)]
    present(own_resp)
    for h in range(2):
        arrive([y_resp[h]])
        r[h] = resp_gather(0, h)
    arrive(x1)
    cores += [core_send((x + 2) % X)]
    present([own_do])
    for a in range(2):
        prepare(do_near, 0, a, do_rows, do_turned)
    present(own_prompt)
    arrive(cores)
    theirs = owner_ref[prompt_ref[x * 4 + (1 - yh) * 2 + c]]
    mine = owner_ref[prompt_ref[dp]]

    def piece(owner, half, a):
        return xbuf[owner // 4, owner % 2, :, :, head_lanes(half, a)]

    ring = []
    for n, (owner, half, peer) in enumerate(
        ((mine, other, y_id), (theirs, yl, yh_id), (theirs, other, diagonal_id))
    ):
        for a in range(2):
            chosen_out[n, a] = piece(owner, half, a)
        ring.append(send(chosen_out.at[n], chosen_in.at[n], peer))
    arrive([y_q[0]])
    prepare(q_far, 1, 0, q_rows, q_turned)
    absorb(0, [z], [])
    pass_on_resp(1)
    arrive(ring)
    here = (mine // 2) % 2 == yh
    for a in range(2):
        for kv in range(2):
            prompt[a, z, kv, yl] = jnp.where(here, piece(mine, yl, a)[kv], chosen_in[1, a, kv])
            prompt[a, z, kv, other] = jnp.where(here, chosen_in[0, a, kv], chosen_in[2, a, kv])
        p[a] = prompt_gather(a, 0)
    y_do = [
        send(do_ref.at[0, :, group_lanes(other, a)], do_far.at[:, a * 1024 : a * 1024 + 1024], y_id)
        for a in range(2)
    ]
    absorb(0, pair(1), [])
    arrive([y_q[1]])
    prepare(q_far, 1, 1, q_rows, q_turned)
    absorb(1, [z] + pair(1), [])
    pass_on(1)
    pass_on_resp(2)
    absorb(0, pair(2), [])
    pass_on(2)
    absorb(1, pair(2), [])
    pass_on_resp(3)
    pass_on(3)
    absorb(0, pair(3), [])
    absorb(1, pair(3), [])
    drain()
    for h in range(2):
        arrive(r[h])
    absorb(0, opposite, [z] + pair(1) + pair(2))
    arrive([y_do[0]])
    prepare(do_far, 1, 0, do_rows, do_turned)
    arrive(p[0])
    absorb(0, [], pair(3) + opposite)
    results = [finish(0)]
    gradients(0, opposite)
    s0 = z_scatter(0, 0)
    absorb(1, opposite, [z] + pair(1) + pair(2))
    gradients(0, pair(3))
    arrive(s0)
    s0 = z_scatter(0, 1)
    arrive([y_do[1]])
    prepare(do_far, 1, 1, do_rows, do_turned)
    arrive(p[1])
    absorb(1, [], pair(3) + opposite)
    results += [finish(1)]
    own_result = fetch(out_near, out_ref.at[0, :, mine_q])
    gradients(1, opposite)
    s1 = z_scatter(1, 0)
    gradients(0, pair(2))
    arrive(s0)
    s0 = z_scatter(0, 2)
    gradients(1, pair(3))
    arrive(s1)
    s1 = z_scatter(1, 1)
    gradients(0, pair(1))
    arrive(s0)
    s0 = z_scatter(0, 3)
    gradients(1, pair(2))
    arrive(s1)
    s1 = z_scatter(1, 2)
    gradients(0, [z])
    arrive(s0)

    t0 = to_y_ring(0)
    gradients(1, pair(1))
    arrive(s1)
    s1 = z_scatter(1, 3)
    arrive(t0)
    t0 = to_core(0)
    gradients(1, [z])
    arrive(t0)
    t0 = x_scatter(0, 0)
    arrive(s1)
    t1 = to_y_ring(1)
    arrive(t0)
    t0 = x_scatter(0, 1)
    arrive(t1)
    t1 = to_core(1)
    drain()
    arrive(t1)
    t1 = x_scatter(1, 0)
    arrive(t0)
    store(0)
    arrive(t1)
    t1 = x_scatter(1, 1)
    arrive(results)
    present([own_result])
    drain()
    arrive(t1)
    store(1)


COPIES = 128


PIECES = 4


def copy_out(*refs):
    ins, outs, held = refs[:3], refs[3:6], refs[6:9]
    in_sem, out_sem = refs[9:]
    parts = [(0, slice(n * 1024, n * 1024 + 1024)) for n in range(PIECES)]
    parts += [(1, slice(0, 512)), (2, slice(0, 512))]

    def move(sources, targets, sem):
        return [
            pltpu.make_async_copy(sources[n].at[0, :, columns], targets[n].at[0, :, columns], sem.at[i])
            for i, (n, columns) in enumerate(parts)
        ]

    loads, stores = move(ins, held, in_sem), move(held, outs, out_sem)
    for copy in loads:
        copy.start()
    for load, save in zip(loads, stores):
        load.wait()
        save.start()
    for copy in stores:
        copy.wait()


def on_device(*arguments):
    block = (2, 2, PROWS, 128)
    vmem = pl.BlockSpec(memory_space=pltpu.VMEM)
    hbm = pl.BlockSpec(memory_space=pltpu.HBM)
    results = pl.pallas_call(
        kernel,
        out_shape=(
            jax.ShapeDtypeStruct((1, ROWS, 4096), BF),
            jax.ShapeDtypeStruct((1, PROWS, 512), F32),
            jax.ShapeDtypeStruct((1, PROWS, 512), F32),
        ),
        in_specs=[hbm] * 10,
        out_specs=(hbm, vmem, vmem),
        scratch_shapes=[
            pltpu.VMEM((ROWS, HALF_Q), BF),
            pltpu.VMEM((ROWS, HALF_Q), BF),
            pltpu.VMEM((ROWS, HALF_Q), BF),
            pltpu.VMEM((ROWS, HALF_Q), BF),
            pltpu.VMEM((ROWS, HALF_Q), BF),
            pltpu.VMEM((ROWS, HALF_Q), BF),
            pltpu.VMEM((16, 256, 128), BF),
            pltpu.VMEM((16, 128, 256), BF),
            pltpu.VMEM((16, 256, 128), BF),
            pltpu.VMEM((16, 128, 256), BF),
            pltpu.VMEM((Z, 2, 2, ROWS, HALF_KV), BF),
            pltpu.VMEM((X, 2, 2, PROWS, 512), BF),
            pltpu.VMEM((3, 2, 2, PROWS, 128), BF),
            pltpu.VMEM((3, 2, 2, PROWS, 128), BF),
            pltpu.VMEM((2, Z) + block, BF),
            pltpu.VMEM((144, 1024), BF),
            pltpu.VMEM((16, 1, 256), F32),
            pltpu.VMEM((16, 144, 256), F32),
            pltpu.VMEM((16, 1, 256), F32),
            pltpu.VMEM((16, 1, 256), F32),
            pltpu.VMEM((2,) + block, F32),
            pltpu.VMEM((2, 2, 4) + block, BF),
            pltpu.VMEM((2, 2, 4) + block, BF),
            pltpu.VMEM((2, 2, PROWS, 128), BF),
            pltpu.VMEM((2, 2) + block, BF),
            pltpu.VMEM((2, 2) + block, BF),
            pltpu.VMEM((2, 2, 2) + block, BF),
            pltpu.VMEM((2, 2, 2) + block, BF),
            pltpu.SMEM((16,), jnp.int32),
            pltpu.SMEM((16,), jnp.int32),
            pltpu.SMEM((16,), jnp.int32),
            pltpu.SMEM((32,), jnp.int32),
            pltpu.SemaphoreType.DMA((COPIES,)),
            pltpu.SemaphoreType.DMA((COPIES,)),
            pltpu.SemaphoreType.DMA((16,)),
        ],
        compiler_params=pltpu.CompilerParams(
            collective_id=0, has_side_effects=True, vmem_limit_bytes=60 * 1024 * 1024
        ),
        cost_estimate=pl.CostEstimate(
            flops=10_000_000_000, bytes_accessed=8 * 1024 * 1024, transcendentals=17_000_000
        ),
    )(*arguments)
    return pl.pallas_call(
        copy_out,
        out_shape=tuple(jax.ShapeDtypeStruct(r.shape, r.dtype) for r in results),
        in_specs=[pl.BlockSpec(memory_space=pl.ANY)] * 3,
        out_specs=(hbm,) * 3,
        scratch_shapes=[pltpu.VMEM(r.shape, r.dtype) for r in results]
        + [pltpu.SemaphoreType.DMA((PIECES + 2,))] * 2,
        compiler_params=pltpu.CompilerParams(vmem_limit_bytes=60 * 1024 * 1024),
    )(*results)


def solution(mesh):
    split = P("dp", "blk", None)
    return jax.shard_map(
        on_device,
        mesh=mesh,
        in_specs=(split,) * 6 + (P(),) * 4,
        out_specs=(split, split, split),
        check_vma=False,
    )
```

time: 109 us -> 98.6 us (0.905)
  Pallas kernels: 104 us -> 97.7 us
  local copies, waits for them, and re-layouts: 3.93 us -> 0 us
    pallas_call x1, Pallas kernels: 104 us -> 95.6 us  [on_device(): pl.pallas_call(kernel, out_shape=(jax.ShapeDtypeStruct((1, ROWS, 4096), B...]
    unnamed x7 -> x0, local copies, waits for them, and re-layouts: 3.93 us -> none
    pallas_call x0 -> x1, Pallas kernels: none -> 2.1 us  [on_device(): pl.pallas_call(copy_out, out_shape=tuple((jax.ShapeDtypeStruct(r.shape, r...]
where the time goes in v3:
time: 98.6 us; the launch traced here: 98.5 us
  Pallas kernels  97.7 us (99%)
    pallas_call x1, Pallas kernels, on_device(): pl.pallas_call(kernel, out_shape=(jax.ShapeDtypeStruct((1, ROWS, 4096), B...  95.6 us
    pallas_call x1, Pallas kernels, on_device(): pl.pallas_call(copy_out, out_shape=tuple((jax.ShapeDtypeStruct(r.shape, r...  2.1 us

profile of v3, /device:TPU:1, one launch (start us, length us, event | category | flops | bytes accessed | tf_op | source)
XLA Modules:
  0.0 98.5 jit_solution(4296145356480473239)
XLA Ops:
  0.6 95.6 %shard_map.121 = (bf16[1,128,4096]{2,1,0:T(8,128)(2,1)}, f32[1,64,512]{2,1,0:T(8,128)}, f32[1,64,512]{2,1,0:T(8,128)}) custom-call(bf16[1,128,4096]{2,1,0:T(8,128)(2,1)} %q_ref.1, bf16[1,128,512]{2,1,0:T(8,128)(2,1)} %rk_ref.1, bf16[1,128,512]{2,1,0:T(8,128)(2,1)} %rv_ref.1, bf16[1,64,512]{2,1,0:T(8,128)(2,1)} %pk_ref.1, bf16[1,64,512]{2,1,0:T(8,128)(2,1)} %pv_ref.1, ...), custom_call_target="tpu_custom_call" | custom-call | flops 10000000000 | bytes 8388608 | tf_op jit(solution)/shard_map/pallas_call | solution.py:516
  96.2 2.1 %shard_map.122 = (bf16[1,128,4096]{2,1,0:T(8,128)(2,1)}, f32[1,64,512]{2,1,0:T(8,128)}, f32[1,64,512]{2,1,0:T(8,128)}) custom-call(bf16[1,128,4096]{2,1,0:T(8,128)(2,1)} %get-tuple-element.6.refs_0_, f32[1,64,512]{2,1,0:T(8,128)} %get-tuple-element.7.refs_1_, f32[1,64,512]{2,1,0:T(8,128)} %get-tuple-element.8.refs_2_), custom_call_target="tpu_custom_call" | custom-call | tf_op jit(solution)/shard_map/pallas_call | solution.py:569

commit v4 on v3

--- a/solution.py
+++ b/solution.py
@@ -38,8 +38,8 @@
 def kernel(
     q_ref, rk_ref, rv_ref, pk_ref, pv_ref, do_ref, owner_hbm, prompt_hbm, length_hbm, half_hbm,
     out_ref, gk_ref, gv_ref,
-    q_near, q_far, do_near, do_far, out_near, out_far, q_rows, q_turned, do_rows, do_turned,
-    resp, xbuf, chosen_out, chosen_in, prompt, v_turned,
+    q_near, q_far, do_near, do_far, out_near, out_far,
+    resp_keys, resp_values, values_in, xbuf, chosen_out, chosen_in, prompt, v_turned,
     m_ref, acc_ref, lse_ref, delta_ref, gacc,
     zs_out, zs_in, share_out, share, core_in, xs_out, xs_in,
     owner_ref, prompt_ref, length_ref, half_ref,
@@ -86,8 +86,8 @@
         fetch(ref.at[0], xbuf.at[x, c, kv]) for kv, ref in enumerate((pk_ref, pv_ref))
     ]
     own_resp = [
-        fetch(ref.at[0, :, mine_kv], resp.at[z, kv, yl])
-        for kv, ref in enumerate((rk_ref, rv_ref))
+        fetch(rk_ref.at[0, :, mine_kv], resp_keys.at[z, yl]),
+        fetch(rv_ref.at[0, :, mine_kv], values_in.at[yl]),
     ]
     tables = [
         fetch(owner_hbm, owner_ref), fetch(prompt_hbm, prompt_ref),
@@ -124,8 +124,8 @@
         for kv, ref in enumerate((pk_ref, pv_ref))
     ]
     y_resp = [
-        send(ref.at[0, :, far_kv], resp.at[z, kv, yl], y_id)
-        for kv, ref in enumerate((rk_ref, rv_ref))
+        send(rk_ref.at[0, :, far_kv], resp_keys.at[z, yl], y_id),
+        send(rv_ref.at[0, :, far_kv], values_in.at[yl], y_id),
     ]
     cores = [
         send(ref.at[0], xbuf.at[x, c, kv], core_id) for kv, ref in enumerate((pk_ref, pv_ref))
@@ -146,7 +146,7 @@
         return copies
 
     def resp_gather(step, h):
-        return gather_step(lambda i, h: resp.at[i, h], z, Z, step, z_right, z_left, (h,))
+        return gather_step(lambda i, h: (resp_values if h else resp_keys).at[i], z, Z, step, z_right, z_left, (h,))
 
     def prompt_gather(a, step):
         return gather_step(lambda i, h: prompt.at[a, i, h], z, Z, step, z_right, z_left)
@@ -154,15 +154,16 @@
     def core_send(i):
         return send(xbuf.at[i, c], xbuf.at[i, c], core_id)
 
-    def prepare(source, part, a, rows, turned):
-        def body(g, carry):
-            h = a * GROUP + g
-            tile = source[:, pl.ds(pl.multiple_of(h * 128, 128), 128)]
-            rows[h, part * ROWS : (part + 1) * ROWS] = tile
-            turned[h, :, part * ROWS : (part + 1) * ROWS] = tile.T
-            return carry
-
-        lax.fori_loop(0, GROUP, body, 0, unroll=4)
+    def head_of(near, far, h):
+        columns = pl.ds(pl.multiple_of(h * 128, 128), 128)
+        return jnp.concatenate([near[:, columns], far[:, columns]], axis=0)
+
+    def turn_values():
+        for a in range(2):
+            for y in range(2):
+                resp_values[z, a, :, y * ROWS : (y + 1) * ROWS] = values_in[
+                    y, :, a * 128 : (a + 1) * 128
+                ].T
 
     present(tables)
     lane = lax.broadcasted_iota(jnp.int32, (1, 2 * ROWS), 1)
@@ -176,11 +177,6 @@
     limit = jnp.minimum(limit, last)
     down = lax.broadcasted_iota(jnp.int32, (64, 2 * ROWS), 0)
 
-    def resp_rows(slots, kv, a):
-        return [
-            resp[i, kv, :, :, a * 128 : (a + 1) * 128].reshape(2 * ROWS, 128) for i in slots
-        ]
-
     def prompt_rows(slots, kv, a):
         return [prompt[a, i, kv].reshape(2 * PROWS, 128) for i in slots]
 
@@ -192,31 +188,52 @@
         bounds += [None] * (2 * len(prompt_slots))
         count = 64 * len(bounds)
 
-        def all_rows(kv):
-            parts = resp_rows(resp_slots, kv, a) + prompt_rows(prompt_slots, kv, a)
-            return jnp.concatenate(parts, axis=0) if len(parts) > 1 else parts[0]
-
-        v_turned[:128, :count] = all_rows(1).T
-
-        def hide(scores):
-            pieces = []
-            for n, bound in enumerate(bounds):
-                piece = scores[64 * n : 64 * n + 64]
-                pieces.append(piece if bound is None else jnp.where(down <= bound, piece, MASKED))
-            return jnp.concatenate(pieces, axis=0)
+        keys = [
+            resp_keys[i, :, :, a * 128 : (a + 1) * 128].reshape(2 * ROWS, 128) for i in resp_slots
+        ] + prompt_rows(prompt_slots, 0, a)
+        for n, part in enumerate(prompt_rows(prompt_slots, 1, a)):
+            v_turned[:, n * 128 : n * 128 + 128] = part.T
+
+        def score(query):
+            pieces, tops, n = [], [], 0
+            for part in keys:
+                scores = nt(part, query) * SCORE_SCALE
+                for m in range(part.shape[0] // 64):
+                    piece = scores[64 * m : 64 * m + 64]
+                    if bounds[n] is not None:
+                        piece = jnp.where(down <= bounds[n], piece, MASKED)
+                    tops.append(jnp.max(piece.reshape(8, 8, 2 * ROWS), axis=0))
+                    pieces.append(piece)
+                    n += 1
+            while len(tops) > 1:
+                tops = [
+                    jnp.maximum(tops[i], tops[i + 1]) if i + 1 < len(tops) else tops[i]
+                    for i in range(0, len(tops), 2)
+                ]
+            return jnp.concatenate(pieces, axis=0), jnp.max(tops[0], axis=0, keepdims=True)
 
         def body(t, carry):
             first = a * GROUP + t * 4
             heads = pl.ds(first, 4)
-            keys, values = all_rows(0), v_turned[:, :count]
+            values = [resp_values[i, a] for i in resp_slots]
+            if prompt_slots:
+                values.append(v_turned[:, : 128 * len(prompt_slots)])
+            values = jnp.concatenate(values, axis=1) if len(values) > 1 else values[0]
+            values = jnp.concatenate([values, jnp.ones((16, count), BF)], axis=0)
             old, old_mixed = m_ref[heads], acc_ref[heads]
-            scores = [hide(nn(keys, q_turned[first + j]) * SCORE_SCALE) for j in range(4)]
             peaks, mixes = [], []
-            for j in range(4):
-                peak = jnp.maximum(old[j], jnp.max(scores[j], axis=0, keepdims=True))
-                weights = jnp.exp2(scores[j] - peak).astype(BF)
+
+            def weigh(j, scores, top):
+                peak = jnp.maximum(old[j], top)
+                weights = jnp.exp2(scores - peak).astype(BF)
                 peaks.append(peak)
                 mixes.append(old_mixed[j] * jnp.exp2(old[j] - peak) + nn(values, weights))
+
+            ready = score(head_of(q_near, q_far, first))
+            for j in range(4):
+                following = score(head_of(q_near, q_far, first + j + 1)) if j < 3 else None
+                weigh(j, *ready)
+                ready = following
             for j in range(4):
                 m_ref[first + j] = peaks[j]
                 acc_ref[first + j] = mixes[j]
@@ -228,14 +245,18 @@
         def body(t, carry):
             first = a * GROUP + t * 4
             heads = pl.ds(first, 4)
-            peak, mixed, turned = m_ref[heads], acc_ref[heads], do_turned[heads]
+            peak, mixed = m_ref[heads], acc_ref[heads]
             outs, sums, deltas = [], [], []
             for j in range(4):
                 total = mixed[j, 128:129]
-                result = mixed[j, :128] / total
+                result = (mixed[j, :128] / total).T
                 sums.append(peak[j] + jnp.log(total) * LOG2E)
-                deltas.append(jnp.sum(turned[j].astype(F32) * result, axis=0, keepdims=True))
-                outs.append(result.T.astype(BF))
+                product = result * head_of(do_near, do_far, first + j).astype(F32)
+                high = product.astype(BF)
+                low = (product - high.astype(F32)).astype(BF)
+                halves = jnp.concatenate([high, low], axis=1)
+                deltas.append(nt(jnp.ones((16, 256), BF), halves)[:1])
+                outs.append(result.astype(BF))
             for j in range(4):
                 h = first + j
                 lse_ref[h] = sums[j]
@@ -253,15 +274,17 @@
     def gradients(a, slots):
         keys = jnp.concatenate(prompt_rows(slots, 0, a), axis=0)
         values = jnp.concatenate(prompt_rows(slots, 1, a), axis=0)
+        heads = range(a * GROUP, a * GROUP + GROUP)
+        queries = [head_of(q_near, q_far, h) for h in heads]
+        cotangents = [head_of(do_near, do_far, h) for h in heads]
         all_probs, all_slopes = [], []
-        for h in range(a * GROUP, a * GROUP + GROUP):
-            probs = jnp.exp2(nn(keys, q_turned[h]) * SCORE_SCALE - lse_ref[h])
-            slopes = probs * (nn(values, do_turned[h]) - delta_ref[h])
+        for h, query, cotangent in zip(heads, queries, cotangents):
+            probs = jnp.exp2(nt(keys, query) * SCORE_SCALE - lse_ref[h])
+            slopes = probs * (nt(values, cotangent) - delta_ref[h])
             all_probs.append(probs.astype(BF))
             all_slopes.append(slopes.astype(BF))
-        heads = slice(a * GROUP, a * GROUP + GROUP)
-        queries = q_rows[heads].reshape(GROUP * 2 * ROWS, 128)
-        cotangents = do_rows[heads].reshape(GROUP * 2 * ROWS, 128)
+        queries = jnp.concatenate(queries, axis=0)
+        cotangents = jnp.concatenate(cotangents, axis=0)
         key_part = nn(jnp.concatenate(all_slopes, axis=1), queries) * SCALE
         value_part = nn(jnp.concatenate(all_probs, axis=1), cotangents)
         for n in range(len(slots)):
@@ -338,7 +361,6 @@
 
     m_ref[...] = jnp.full(m_ref.shape, LOWEST, F32)
     acc_ref[...] = jnp.zeros(acc_ref.shape, F32)
-    v_turned[128:] = jnp.ones((16, v_turned.shape[1]), BF)
 
     def pair(step):
         return [(z + step) % Z, (z + Z - step) % Z]
@@ -356,22 +378,18 @@
             arrive(r[h])
             r[h] = resp_gather(step, h)
 
-    present([own_q])
-    for a in range(2):
-        prepare(q_near, 0, a, q_rows, q_turned)
     arrive(x0)
     x1 = gather_step(lambda i, h: xbuf.at[i, c, h], x, X, 1, x_right, x_left)
     cores += [core_send((x + 1) % X), core_send((x + X - 1) % X)]
     present(own_resp)
-    for h in range(2):
-        arrive([y_resp[h]])
-        r[h] = resp_gather(0, h)
+    arrive([y_resp[0]])
+    r[0] = resp_gather(0, 0)
+    arrive([y_resp[1]])
+    turn_values()
+    r[1] = resp_gather(0, 1)
     arrive(x1)
     cores += [core_send((x + 2) % X)]
-    present([own_do])
-    for a in range(2):
-        prepare(do_near, 0, a, do_rows, do_turned)
-    present(own_prompt)
+    present(own_prompt + [own_q, own_do])
     arrive(cores)
     theirs = owner_ref[prompt_ref[x * 4 + (1 - yh) * 2 + c]]
     mine = owner_ref[prompt_ref[dp]]
@@ -387,7 +405,6 @@
             chosen_out[n, a] = piece(owner, half, a)
         ring.append(send(chosen_out.at[n], chosen_in.at[n], peer))
     arrive([y_q[0]])
-    prepare(q_far, 1, 0, q_rows, q_turned)
     absorb(0, [z], [])
     pass_on_resp(1)
     arrive(ring)
@@ -403,7 +420,6 @@
     ]
     absorb(0, pair(1), [])
     arrive([y_q[1]])
-    prepare(q_far, 1, 1, q_rows, q_turned)
     absorb(1, [z] + pair(1), [])
     pass_on(1)
     pass_on_resp(2)
@@ -419,7 +435,6 @@
         arrive(r[h])
     absorb(0, opposite, [z] + pair(1) + pair(2))
     arrive([y_do[0]])
-    prepare(do_far, 1, 0, do_rows, do_turned)
     arrive(p[0])
     absorb(0, [], pair(3) + opposite)
     results = [finish(0)]
@@ -430,7 +445,6 @@
     arrive(s0)
     s0 = z_scatter(0, 1)
     arrive([y_do[1]])
-    prepare(do_far, 1, 1, do_rows, do_turned)
     arrive(p[1])
     absorb(1, [], pair(3) + opposite)
     results += [finish(1)]
@@ -529,16 +543,14 @@
             pltpu.VMEM((ROWS, HALF_Q), BF),
             pltpu.VMEM((ROWS, HALF_Q), BF),
             pltpu.VMEM((ROWS, HALF_Q), BF),
-            pltpu.VMEM((16, 256, 128), BF),
-            pltpu.VMEM((16, 128, 256), BF),
-            pltpu.VMEM((16, 256, 128), BF),
-            pltpu.VMEM((16, 128, 256), BF),
-            pltpu.VMEM((Z, 2, 2, ROWS, HALF_KV), BF),
+            pltpu.VMEM((Z, 2, ROWS, HALF_KV), BF),
+            pltpu.VMEM((Z, 2, 128, 2 * ROWS), BF),
+            pltpu.VMEM((2, ROWS, HALF_KV), BF),
             pltpu.VMEM((X, 2, 2, PROWS, 512), BF),
             pltpu.VMEM((3, 2, 2, PROWS, 128), BF),
             pltpu.VMEM((3, 2, 2, PROWS, 128), BF),
             pltpu.VMEM((2, Z) + block, BF),
-            pltpu.VMEM((144, 1024), BF),
+            pltpu.VMEM((128, 1024), BF),
             pltpu.VMEM((16, 1, 256), F32),
             pltpu.VMEM((16, 144, 256), F32),
             pltpu.VMEM((16, 1, 256), F32),

time: 98.6 us -> 101 us (1.024)
  Pallas kernels: 97.7 us -> 100 us
    pallas_call x1, Pallas kernels: 95.6 us -> 98 us  [on_device(): pl.pallas_call(kernel, out_shape=(jax.ShapeDtypeStruct((1, ROWS, 4096), B...]
where the time goes in v4:
time: 101 us
  Pallas kernels  100 us (99%)
    pallas_call x1, Pallas kernels, on_device(): pl.pallas_call(kernel, out_shape=(jax.ShapeDtypeStruct((1, ROWS, 4096), B...  98 us
    pallas_call x1, Pallas kernels, on_device(): pl.pallas_call(copy_out, out_shape=tuple((jax.ShapeDtypeStruct(r.shape, r...  2.1 us

profile of v4, /device:TPU:1, one launch (start us, length us, event | category | flops | bytes accessed | tf_op | source)
XLA Modules:
  0.0 100.9 jit_solution(3400873999706209745)
XLA Ops:
  0.6 98.0 %shard_map.121 = (bf16[1,128,4096]{2,1,0:T(8,128)(2,1)}, f32[1,64,512]{2,1,0:T(8,128)}, f32[1,64,512]{2,1,0:T(8,128)}) custom-call(bf16[1,128,4096]{2,1,0:T(8,128)(2,1)} %q_ref.1, bf16[1,128,512]{2,1,0:T(8,128)(2,1)} %rk_ref.1, bf16[1,128,512]{2,1,0:T(8,128)(2,1)} %rv_ref.1, bf16[1,64,512]{2,1,0:T(8,128)(2,1)} %pk_ref.1, bf16[1,64,512]{2,1,0:T(8,128)(2,1)} %pv_ref.1, ...), custom_call_target="tpu_custom_call" | custom-call | flops 10000000000 | bytes 8388608 | tf_op jit(solution)/shard_map/pallas_call | solution.py:530
  98.7 2.1 %shard_map.122 = (bf16[1,128,4096]{2,1,0:T(8,128)(2,1)}, f32[1,64,512]{2,1,0:T(8,128)}, f32[1,64,512]{2,1,0:T(8,128)}) custom-call(bf16[1,128,4096]{2,1,0:T(8,128)(2,1)} %get-tuple-element.6.refs_0_, f32[1,64,512]{2,1,0:T(8,128)} %get-tuple-element.7.refs_1_, f32[1,64,512]{2,1,0:T(8,128)} %get-tuple-element.8.refs_2_), custom_call_target="tpu_custom_call" | custom-call | tf_op jit(solution)/shard_map/pallas_call | solution.py:581

commit v5 on v4

v5 whole, which is shorter than its diff:
```python
import jax
import jax.numpy as jnp
from jax import lax
from jax.experimental import pallas as pl
from jax.experimental.pallas import tpu as pltpu
from jax.sharding import PartitionSpec as P

MESH = pl.DeviceIdType.MESH
HEAD_WIDTH = 128
SCALE = HEAD_WIDTH ** (-0.5)
LOG2E = 1.4426950408889634
SCORE_SCALE = SCALE * LOG2E
MASKED = -1e30
LOWEST = -1e20
BF = jnp.bfloat16
F32 = jnp.float32

X, YH, CORES, YL, Z = 4, 2, 2, 2, 8
GROUP = 8
ROWS = 128
PROWS = 64
HALF_KV = 256
HALF_Q = 2048


def nt(a, b):
    return lax.dot_general(a, b, (((1,), (1,)), ((), ())), preferred_element_type=F32)


def nn(a, b):
    return lax.dot_general(a, b, (((1,), (0,)), ((), ())), preferred_element_type=F32)


def tn(a, b):
    return lax.dot_general(a, b, (((0,), (0,)), ((), ())), preferred_element_type=F32)


def kernel(
    q_ref, rk_ref, rv_ref, pk_ref, pv_ref, do_ref, owner_hbm, prompt_hbm, length_hbm, half_hbm,
    out_ref, gk_ref, gv_ref,
    q_near, q_far, do_near, do_far, out_near, out_far,
    resp_keys, resp_values, values_in, xbuf, chosen_out, chosen_in, prompt, limit_ref,
    m_ref, acc_ref, lse_ref, delta_ref, gacc,
    zs_out, zs_in, share_out, share, core_in, xs_out, xs_in,
    owner_ref, prompt_ref, length_ref, half_ref,
    send_sem, recv_sem, local_sem,
):
    dp = lax.axis_index("dp")
    blk = lax.axis_index("blk")
    x, yh, c = dp // 4, (dp // 2) % 2, dp % 2
    yl, z = blk // Z, blk % Z
    other = 1 - yl
    y_id = (dp, other * Z + z)
    z_right, z_left = (dp, yl * Z + (z + 1) % Z), (dp, yl * Z + (z + Z - 1) % Z)
    x_right = (((x + 1) % X) * 4 + yh * 2 + c, blk)
    x_left = (((x + X - 1) % X) * 4 + yh * 2 + c, blk)
    core_id = (x * 4 + yh * 2 + (1 - c), blk)
    yh_id = (x * 4 + (1 - yh) * 2 + c, blk)
    diagonal_id = (x * 4 + (1 - yh) * 2 + c, other * Z + z)

    def lanes(which, width):
        return pl.ds(pl.multiple_of(which * width, width), width)

    def head_lanes(half, a):
        return pl.ds(pl.multiple_of(half * HALF_KV + a * 128, 128), 128)

    def group_lanes(half, a):
        return pl.ds(pl.multiple_of(half * HALF_Q + a * 1024, 1024), 1024)

    mine_kv, far_kv = lanes(yl, HALF_KV), lanes(other, HALF_KV)
    mine_q = lanes(yl, HALF_Q)

    fetched = []

    def fetch(src, dst):
        copy = pltpu.make_async_copy(src, dst, local_sem.at[len(fetched)])
        copy.start()
        fetched.append(copy)
        return copy

    def present(copies):
        for copy in copies:
            copy.wait()

    own_prompt = [
        fetch(ref.at[0], xbuf.at[x, c, kv]) for kv, ref in enumerate((pk_ref, pv_ref))
    ]
    own_resp = [
        fetch(rk_ref.at[0, :, mine_kv], resp_keys.at[z, yl]),
        fetch(rv_ref.at[0, :, mine_kv], values_in.at[yl]),
    ]
    tables = [
        fetch(owner_hbm, owner_ref), fetch(prompt_hbm, prompt_ref),
        fetch(length_hbm, length_ref), fetch(half_hbm, half_ref),
    ]
    own_q = fetch(q_ref.at[0, :, mine_q], q_near)
    own_do = fetch(do_ref.at[0, :, mine_q], do_near)

    barrier = pltpu.get_barrier_semaphore()
    peers = (y_id, z_right, z_left, x_right, x_left, core_id, yh_id, diagonal_id)
    for peer in peers:
        pl.semaphore_signal(barrier, inc=1, device_id=peer, device_id_type=MESH)
    pl.semaphore_wait(barrier, len(peers))

    total = [0]

    def room(n):
        total[0] += n
        return total[0] - n

    def copy(index, src, dst, peer):
        return pltpu.make_async_remote_copy(
            src_ref=src, dst_ref=dst, send_sem=send_sem.at[index], recv_sem=recv_sem.at[index],
            device_id=peer, device_id_type=MESH,
        )

    def start(copies):
        for one in copies:
            one.start()

    def arrive(copies):
        for one in copies:
            one.wait_recv()

    def drain(copies):
        for one in copies:
            one.wait_send()

    def gather(base, slot, pos, n, step, right, left, halves):
        copies = []
        for h in halves:
            for way, peer in enumerate((right, left)):
                if step < n // 2 - 1 or h == way:
                    at = slot((pos + n - step) % n if way == 0 else (pos + step) % n, h)
                    copies.append(copy(base + h * 2 + way, at, at, peer))
        return copies

    x_base, core_base, ys_base, yq_base, yd_base = room(8), room(5), room(2), room(2), room(2)
    ring_base, r_base, p_base, result_base = room(3), room(16), room(32), room(2)
    zs_base, yr_base, cs_base, xs_base = room(32), room(6), room(2), room(16)

    def x_copies(step):
        if step == 0:
            return [
                copy(x_base + kv * 2 + way, ref.at[0], xbuf.at[x, c, kv], peer)
                for way, peer in enumerate((x_right, x_left))
                for kv, ref in enumerate((pk_ref, pv_ref))
            ]
        return gather(
            x_base + 4, lambda i, h: xbuf.at[i, c, h], x, X, 1, x_right, x_left, (0, 1)
        )

    def core_copies(which):
        if which == 0:
            return [
                copy(core_base + kv, ref.at[0], xbuf.at[x, c, kv], core_id)
                for kv, ref in enumerate((pk_ref, pv_ref))
            ]
        slots = ((x + 1) % X, (x + X - 1) % X) if which == 1 else ((x + 2) % X,)
        return [
            copy(core_base + which * 2 + n, xbuf.at[i, c], xbuf.at[i, c], core_id)
            for n, i in enumerate(slots)
        ]

    y_resp = [
        copy(ys_base, rk_ref.at[0, :, far_kv], resp_keys.at[z, yl], y_id),
        copy(ys_base + 1, rv_ref.at[0, :, far_kv], values_in.at[yl], y_id),
    ]

    def y_group(base, ref, far):
        return [
            copy(base + a, ref.at[0, :, group_lanes(other, a)], far.at[:, a * 1024 : a * 1024 + 1024], y_id)
            for a in range(2)
        ]

    y_q, y_do = y_group(yq_base, q_ref, q_far), y_group(yd_base, do_ref, do_far)
    ring = [
        copy(ring_base + n, chosen_out.at[n], chosen_in.at[n], peer)
        for n, peer in enumerate((y_id, yh_id, diagonal_id))
    ]

    def r_copies(step, h):
        return gather(
            r_base + step * 4, lambda i, h: (resp_values if h else resp_keys).at[i],
            z, Z, step, z_right, z_left, (h,),
        )

    def p_copies(a, step):
        return gather(
            p_base + a * 16 + step * 4, lambda i, h: prompt.at[a, i, h],
            z, Z, step, z_right, z_left, (0, 1),
        )

    def result_copies(a):
        columns = pl.ds(pl.multiple_of(a * 1024, 1024), 1024)
        return [copy(result_base + a, out_far.at[:, columns], out_ref.at[0, :, group_lanes(yl, a)], y_id)]

    def sums(base, outgoing, incoming, a, step, right, left):
        return [
            copy(
                base + step * 4 + way * 2 + h,
                outgoing.at[a, way, step, h], incoming.at[a, way, step, h], peer,
            )
            for way, peer in enumerate((right, left))
            for h in range(2)
            if step > 0 or h == way
        ]

    def zs_copies(a, step):
        return sums(zs_base + a * 16, zs_out, zs_in, a, step, z_right, z_left)

    def xs_copies(a, step):
        return sums(xs_base + a * 8, xs_out, xs_in, a, step, x_right, x_left)

    def yr_copies(a):
        return [
            copy(yr_base + a * 3, share_out.at[a], share.at[a, 0, 1], y_id),
            copy(yr_base + a * 3 + 1, share.at[a, 0, 0], share.at[a, 1, 0], yh_id),
            copy(yr_base + a * 3 + 2, share_out.at[a], share.at[a, 1, 1], diagonal_id),
        ]

    def cs_copies(a):
        return [copy(cs_base + a, share.at[a], core_in.at[a], core_id)]

    def head_of(near, far, h):
        columns = pl.ds(pl.multiple_of(h * 128, 128), 128)
        return jnp.concatenate([near[:, columns], far[:, columns]], axis=0)

    def loop(count, body):
        def step(i, carry):
            body(i)
            return carry

        lax.fori_loop(0, count, step, 0)

    start(x_copies(0))
    start(y_resp)
    start(core_copies(0))
    start(y_q)

    present(tables)
    lane = lax.broadcasted_iota(jnp.int32, (1, 2 * ROWS), 1)
    last = length_ref[dp] - 1
    limit = jnp.zeros((1, 2 * ROWS), jnp.int32)
    for part, holder in enumerate((blk, other * Z + z)):
        for e in range(2):
            block = part * 2 + e
            inside = (lane >= block * 64) & (lane < block * 64 + 64)
            limit = jnp.where(inside, half_ref[2 * holder + e] * 64 + lane - block * 64, limit)
    limit_ref[...] = jnp.minimum(limit, last)
    m_ref[...] = jnp.full(m_ref.shape, LOWEST, F32)
    acc_ref[...] = jnp.zeros(acc_ref.shape, F32)

    def absorb(a, keys, values, bounds):
        def score(query):
            pieces, tops = [], []
            down = lax.broadcasted_iota(jnp.int32, (64, 2 * ROWS), 0)
            for part, offset in zip(keys, range(0, 64 * len(bounds), keys[0].shape[0])):
                scores = nt(part, query) * SCORE_SCALE
                for m in range(part.shape[0] // 64):
                    piece, bound = scores[64 * m : 64 * m + 64], bounds[offset // 64 + m]
                    if bound is not None:
                        piece = jnp.where(down <= bound, piece, MASKED)
                    tops.append(jnp.max(piece.reshape(8, 8, 2 * ROWS), axis=0))
                    pieces.append(piece)
            while len(tops) > 1:
                tops = [jnp.maximum(tops[i], tops[i + 1]) for i in range(0, len(tops), 2)]
            return jnp.concatenate(pieces, axis=0), jnp.max(tops[0], axis=0, keepdims=True)

        values = jnp.concatenate([values, jnp.ones((16, 64 * len(bounds)), BF)], axis=0)

        def body(t):
            first = a * GROUP + t * UNROLL
            heads = pl.ds(first, UNROLL)
            old, old_mixed = m_ref[heads], acc_ref[heads]
            peaks, mixes = [], []

            def weigh(j, scores, top):
                peak = jnp.maximum(old[j], top)
                weights = jnp.exp2(scores - peak).astype(BF)
                peaks.append(peak)
                mixes.append(old_mixed[j] * jnp.exp2(old[j] - peak) + nn(values, weights))

            ready = score(head_of(q_near, q_far, first))
            for j in range(UNROLL):
                following = score(head_of(q_near, q_far, first + j + 1)) if j < UNROLL - 1 else None
                weigh(j, *ready)
                ready = following
            for j in range(UNROLL):
                m_ref[first + j] = peaks[j]
                acc_ref[first + j] = mixes[j]

        loop(GROUP // UNROLL, body)

    def absorb_resp(a, slots):
        columns = pl.ds(pl.multiple_of(a * 128, 128), 128)
        keys = [resp_keys[i, :, :, columns].reshape(2 * ROWS, 128) for i in slots]
        values = jnp.concatenate([resp_values[i, a] for i in slots], axis=1)
        limit = limit_ref[...]
        bounds = [
            limit - half_ref[2 * ((n // 2) * Z + i) + n % 2] * 64 for i in slots for n in range(4)
        ]
        absorb(a, keys, values, bounds)

    def absorb_prompt(a, slots):
        keys = jnp.concatenate([prompt[a, i, 0].reshape(2 * PROWS, 128) for i in slots], axis=0)
        values = [prompt[a, i, 1].reshape(2 * PROWS, 128).T for i in slots]
        absorb(a, [keys], jnp.concatenate(values, axis=1), [None] * (2 * len(slots)))

    def finish(a):
        def body(t):
            first = a * GROUP + t * UNROLL
            heads = pl.ds(first, UNROLL)
            peak, mixed = m_ref[heads], acc_ref[heads]
            outs, logs, deltas = [], [], []
            for j in range(UNROLL):
                total = mixed[j, 128:129]
                result = (mixed[j, :128] / total).T
                logs.append(peak[j] + jnp.log(total) * LOG2E)
                product = result * head_of(do_near, do_far, first + j).astype(F32)
                high = product.astype(BF)
                low = (product - high.astype(F32)).astype(BF)
                halves = jnp.concatenate([high, low], axis=1)
                deltas.append(nt(jnp.ones((16, 256), BF), halves)[:1])
                outs.append(result.astype(BF))
            for j in range(UNROLL):
                h = first + j
                lse_ref[h] = logs[j]
                delta_ref[h] = deltas[j]
                columns = pl.ds(pl.multiple_of(h * 128, 128), 128)
                out_near[:, columns] = outs[j][:ROWS]
                out_far[:, columns] = outs[j][ROWS:]

        loop(GROUP // UNROLL, body)

    def gradients(a, k, slots):
        keys = jnp.concatenate([prompt[a, i, 0].reshape(2 * PROWS, 128) for i in slots], axis=0)
        values = jnp.concatenate([prompt[a, i, 1].reshape(2 * PROWS, 128) for i in slots], axis=0)
        heads = [a * GROUP + j for j in range(GROUP)]
        queries = [head_of(q_near, q_far, h) for h in heads]
        cotangents = [head_of(do_near, do_far, h) for h in heads]
        all_probs, all_slopes = [], []
        for h, query, cotangent in zip(heads, queries, cotangents):
            probs = jnp.exp2(nt(keys, query) * SCORE_SCALE - lse_ref[h])
            slopes = probs * (nt(values, cotangent) - delta_ref[h])
            all_probs.append(probs.astype(BF))
            all_slopes.append(slopes.astype(BF))
        queries = jnp.concatenate(queries, axis=0)
        cotangents = jnp.concatenate(cotangents, axis=0)
        key_part = nn(jnp.concatenate(all_slopes, axis=1), queries) * SCALE
        value_part = nn(jnp.concatenate(all_probs, axis=1), cotangents)
        for n in range(2):
            gacc[a, k, n, 0] = key_part[n * 128 : n * 128 + 128].reshape(2, PROWS, 128)
            gacc[a, k, n, 1] = value_part[n * 128 : n * 128 + 128].reshape(2, PROWS, 128)

    def z_messages(a, step):
        for way in range(2):
            for h in range(2):
                if step > 0 or h == way:
                    if way == 0 and step > 0:
                        part = gacc[a, step - 1, 1, h]
                    else:
                        part = gacc[a, step, 0, h]
                    if step > 1 or (step == 1 and h == way):
                        part = part + zs_in[a, way, step - 1, h].astype(F32)
                    zs_out[a, way, step, h] = part.astype(BF)
        start(zs_copies(a, step))

    def to_y_ring(a):
        for h in range(2):
            for n, where in enumerate((yl, other)):
                part = gacc[a, 3, 1, h, where]
                for way in range(2):
                    part = part + zs_in[a, way, 3, h, where].astype(F32)
                (share.at[a, 0, 0] if n == 0 else share_out.at[a])[h] = part.astype(BF)
        start(yr_copies(a))

    def destined(a, target, h):
        result = jnp.zeros((2, PROWS, 128), F32)
        for n in range(4):
            source = x * 4 + (yh if n % 2 == 0 else 1 - yh) * 2 + (c if n < 2 else 1 - c)
            owner = owner_ref[prompt_ref[source]]
            part = (share if n < 2 else core_in)[a, n % 2, :, h].astype(F32)
            result = result + jnp.where(owner == target * 4 + yh * 2 + c, part, 0.0)
        return result

    def x_messages(a, step):
        for way in range(2):
            distance = 2 - step
            target = (x + distance) % X if way == 0 else (x + X - distance) % X
            for h in range(2):
                if step > 0 or h == way:
                    part = destined(a, target, h)
                    if step == 1 and h == way:
                        part = part + xs_in[a, way, 0, h].astype(F32)
                    xs_out[a, way, step, h] = part.astype(BF)
        start(xs_copies(a, step))

    def store(a):
        for h, ref in enumerate((gk_ref, gv_ref)):
            part = destined(a, x, h)
            for way in range(2):
                part = part + xs_in[a, way, 1, h].astype(F32)
            ref[0, :, head_lanes(yl, a)] = part[0]
            ref[0, :, head_lanes(other, a)] = part[1]

    arrive(x_copies(0))
    start(x_copies(1))
    start(core_copies(1))
    present(own_resp)
    arrive(y_resp[:1])
    start(r_copies(0, 0))
    arrive(y_resp[1:])
    for a in range(2):
        for y in range(2):
            resp_values[z, a, :, y * ROWS : (y + 1) * ROWS] = values_in[
                y, :, a * 128 : (a + 1) * 128
            ].T
    start(r_copies(0, 1))
    arrive(x_copies(1))
    start(core_copies(2))
    present(own_prompt + [own_q, own_do])
    for which in range(3):
        arrive(core_copies(which))
    theirs = owner_ref[prompt_ref[x * 4 + (1 - yh) * 2 + c]]
    mine = owner_ref[prompt_ref[dp]]

    def piece(owner, half, a):
        return xbuf[owner // 4, owner % 2, :, :, head_lanes(half, a)]

    for n, (owner, half) in enumerate(((mine, other), (theirs, yl), (theirs, other))):
        for a in range(2):
            chosen_out[n, a] = piece(owner, half, a)
        start(ring[n : n + 1])

    def pass_on(step):
        for a in range(2):
            arrive(p_copies(a, step - 1))
            start(p_copies(a, step))

    def resp_unit(u):
        a, s = u % 2, u // 2

        @pl.when(u == 0)
        def _():
            arrive(y_q[:1])

        @pl.when(u == 1)
        def _():
            arrive(y_q[1:])
            arrive(ring)
            here = (mine // 2) % 2 == yh
            for a in range(2):
                for kv in range(2):
                    prompt[a, z, kv, yl] = jnp.where(
                        here, piece(mine, yl, a)[kv], chosen_in[1, a, kv]
                    )
                    prompt[a, z, kv, other] = jnp.where(
                        here, chosen_in[0, a, kv], chosen_in[2, a, kv]
                    )
                start(p_copies(a, 0))
            start(y_do)

        for step in range(1, 5):

            @pl.when(u == 2 * step - 2)
            def _():
                for h in range(2):
                    arrive(r_copies(step - 1, h))
                    if step < 4:
                        start(r_copies(step, h))

            if step < 4:

                @pl.when(u == 2 * step + 1)
                def _():
                    pass_on(step)

        absorb_resp(a, [(z + Z - s) % Z, (z + s + 1) % Z])

    loop(8, resp_unit)
    arrive(y_do)

    def key_head(a):
        def prompt_unit(w):
            @pl.when(w == 1)
            def _():
                arrive(p_copies(a, 3))

            sign = 1 - 2 * w
            absorb_prompt(
                a,
                [(z + 4 * w) % Z, (z + Z + 4 * w + sign) % Z, (z + Z - 4 * w - sign) % Z, (z + 2 + 4 * w) % Z],
            )

        loop(2, prompt_unit)

        @pl.when(a == 1)
        def _():
            arrive(zs_copies(0, 3))
            to_y_ring(0)

        finish(a)
        start(result_copies(a))

        @pl.when(a == 1)
        def _():
            arrive(yr_copies(0))
            start(cs_copies(0))

        def gradient_unit(k):
            gradients(a, k, [(z + 4 + k) % Z, (z + 3 + Z - k) % Z])
            for step in range(4):

                @pl.when(k == step)
                def _():
                    if step > 0:
                        arrive(zs_copies(a, step - 1))
                    z_messages(a, step)

            for step in range(3):

                @pl.when((a == 1) & (k == step))
                def _():
                    if step == 0:
                        arrive(cs_copies(0))
                        x_messages(0, 0)
                    elif step == 1:
                        arrive(xs_copies(0, 0))
                        x_messages(0, 1)
                    else:
                        arrive(xs_copies(0, 1))
                        store(0)

        loop(4, gradient_unit)

    loop(2, key_head)
    own_result = fetch(out_near, out_ref.at[0, :, mine_q])

    early = [x_copies(0), x_copies(1), core_copies(0), core_copies(1), core_copies(2)]
    early += [y_resp, y_q, y_do, ring, zs_copies(0, 3), yr_copies(0), cs_copies(0)]
    for step in range(4):
        early += [r_copies(step, h) for h in range(2)] + [p_copies(a, step) for a in range(2)]
    for step in range(3):
        early += [zs_copies(a, step) for a in range(2)]
    early += [xs_copies(0, 0), xs_copies(0, 1)]
    for copies in early[: len(early) // 2]:
        drain(copies)
    arrive(zs_copies(1, 3))
    to_y_ring(1)
    for copies in early[len(early) // 2 :]:
        drain(copies)
    arrive(yr_copies(1))
    start(cs_copies(1))
    drain(zs_copies(1, 3))
    for a in range(2):
        arrive(result_copies(a))
        drain(result_copies(a))
    present([own_result])
    arrive(cs_copies(1))
    x_messages(1, 0)
    drain(yr_copies(1) + cs_copies(1))
    arrive(xs_copies(1, 0))
    x_messages(1, 1)
    drain(xs_copies(1, 0))
    arrive(xs_copies(1, 1))
    store(1)
    drain(xs_copies(1, 1))


COPIES = 128
UNROLL = 4
PIECES = 4


def copy_out(*refs):
    ins, outs, held = refs[:3], refs[3:6], refs[6:9]
    in_sem, out_sem = refs[9:]
    parts = [(0, slice(n * 1024, n * 1024 + 1024)) for n in range(PIECES)]
    parts += [(1, slice(0, 512)), (2, slice(0, 512))]

    def move(sources, targets, sem):
        return [
            pltpu.make_async_copy(sources[n].at[0, :, columns], targets[n].at[0, :, columns], sem.at[i])
            for i, (n, columns) in enumerate(parts)
        ]

    loads, stores = move(ins, held, in_sem), move(held, outs, out_sem)
    for copy in loads:
        copy.start()
    for load, save in zip(loads, stores):
        load.wait()
        save.start()
    for copy in stores:
        copy.wait()


def on_device(*arguments):
    block = (2, 2, PROWS, 128)
    vmem = pl.BlockSpec(memory_space=pltpu.VMEM)
    hbm = pl.BlockSpec(memory_space=pltpu.HBM)
    results = pl.pallas_call(
        kernel,
        out_shape=(
            jax.ShapeDtypeStruct((1, ROWS, 4096), BF),
            jax.ShapeDtypeStruct((1, PROWS, 512), F32),
            jax.ShapeDtypeStruct((1, PROWS, 512), F32),
        ),
        in_specs=[hbm] * 10,
        out_specs=(hbm, vmem, vmem),
        scratch_shapes=[
            pltpu.VMEM((ROWS, HALF_Q), BF),
            pltpu.VMEM((ROWS, HALF_Q), BF),
            pltpu.VMEM((ROWS, HALF_Q), BF),
            pltpu.VMEM((ROWS, HALF_Q), BF),
            pltpu.VMEM((ROWS, HALF_Q), BF),
            pltpu.VMEM((ROWS, HALF_Q), BF),
            pltpu.VMEM((Z, 2, ROWS, HALF_KV), BF),
            pltpu.VMEM((Z, 2, 128, 2 * ROWS), BF),
            pltpu.VMEM((2, ROWS, HALF_KV), BF),
            pltpu.VMEM((X, 2, 2, PROWS, 512), BF),
            pltpu.VMEM((3, 2, 2, PROWS, 128), BF),
            pltpu.VMEM((3, 2, 2, PROWS, 128), BF),
            pltpu.VMEM((2, Z) + block, BF),
            pltpu.VMEM((1, 2 * ROWS), jnp.int32),
            pltpu.VMEM((16, 1, 256), F32),
            pltpu.VMEM((16, 144, 256), F32),
            pltpu.VMEM((16, 1, 256), F32),
            pltpu.VMEM((16, 1, 256), F32),
            pltpu.VMEM((2, 4, 2) + block, F32),
            pltpu.VMEM((2, 2, 4) + block, BF),
            pltpu.VMEM((2, 2, 4) + block, BF),
            pltpu.VMEM((2, 2, PROWS, 128), BF),
            pltpu.VMEM((2, 2) + block, BF),
            pltpu.VMEM((2, 2) + block, BF),
            pltpu.VMEM((2, 2, 2) + block, BF),
            pltpu.VMEM((2, 2, 2) + block, BF),
            pltpu.SMEM((16,), jnp.int32),
            pltpu.SMEM((16,), jnp.int32),
            pltpu.SMEM((16,), jnp.int32),
            pltpu.SMEM((32,), jnp.int32),
            pltpu.SemaphoreType.DMA((COPIES,)),
            pltpu.SemaphoreType.DMA((COPIES,)),
            pltpu.SemaphoreType.DMA((16,)),
        ],
        compiler_params=pltpu.CompilerParams(
            collective_id=0, has_side_effects=True, vmem_limit_bytes=60 * 1024 * 1024
        ),
        cost_estimate=pl.CostEstimate(
            flops=10_000_000_000, bytes_accessed=8 * 1024 * 1024, transcendentals=17_000_000
        ),
    )(*arguments)
    return pl.pallas_call(
        copy_out,
        out_shape=tuple(jax.ShapeDtypeStruct(r.shape, r.dtype) for r in results),
        in_specs=[pl.BlockSpec(memory_space=pl.ANY)] * 3,
        out_specs=(hbm,) * 3,
        scratch_shapes=[pltpu.VMEM(r.shape, r.dtype) for r in results]
        + [pltpu.SemaphoreType.DMA((PIECES + 2,))] * 2,
        compiler_params=pltpu.CompilerParams(vmem_limit_bytes=60 * 1024 * 1024),
    )(*results)


def solution(mesh):
    split = P("dp", "blk", None)
    return jax.shard_map(
        on_device,
        mesh=mesh,
        in_specs=(split,) * 6 + (P(),) * 4,
        out_specs=(split, split, split),
        check_vma=False,
    )
```

time: 101 us -> 111 us (1.099)
  Pallas kernels: 100 us -> 111 us
    pallas_call x1, Pallas kernels: 98 us -> 108 us  [on_device(): pl.pallas_call(kernel, out_shape=(jax.ShapeDtypeStruct((1, ROWS, 4096), B...]
where the time goes in v5:
time: 111 us
  Pallas kernels  111 us (100%)
    pallas_call x1, Pallas kernels, on_device(): pl.pallas_call(kernel, out_shape=(jax.ShapeDtypeStruct((1, ROWS, 4096), B...  108 us

profile of v5, /device:TPU:1, one launch (start us, length us, event | category | flops | bytes accessed | tf_op | source)
XLA Modules:
  0.0 111.2 jit_solution(11734981040736780768)
XLA Ops:
  0.6 108.4 %shard_map.121 = (bf16[1,128,4096]{2,1,0:T(8,128)(2,1)}, f32[1,64,512]{2,1,0:T(8,128)}, f32[1,64,512]{2,1,0:T(8,128)}) custom-call(bf16[1,128,4096]{2,1,0:T(8,128)(2,1)} %q_ref.1, bf16[1,128,512]{2,1,0:T(8,128)(2,1)} %rk_ref.1, bf16[1,128,512]{2,1,0:T(8,128)(2,1)} %rv_ref.1, bf16[1,64,512]{2,1,0:T(8,128)(2,1)} %pk_ref.1, bf16[1,64,512]{2,1,0:T(8,128)(2,1)} %pv_ref.1, ...), custom_call_target="tpu_custom_call" | custom-call | flops 10000000000 | bytes 8388608 | tf_op jit(solution)/shard_map/pallas_call | solution.py:602
  109.1 2.1 %shard_map.122 = (bf16[1,128,4096]{2,1,0:T(8,128)(2,1)}, f32[1,64,512]{2,1,0:T(8,128)}, f32[1,64,512]{2,1,0:T(8,128)}) custom-call(bf16[1,128,4096]{2,1,0:T(8,128)(2,1)} %get-tuple-element.6.refs_0_, f32[1,64,512]{2,1,0:T(8,128)} %get-tuple-element.7.refs_1_, f32[1,64,512]{2,1,0:T(8,128)} %get-tuple-element.8.refs_2_), custom_call_target="tpu_custom_call" | custom-call | tf_op jit(solution)/shard_map/pallas_call | solution.py:653

commit v6 on v5

--- a/solution.py
+++ b/solution.py
@@ -35,14 +35,10 @@
     return lax.dot_general(a, b, (((0,), (0,)), ((), ())), preferred_element_type=F32)
 
 
-def kernel(
-    q_ref, rk_ref, rv_ref, pk_ref, pv_ref, do_ref, owner_hbm, prompt_hbm, length_hbm, half_hbm,
-    out_ref, gk_ref, gv_ref,
-    q_near, q_far, do_near, do_far, out_near, out_far,
-    resp_keys, resp_values, values_in, xbuf, chosen_out, chosen_in, prompt, limit_ref,
-    m_ref, acc_ref, lse_ref, delta_ref, gacc,
-    zs_out, zs_in, share_out, share, core_in, xs_out, xs_in,
-    owner_ref, prompt_ref, length_ref, half_ref,
+def gather_kernel(
+    q_ref, rk_ref, rv_ref, pk_ref, pv_ref, do_ref, owner_hbm, prompt_hbm,
+    q_far, do_far, resp_keys, resp_values, prompt,
+    values_in, xbuf, chosen_out, chosen_in, owner_ref, prompt_ref,
     send_sem, recv_sem, local_sem,
 ):
     dp = lax.axis_index("dp")
@@ -89,12 +85,7 @@
         fetch(rk_ref.at[0, :, mine_kv], resp_keys.at[z, yl]),
         fetch(rv_ref.at[0, :, mine_kv], values_in.at[yl]),
     ]
-    tables = [
-        fetch(owner_hbm, owner_ref), fetch(prompt_hbm, prompt_ref),
-        fetch(length_hbm, length_ref), fetch(half_hbm, half_ref),
-    ]
-    own_q = fetch(q_ref.at[0, :, mine_q], q_near)
-    own_do = fetch(do_ref.at[0, :, mine_q], do_near)
+    tables = [fetch(owner_hbm, owner_ref), fetch(prompt_hbm, prompt_ref)]
 
     barrier = pltpu.get_barrier_semaphore()
     peers = (y_id, z_right, z_left, x_right, x_left, core_id, yh_id, diagonal_id)
@@ -136,8 +127,7 @@
         return copies
 
     x_base, core_base, ys_base, yq_base, yd_base = room(8), room(5), room(2), room(2), room(2)
-    ring_base, r_base, p_base, result_base = room(3), room(16), room(32), room(2)
-    zs_base, yr_base, cs_base, xs_base = room(32), room(6), room(2), room(16)
+    ring_base, r_base, p_base = room(3), room(16), room(32)
 
     def x_copies(step):
         if step == 0:
@@ -191,36 +181,90 @@
             z, Z, step, z_right, z_left, (0, 1),
         )
 
-    def result_copies(a):
-        columns = pl.ds(pl.multiple_of(a * 1024, 1024), 1024)
-        return [copy(result_base + a, out_far.at[:, columns], out_ref.at[0, :, group_lanes(yl, a)], y_id)]
-
-    def sums(base, outgoing, incoming, a, step, right, left):
-        return [
-            copy(
-                base + step * 4 + way * 2 + h,
-                outgoing.at[a, way, step, h], incoming.at[a, way, step, h], peer,
-            )
-            for way, peer in enumerate((right, left))
-            for h in range(2)
-            if step > 0 or h == way
-        ]
-
-    def zs_copies(a, step):
-        return sums(zs_base + a * 16, zs_out, zs_in, a, step, z_right, z_left)
-
-    def xs_copies(a, step):
-        return sums(xs_base + a * 8, xs_out, xs_in, a, step, x_right, x_left)
-
-    def yr_copies(a):
-        return [
-            copy(yr_base + a * 3, share_out.at[a], share.at[a, 0, 1], y_id),
-            copy(yr_base + a * 3 + 1, share.at[a, 0, 0], share.at[a, 1, 0], yh_id),
-            copy(yr_base + a * 3 + 2, share_out.at[a], share.at[a, 1, 1], diagonal_id),
-        ]
-
-    def cs_copies(a):
-        return [copy(cs_base + a, share.at[a], core_in.at[a], core_id)]
+    start(x_copies(0))
+    start(y_resp)
+    start(core_copies(0))
+    start(y_q)
+    present(tables)
+    arrive(x_copies(0))
+    start(x_copies(1))
+    start(core_copies(1))
+    present(own_resp)
+    arrive(y_resp[:1])
+    start(r_copies(0, 0))
+    arrive(y_resp[1:])
+    for a in range(2):
+        for y in range(2):
+            resp_values[z, a, :, y * ROWS : (y + 1) * ROWS] = values_in[
+                y, :, a * 128 : (a + 1) * 128
+            ].T
+    start(r_copies(0, 1))
+    arrive(x_copies(1))
+    start(core_copies(2))
+    present(own_prompt)
+    for which in range(3):
+        arrive(core_copies(which))
+    theirs = owner_ref[prompt_ref[x * 4 + (1 - yh) * 2 + c]]
+    mine = owner_ref[prompt_ref[dp]]
+
+    def piece(owner, half, a):
+        return xbuf[owner // 4, owner % 2, :, :, head_lanes(half, a)]
+
+    for n, (owner, half) in enumerate(((mine, other), (theirs, yl), (theirs, other))):
+        for a in range(2):
+            chosen_out[n, a] = piece(owner, half, a)
+        start(ring[n : n + 1])
+    start(y_do)
+
+    def pass_resp(step):
+        for h in range(2):
+            arrive(r_copies(step - 1, h))
+            start(r_copies(step, h))
+
+    pass_resp(1)
+    arrive(ring)
+    here = (mine // 2) % 2 == yh
+    for a in range(2):
+        for kv in range(2):
+            prompt[a, z, kv, yl] = jnp.where(here, piece(mine, yl, a)[kv], chosen_in[1, a, kv])
+            prompt[a, z, kv, other] = jnp.where(here, chosen_in[0, a, kv], chosen_in[2, a, kv])
+        start(p_copies(a, 0))
+    for step in range(1, 4):
+        for a in range(2):
+            arrive(p_copies(a, step - 1))
+            start(p_copies(a, step))
+        if step < 3:
+            pass_resp(step + 1)
+    every = [x_copies(0), x_copies(1), core_copies(0), core_copies(1), core_copies(2)]
+    every += [y_resp, y_q, y_do, ring]
+    for step in range(4):
+        every += [r_copies(step, h) for h in range(2)] + [p_copies(a, step) for a in range(2)]
+    for copies in every:
+        drain(copies)
+    arrive(y_q + y_do)
+    for h in range(2):
+        arrive(r_copies(3, h))
+        arrive(p_copies(h, 3))
+
+
+def compute_kernel(
+    q_ref, do_ref, q_far, do_far, resp_keys, resp_values, prompt, length_ref, half_ref,
+    out_near, out_far, gacc,
+    q_near, do_near, limit_ref, m_ref, acc_ref, lse_ref, delta_ref, local_sem,
+):
+    dp = lax.axis_index("dp")
+    blk = lax.axis_index("blk")
+    yl, z = blk // Z, blk % Z
+    other = 1 - yl
+    mine_q = pl.ds(pl.multiple_of(yl * HALF_Q, HALF_Q), HALF_Q)
+    loads = [
+        pltpu.make_async_copy(q_ref.at[0, :, mine_q], q_near, local_sem.at[0]),
+        pltpu.make_async_copy(do_ref.at[0, :, mine_q], do_near, local_sem.at[1]),
+    ]
+    for load in loads:
+        load.start()
+    for load in loads:
+        load.wait()
 
     def head_of(near, far, h):
         columns = pl.ds(pl.multiple_of(h * 128, 128), 128)
@@ -233,12 +277,6 @@
 
         lax.fori_loop(0, count, step, 0)
 
-    start(x_copies(0))
-    start(y_resp)
-    start(core_copies(0))
-    start(y_q)
-
-    present(tables)
     lane = lax.broadcasted_iota(jnp.int32, (1, 2 * ROWS), 1)
     last = length_ref[dp] - 1
     limit = jnp.zeros((1, 2 * ROWS), jnp.int32)
@@ -353,6 +391,131 @@
             gacc[a, k, n, 0] = key_part[n * 128 : n * 128 + 128].reshape(2, PROWS, 128)
             gacc[a, k, n, 1] = value_part[n * 128 : n * 128 + 128].reshape(2, PROWS, 128)
 
+    def resp_unit(u):
+        s = u // 2
+        absorb_resp(u % 2, [(z + Z - s) % Z, (z + s + 1) % Z])
+
+    def prompt_unit(u):
+        absorb_prompt(u % 2, [(u // 2) * 4 + n for n in range(4)])
+
+    def gradient_unit(u):
+        a, k = u % 2, u // 2
+        gradients(a, k, [(z + 4 + k) % Z, (z + 3 + Z - k) % Z])
+
+    loop(8, resp_unit)
+    loop(4, prompt_unit)
+    loop(2, finish)
+    loop(8, gradient_unit)
+
+
+def reduce_kernel(
+    out_near, out_far, gacc, owner_hbm, prompt_hbm,
+    out_ref, gk_ref, gv_ref,
+    zs_out, zs_in, share_out, share, core_in, xs_out, xs_in, owner_ref, prompt_ref,
+    send_sem, recv_sem, local_sem,
+):
+    dp = lax.axis_index("dp")
+    blk = lax.axis_index("blk")
+    x, yh, c = dp // 4, (dp // 2) % 2, dp % 2
+    yl, z = blk // Z, blk % Z
+    other = 1 - yl
+    y_id = (dp, other * Z + z)
+    z_right, z_left = (dp, yl * Z + (z + 1) % Z), (dp, yl * Z + (z + Z - 1) % Z)
+    x_right = (((x + 1) % X) * 4 + yh * 2 + c, blk)
+    x_left = (((x + X - 1) % X) * 4 + yh * 2 + c, blk)
+    core_id = (x * 4 + yh * 2 + (1 - c), blk)
+    yh_id = (x * 4 + (1 - yh) * 2 + c, blk)
+    diagonal_id = (x * 4 + (1 - yh) * 2 + c, other * Z + z)
+
+    def lanes(which, width):
+        return pl.ds(pl.multiple_of(which * width, width), width)
+
+    def head_lanes(half, a):
+        return pl.ds(pl.multiple_of(half * HALF_KV + a * 128, 128), 128)
+
+    def group_lanes(half, a):
+        return pl.ds(pl.multiple_of(half * HALF_Q + a * 1024, 1024), 1024)
+
+    mine_kv, far_kv = lanes(yl, HALF_KV), lanes(other, HALF_KV)
+    mine_q = lanes(yl, HALF_Q)
+
+    fetched = []
+
+    def fetch(src, dst):
+        copy = pltpu.make_async_copy(src, dst, local_sem.at[len(fetched)])
+        copy.start()
+        fetched.append(copy)
+        return copy
+
+    def present(copies):
+        for copy in copies:
+            copy.wait()
+
+    tables = [fetch(owner_hbm, owner_ref), fetch(prompt_hbm, prompt_ref)]
+    own_result = fetch(out_near, out_ref.at[0, :, mine_q])
+    barrier = pltpu.get_barrier_semaphore()
+    peers = (y_id, z_right, z_left, x_right, x_left, core_id, yh_id, diagonal_id)
+    for peer in peers:
+        pl.semaphore_signal(barrier, inc=1, device_id=peer, device_id_type=MESH)
+    pl.semaphore_wait(barrier, len(peers))
+
+    total = [0]
+
+    def room(n):
+        total[0] += n
+        return total[0] - n
+
+    def copy(index, src, dst, peer):
+        return pltpu.make_async_remote_copy(
+            src_ref=src, dst_ref=dst, send_sem=send_sem.at[index], recv_sem=recv_sem.at[index],
+            device_id=peer, device_id_type=MESH,
+        )
+
+    def start(copies):
+        for one in copies:
+            one.start()
+
+    def arrive(copies):
+        for one in copies:
+            one.wait_recv()
+
+    def drain(copies):
+        for one in copies:
+            one.wait_send()
+
+    result_base, zs_base, yr_base, cs_base, xs_base = room(2), room(32), room(6), room(2), room(16)
+
+    def result_copies(a):
+        columns = pl.ds(pl.multiple_of(a * 1024, 1024), 1024)
+        return [copy(result_base + a, out_far.at[:, columns], out_ref.at[0, :, group_lanes(yl, a)], y_id)]
+
+    def sums(base, outgoing, incoming, a, step, right, left):
+        return [
+            copy(
+                base + step * 4 + way * 2 + h,
+                outgoing.at[a, way, step, h], incoming.at[a, way, step, h], peer,
+            )
+            for way, peer in enumerate((right, left))
+            for h in range(2)
+            if step > 0 or h == way
+        ]
+
+    def zs_copies(a, step):
+        return sums(zs_base + a * 16, zs_out, zs_in, a, step, z_right, z_left)
+
+    def xs_copies(a, step):
+        return sums(xs_base + a * 8, xs_out, xs_in, a, step, x_right, x_left)
+
+    def yr_copies(a):
+        return [
+            copy(yr_base + a * 3, share_out.at[a], share.at[a, 0, 1], y_id),
+            copy(yr_base + a * 3 + 1, share.at[a, 0, 0], share.at[a, 1, 0], yh_id),
+            copy(yr_base + a * 3 + 2, share_out.at[a], share.at[a, 1, 1], diagonal_id),
+        ]
+
+    def cs_copies(a):
+        return [copy(cs_base + a, share.at[a], core_in.at[a], core_id)]
+
     def z_messages(a, step):
         for way in range(2):
             for h in range(2):
@@ -404,171 +567,38 @@
             ref[0, :, head_lanes(yl, a)] = part[0]
             ref[0, :, head_lanes(other, a)] = part[1]
 
-    arrive(x_copies(0))
-    start(x_copies(1))
-    start(core_copies(1))
-    present(own_resp)
-    arrive(y_resp[:1])
-    start(r_copies(0, 0))
-    arrive(y_resp[1:])
     for a in range(2):
-        for y in range(2):
-            resp_values[z, a, :, y * ROWS : (y + 1) * ROWS] = values_in[
-                y, :, a * 128 : (a + 1) * 128
-            ].T
-    start(r_copies(0, 1))
-    arrive(x_copies(1))
-    start(core_copies(2))
-    present(own_prompt + [own_q, own_do])
-    for which in range(3):
-        arrive(core_copies(which))
-    theirs = owner_ref[prompt_ref[x * 4 + (1 - yh) * 2 + c]]
-    mine = owner_ref[prompt_ref[dp]]
-
-    def piece(owner, half, a):
-        return xbuf[owner // 4, owner % 2, :, :, head_lanes(half, a)]
-
-    for n, (owner, half) in enumerate(((mine, other), (theirs, yl), (theirs, other))):
+        z_messages(a, 0)
+        start(result_copies(a))
+    present(tables)
+    for step in range(1, 4):
         for a in range(2):
-            chosen_out[n, a] = piece(owner, half, a)
-        start(ring[n : n + 1])
-
-    def pass_on(step):
+            arrive(zs_copies(a, step - 1))
+            z_messages(a, step)
+    for a in range(2):
+        arrive(zs_copies(a, 3))
+        to_y_ring(a)
+    for a in range(2):
+        arrive(yr_copies(a))
+        start(cs_copies(a))
+    for a in range(2):
+        arrive(cs_copies(a))
+        x_messages(a, 0)
+    for a in range(2):
+        arrive(xs_copies(a, 0))
+        x_messages(a, 1)
+    for step in range(4):
         for a in range(2):
-            arrive(p_copies(a, step - 1))
-            start(p_copies(a, step))
-
-    def resp_unit(u):
-        a, s = u % 2, u // 2
-
-        @pl.when(u == 0)
-        def _():
-            arrive(y_q[:1])
-
-        @pl.when(u == 1)
-        def _():
-            arrive(y_q[1:])
-            arrive(ring)
-            here = (mine // 2) % 2 == yh
-            for a in range(2):
-                for kv in range(2):
-                    prompt[a, z, kv, yl] = jnp.where(
-                        here, piece(mine, yl, a)[kv], chosen_in[1, a, kv]
-                    )
-                    prompt[a, z, kv, other] = jnp.where(
-                        here, chosen_in[0, a, kv], chosen_in[2, a, kv]
-                    )
-                start(p_copies(a, 0))
-            start(y_do)
-
-        for step in range(1, 5):
-
-            @pl.when(u == 2 * step - 2)
-            def _():
-                for h in range(2):
-                    arrive(r_copies(step - 1, h))
-                    if step < 4:
-                        start(r_copies(step, h))
-
-            if step < 4:
-
-                @pl.when(u == 2 * step + 1)
-                def _():
-                    pass_on(step)
-
-        absorb_resp(a, [(z + Z - s) % Z, (z + s + 1) % Z])
-
-    loop(8, resp_unit)
-    arrive(y_do)
-
-    def key_head(a):
-        def prompt_unit(w):
-            @pl.when(w == 1)
-            def _():
-                arrive(p_copies(a, 3))
-
-            sign = 1 - 2 * w
-            absorb_prompt(
-                a,
-                [(z + 4 * w) % Z, (z + Z + 4 * w + sign) % Z, (z + Z - 4 * w - sign) % Z, (z + 2 + 4 * w) % Z],
-            )
-
-        loop(2, prompt_unit)
-
-        @pl.when(a == 1)
-        def _():
-            arrive(zs_copies(0, 3))
-            to_y_ring(0)
-
-        finish(a)
-        start(result_copies(a))
-
-        @pl.when(a == 1)
-        def _():
-            arrive(yr_copies(0))
-            start(cs_copies(0))
-
-        def gradient_unit(k):
-            gradients(a, k, [(z + 4 + k) % Z, (z + 3 + Z - k) % Z])
-            for step in range(4):
-
-                @pl.when(k == step)
-                def _():
-                    if step > 0:
-                        arrive(zs_copies(a, step - 1))
-                    z_messages(a, step)
-
-            for step in range(3):
-
-                @pl.when((a == 1) & (k == step))
-                def _():
-                    if step == 0:
-                        arrive(cs_copies(0))
-                        x_messages(0, 0)
-                    elif step == 1:
-                        arrive(xs_copies(0, 0))
-                        x_messages(0, 1)
-                    else:
-                        arrive(xs_copies(0, 1))
-                        store(0)
-
-        loop(4, gradient_unit)
-
-    loop(2, key_head)
-    own_result = fetch(out_near, out_ref.at[0, :, mine_q])
-
-    early = [x_copies(0), x_copies(1), core_copies(0), core_copies(1), core_copies(2)]
-    early += [y_resp, y_q, y_do, ring, zs_copies(0, 3), yr_copies(0), cs_copies(0)]
-    for step in range(4):
-        early += [r_copies(step, h) for h in range(2)] + [p_copies(a, step) for a in range(2)]
-    for step in range(3):
-        early += [zs_copies(a, step) for a in range(2)]
-    early += [xs_copies(0, 0), xs_copies(0, 1)]
-    for copies in early[: len(early) // 2]:
-        drain(copies)
-    arrive(zs_copies(1, 3))
-    to_y_ring(1)
-    for copies in early[len(early) // 2 :]:
-        drain(copies)
-    arrive(yr_copies(1))
-    start(cs_copies(1))
-    drain(zs_copies(1, 3))
+            drain(zs_copies(a, step))
     for a in range(2):
+        drain(result_copies(a) + yr_copies(a) + cs_copies(a) + xs_copies(a, 0))
         arrive(result_copies(a))
-        drain(result_copies(a))
+        arrive(xs_copies(a, 1))
+        store(a)
+        drain(xs_copies(a, 1))
     present([own_result])
-    arrive(cs_copies(1))
-    x_messages(1, 0)
-    drain(yr_copies(1) + cs_copies(1))
-    arrive(xs_copies(1, 0))
-    x_messages(1, 1)
-    drain(xs_copies(1, 0))
-    arrive(xs_copies(1, 1))
-    store(1)
-    drain(xs_copies(1, 1))
-
-
-COPIES = 128
+
+
 UNROLL = 4
 PIECES = 4
 
@@ -595,39 +625,73 @@
         copy.wait()
 
 
-def on_device(*arguments):
+def on_device(q, rk, rv, pk, pv, do, owner, prompt_index, length, half):
     block = (2, 2, PROWS, 128)
+    hbm = pl.BlockSpec(memory_space=pltpu.HBM)
     vmem = pl.BlockSpec(memory_space=pltpu.VMEM)
-    hbm = pl.BlockSpec(memory_space=pltpu.HBM)
+    smem = pl.BlockSpec(memory_space=pltpu.SMEM)
+
+    def parameters(number=None):
+        extra = {} if number is None else dict(collective_id=number, has_side_effects=True)
+        return pltpu.CompilerParams(vmem_limit_bytes=60 * 1024 * 1024, **extra)
+
+    def sems(*counts):
+        return [pltpu.SemaphoreType.DMA((n,)) for n in counts]
+
+    tables = [pltpu.SMEM((16,), jnp.int32)] * 2
+    half_shape = jax.ShapeDtypeStruct((ROWS, HALF_Q), BF)
+    q_far, do_far, keys, values, prompt = pl.pallas_call(
+        gather_kernel,
+        out_shape=(
+            half_shape,
+            half_shape,
+            jax.ShapeDtypeStruct((Z, 2, ROWS, HALF_KV), BF),
+            jax.ShapeDtypeStruct((Z, 2, 128, 2 * ROWS), BF),
+            jax.ShapeDtypeStruct((2, Z) + block, BF),
+        ),
+        in_specs=[hbm] * 8,
+        out_specs=(vmem,) * 5,
+        scratch_shapes=[
+            pltpu.VMEM((2, ROWS, HALF_KV), BF),
+            pltpu.VMEM((X, 2, 2, PROWS, 512), BF),
+            pltpu.VMEM((3, 2, 2, PROWS, 128), BF),
+            pltpu.VMEM((3, 2, 2, PROWS, 128), BF),
+        ]
+        + tables
+        + sems(80, 80, 16),
+        compiler_params=parameters(0),
+    )(q, rk, rv, pk, pv, do, owner, prompt_index)
+    out_near, out_far, partial = pl.pallas_call(
+        compute_kernel,
+        out_shape=(
+            half_shape,
+            half_shape,
+            jax.ShapeDtypeStruct((2, 4, 2) + block, F32),
+        ),
+        in_specs=[hbm] * 2 + [vmem] * 5 + [smem] * 2,
+        out_specs=(vmem,) * 3,
+        scratch_shapes=[
+            pltpu.VMEM((ROWS, HALF_Q), BF),
+            pltpu.VMEM((ROWS, HALF_Q), BF),
+            pltpu.VMEM((1, 2 * ROWS), jnp.int32),
+            pltpu.VMEM((16, 1, 256), F32),
+            pltpu.VMEM((16, 144, 256), F32),
+            pltpu.VMEM((16, 1, 256), F32),
+            pltpu.VMEM((16, 1, 256), F32),
+        ]
+        + sems(2),
+        compiler_params=parameters(),
+    )(q, do, q_far, do_far, keys, values, prompt, length, half)
     results = pl.pallas_call(
-        kernel,
+        reduce_kernel,
         out_shape=(
             jax.ShapeDtypeStruct((1, ROWS, 4096), BF),
             jax.ShapeDtypeStruct((1, PROWS, 512), F32),
             jax.ShapeDtypeStruct((1, PROWS, 512), F32),
         ),
-        in_specs=[hbm] * 10,
+        in_specs=[vmem] * 3 + [hbm] * 2,
         out_specs=(hbm, vmem, vmem),
         scratch_shapes=[
-            pltpu.VMEM((ROWS, HALF_Q), BF),
-            pltpu.VMEM((ROWS, HALF_Q), BF),
-            pltpu.VMEM((ROWS, HALF_Q), BF),
-            pltpu.VMEM((ROWS, HALF_Q), BF),
-            pltpu.VMEM((ROWS, HALF_Q), BF),
-            pltpu.VMEM((ROWS, HALF_Q), BF),
-            pltpu.VMEM((Z, 2, ROWS, HALF_KV), BF),
-            pltpu.VMEM((Z, 2, 128, 2 * ROWS), BF),
-            pltpu.VMEM((2, ROWS, HALF_KV), BF),
-            pltpu.VMEM((X, 2, 2, PROWS, 512), BF),
-            pltpu.VMEM((3, 2, 2, PROWS, 128), BF),
-            pltpu.VMEM((3, 2, 2, PROWS, 128), BF),
-            pltpu.VMEM((2, Z) + block, BF),
-            pltpu.VMEM((1, 2 * ROWS), jnp.int32),
-            pltpu.VMEM((16, 1, 256), F32),
-            pltpu.VMEM((16, 144, 256), F32),
-            pltpu.VMEM((16, 1, 256), F32),
-            pltpu.VMEM((16, 1, 256), F32),
-            pltpu.VMEM((2, 4, 2) + block, F32),
             pltpu.VMEM((2, 2, 4) + block, BF),
             pltpu.VMEM((2, 2, 4) + block, BF),
             pltpu.VMEM((2, 2, PROWS, 128), BF),
@@ -635,21 +699,11 @@
             pltpu.VMEM((2, 2) + block, BF),
             pltpu.VMEM((2, 2, 2) + block, BF),
             pltpu.VMEM((2, 2, 2) + block, BF),
-            pltpu.SMEM((16,), jnp.int32),
-            pltpu.SMEM((16,), jnp.int32),
-            pltpu.SMEM((16,), jnp.int32),
-            pltpu.SMEM((32,), jnp.int32),
-            pltpu.SemaphoreType.DMA((COPIES,)),
-            pltpu.SemaphoreType.DMA((COPIES,)),
-            pltpu.SemaphoreType.DMA((16,)),
-        ],
-        compiler_params=pltpu.CompilerParams(
-            collective_id=0, has_side_effects=True, vmem_limit_bytes=60 * 1024 * 1024
-        ),
-        cost_estimate=pl.CostEstimate(
-            flops=10_000_000_000, bytes_accessed=8 * 1024 * 1024, transcendentals=17_000_000
-        ),
-    )(*arguments)
+        ]
+        + tables
+        + sems(64, 64, 4),
+        compiler_params=parameters(1),
+    )(out_near, out_far, partial, owner, prompt_index)
     return pl.pallas_call(
         copy_out,
         out_shape=tuple(jax.ShapeDtypeStruct(r.shape, r.dtype) for r in results),

time: 111 us -> 135 us (1.22)
  Pallas kernels: 111 us -> 135 us
    pallas_call x1 -> x3, Pallas kernels: 108 us -> 132 us  [the longest x1 50.2 us: on_device(): pl.pallas_call(gather_kernel, out_shape=(half_shape, half_shape, jax.Shap...]
where the time goes in v6:
time: 135 us
  Pallas kernels  135 us (100%)
    pallas_call x1, Pallas kernels, on_device(): pl.pallas_call(gather_kernel, out_shape=(half_shape, half_shape, jax.Shap...  50.2 us
    pallas_call x1, Pallas kernels, on_device(): pl.pallas_call(compute_kernel, out_shape=(half_shape, half_shape, jax.Sha...  42.6 us
    pallas_call x1, Pallas kernels, on_device(): pl.pallas_call(reduce_kernel, out_shape=(jax.ShapeDtypeStruct((1, ROWS, 4...  39.7 us

profile of v6, /device:TPU:1, one launch (start us, length us, event | category | flops | bytes accessed | tf_op | source)
XLA Modules:
  0.0 135.2 jit_solution(9791895690917809530)
XLA Ops:
  0.6 50.2 %shard_map.121 = (bf16[128,2048]{1,0:T(8,128)(2,1)}, bf16[128,2048]{1,0:T(8,128)(2,1)}, bf16[8,2,128,256]{3,2,1,0:T(8,128)(2,1)}, bf16[8,2,128,256]{3,2,1,0:T(8,128)(2,1)}, bf16[2,8,2,2,64,128]{5,4,3,2,1,0:T(8,128)(2,1)}) custom-call(bf16[1,128,4096]{2,1,0:T(8,128)(2,1)} %q_ref.3, bf16[1,128,512]{2,1,0:T(8,128)(2,1)} %rk_ref.1, bf16[1,128,512]{2,1,0:T(8,128)(2,1)} %rv_ref.1, ...), custom_call_target="tpu_custom_call" | custom-call | tf_op jit(solution)/shard_map/pallas_call | solution.py:643
  50.8 42.6 %shard_map.122 = (bf16[128,2048]{1,0:T(8,128)(2,1)}, bf16[128,2048]{1,0:T(8,128)(2,1)}, f32[2,4,2,2,2,64,128]{6,5,4,3,2,1,0:T(8,128)}) custom-call(bf16[1,128,4096]{2,1,0:T(8,128)(2,1)} %q_ref.3, bf16[1,128,4096]{2,1,0:T(8,128)(2,1)} %do_ref.3, bf16[128,2048]{1,0:T(8,128)(2,1)} %get-tuple-element.14.q_far, bf16[128,2048]{1,0:T(8,128)(2,1)} %get-tuple-element.15.do_far, ...), custom_call_target="tpu_custom_call" | custom-call | tf_op jit(solution)/shard_map/pallas_call | solution.py:664
  93.4 39.7 %shard_map.123 = (bf16[1,128,4096]{2,1,0:T(8,128)(2,1)}, f32[1,64,512]{2,1,0:T(8,128)}, f32[1,64,512]{2,1,0:T(8,128)}) custom-call(bf16[128,2048]{1,0:T(8,128)(2,1)} %get-tuple-element.19.out_near, bf16[128,2048]{1,0:T(8,128)(2,1)} %get-tuple-element.20.out_far, f32[2,4,2,2,2,64,128]{6,5,4,3,2,1,0:T(8,128)} %get-tuple-element.21.gacc, s32[16]{0:T(128)} %owner_hbm.3, ...), custom_call_target="tpu_custom_call" | custom-call | tf_op jit(solution)/shard_map/pallas_call | solution.py:685
  133.2 2.1 %shard_map.124 = (bf16[1,128,4096]{2,1,0:T(8,128)(2,1)}, f32[1,64,512]{2,1,0:T(8,128)}, f32[1,64,512]{2,1,0:T(8,128)}) custom-call(bf16[1,128,4096]{2,1,0:T(8,128)(2,1)} %get-tuple-element.22.refs_0_, f32[1,64,512]{2,1,0:T(8,128)} %get-tuple-element.23.refs_1_, f32[1,64,512]{2,1,0:T(8,128)} %get-tuple-element.24.refs_2_), custom_call_target="tpu_custom_call" | custom-call | tf_op jit(solution)/shard_map/pallas_call | solution.py:707

commit v7 on v4

--- a/solution.py
+++ b/solution.py
@@ -39,7 +39,7 @@
     q_ref, rk_ref, rv_ref, pk_ref, pv_ref, do_ref, owner_hbm, prompt_hbm, length_hbm, half_hbm,
     out_ref, gk_ref, gv_ref,
     q_near, q_far, do_near, do_far, out_near, out_far,
-    resp_keys, resp_values, values_in, xbuf, chosen_out, chosen_in, prompt, v_turned,
+    resp, far_block, values_in, xbuf, chosen_out, chosen_in, prompt, v_turned,
     m_ref, acc_ref, lse_ref, delta_ref, gacc,
     zs_out, zs_in, share_out, share, core_in, xs_out, xs_in,
     owner_ref, prompt_ref, length_ref, half_ref,
@@ -56,6 +56,7 @@
     x_left = (((x + X - 1) % X) * 4 + yh * 2 + c, blk)
     core_id = (x * 4 + yh * 2 + (1 - c), blk)
     yh_id = (x * 4 + (1 - yh) * 2 + c, blk)
+    far_x_id = (((x + 2) % X) * 4 + yh * 2 + c, blk)
     diagonal_id = (x * 4 + (1 - yh) * 2 + c, other * Z + z)
 
     def lanes(which, width):
@@ -85,9 +86,11 @@
     own_prompt = [
         fetch(ref.at[0], xbuf.at[x, c, kv]) for kv, ref in enumerate((pk_ref, pv_ref))
     ]
-    own_resp = [
-        fetch(rk_ref.at[0, :, mine_kv], resp_keys.at[z, yl]),
-        fetch(rv_ref.at[0, :, mine_kv], values_in.at[yl]),
+    own_resp = [fetch(rv_ref.at[0], values_in)]
+    own_resp += [
+        fetch(rk_ref.at[0, :, head_lanes(half, a)], to.at[0, a])
+        for half, to in ((yl, resp.at[z, yl]), (other, far_block))
+        for a in range(2)
     ]
     tables = [
         fetch(owner_hbm, owner_ref), fetch(prompt_hbm, prompt_ref),
@@ -97,7 +100,7 @@
     own_do = fetch(do_ref.at[0, :, mine_q], do_near)
 
     barrier = pltpu.get_barrier_semaphore()
-    peers = (y_id, z_right, z_left, x_right, x_left, core_id, yh_id, diagonal_id)
+    peers = (y_id, z_right, z_left, x_right, x_left, core_id, yh_id, diagonal_id, far_x_id)
     for peer in peers:
         pl.semaphore_signal(barrier, inc=1, device_id=peer, device_id_type=MESH)
     pl.semaphore_wait(barrier, len(peers))
@@ -123,33 +126,30 @@
         for peer in (x_right, x_left)
         for kv, ref in enumerate((pk_ref, pv_ref))
     ]
-    y_resp = [
-        send(rk_ref.at[0, :, far_kv], resp_keys.at[z, yl], y_id),
-        send(rv_ref.at[0, :, far_kv], values_in.at[yl], y_id),
-    ]
+    y_q = [None, None]
+
+    def send_queries(a):
+        near, far = q_ref.at[0, :, group_lanes(other, a)], q_far.at[:, a * 1024 : a * 1024 + 1024]
+        y_q[a] = send(near, far, y_id)
+
+    send_queries(0)
     cores = [
         send(ref.at[0], xbuf.at[x, c, kv], core_id) for kv, ref in enumerate((pk_ref, pv_ref))
     ]
-    y_q = [
-        send(q_ref.at[0, :, group_lanes(other, a)], q_far.at[:, a * 1024 : a * 1024 + 1024], y_id)
-        for a in range(2)
-    ]
-
-    def gather_step(slot, pos, n, step, right, left, halves=(0, 1)):
-        final = step == n // 2 - 1
+
+    def gather_step(slot, pos, n, step, right, left):
         copies = []
-        for h in halves:
-            for way, peer in enumerate((right, left)):
-                if not final or h == way:
-                    at = slot((pos + n - step) % n if way == 0 else (pos + step) % n, h)
-                    copies.append(send(at, at, peer))
+        for way, peer in enumerate((right, left)):
+            at = slot((pos + n - step) % n if way == 0 else (pos + step) % n)
+            at = at.at[way] if step == n // 2 - 1 else at
+            copies.append(send(at, at, peer))
         return copies
 
-    def resp_gather(step, h):
-        return gather_step(lambda i, h: (resp_values if h else resp_keys).at[i], z, Z, step, z_right, z_left, (h,))
+    def resp_gather(y, step):
+        return gather_step(lambda i: resp.at[i, y], z, Z, step, z_right, z_left)
 
     def prompt_gather(a, step):
-        return gather_step(lambda i, h: prompt.at[a, i, h], z, Z, step, z_right, z_left)
+        return gather_step(lambda i: prompt.at[a, i], z, Z, step, z_right, z_left)
 
     def core_send(i):
         return send(xbuf.at[i, c], xbuf.at[i, c], core_id)
@@ -159,11 +159,9 @@
         return jnp.concatenate([near[:, columns], far[:, columns]], axis=0)
 
     def turn_values():
-        for a in range(2):
-            for y in range(2):
-                resp_values[z, a, :, y * ROWS : (y + 1) * ROWS] = values_in[
-                    y, :, a * 128 : (a + 1) * 128
-                ].T
+        for half, to in ((yl, resp.at[z, yl]), (other, far_block)):
+            for a in range(2):
+                to[1, a] = values_in[:, head_lanes(half, a)].T
 
     present(tables)
     lane = lax.broadcasted_iota(jnp.int32, (1, 2 * ROWS), 1)
@@ -182,29 +180,25 @@
 
     def absorb(a, resp_slots, prompt_slots):
         bounds = []
-        for i in resp_slots:
-            for n in range(4):
-                bounds.append(limit - half_ref[2 * ((n // 2) * Z + i) + n % 2] * 64)
+        for i, y in resp_slots:
+            bounds += [limit - half_ref[2 * (y * Z + i) + e] * 64 for e in range(2)]
         bounds += [None] * (2 * len(prompt_slots))
         count = 64 * len(bounds)
 
-        keys = [
-            resp_keys[i, :, :, a * 128 : (a + 1) * 128].reshape(2 * ROWS, 128) for i in resp_slots
-        ] + prompt_rows(prompt_slots, 0, a)
+        keys = [resp[i, y, 0, a] for i, y in resp_slots] + prompt_rows(prompt_slots, 0, a)
+        keys = jnp.concatenate(keys, axis=0)
         for n, part in enumerate(prompt_rows(prompt_slots, 1, a)):
             v_turned[:, n * 128 : n * 128 + 128] = part.T
 
         def score(query):
-            pieces, tops, n = [], [], 0
-            for part in keys:
-                scores = nt(part, query) * SCORE_SCALE
-                for m in range(part.shape[0] // 64):
-                    piece = scores[64 * m : 64 * m + 64]
-                    if bounds[n] is not None:
-                        piece = jnp.where(down <= bounds[n], piece, MASKED)
-                    tops.append(jnp.max(piece.reshape(8, 8, 2 * ROWS), axis=0))
-                    pieces.append(piece)
-                    n += 1
+            pieces, tops = [], []
+            scores = nt(keys, query) * SCORE_SCALE
+            for n, bound in enumerate(bounds):
+                piece = scores[64 * n : 64 * n + 64]
+                if bound is not None:
+                    piece = jnp.where(down <= bound, piece, MASKED)
+                tops.append(jnp.max(piece.reshape(8, 8, 2 * ROWS), axis=0))
+                pieces.append(piece)
             while len(tops) > 1:
                 tops = [
                     jnp.maximum(tops[i], tops[i + 1]) if i + 1 < len(tops) else tops[i]
@@ -215,7 +209,7 @@
         def body(t, carry):
             first = a * GROUP + t * 4
             heads = pl.ds(first, 4)
-            values = [resp_values[i, a] for i in resp_slots]
+            values = [resp[i, y, 1, a] for i, y in resp_slots]
             if prompt_slots:
                 values.append(v_turned[:, : 128 * len(prompt_slots)])
             values = jnp.concatenate(values, axis=1) if len(values) > 1 else values[0]
@@ -291,22 +285,20 @@
             gacc[n, 0] = key_part[n * 128 : n * 128 + 128].reshape(2, PROWS, 128)
             gacc[n, 1] = value_part[n * 128 : n * 128 + 128].reshape(2, PROWS, 128)
 
-    def scatter_step(own, outgoing, incoming, step, right, left):
-        halves = ((0,), (1,)) if step == 0 else ((0, 1), (0, 1))
-        before = ((0,), (1,)) if step == 1 else ((0, 1), (0, 1))
+    def z_scatter(a, step):
         copies = []
-        for way, peer in enumerate((right, left)):
-            for h in halves[way]:
-                part = own(way, h)
-                if step > 0 and h in before[way]:
-                    part = part + incoming[way, step - 1, h].astype(F32)
-                outgoing[way, step, h] = part.astype(BF)
-                copies.append(send(outgoing.at[way, step, h], incoming.at[way, step, h], peer))
+        for way, peer in enumerate((z_right, z_left)):
+            n = 0 if step == 0 else way
+            for h in (way,) if step == 0 else (0, 1):
+                part = gacc[n, h]
+                if step > 1 or (step == 1 and h == way):
+                    part = part + zs_in[a, way, step - 1, h].astype(F32)
+                zs_out[a, way, step, h] = part.astype(BF)
+            src, dst = zs_out.at[a, way, step], zs_in.at[a, way, step]
+            if step == 0:
+                src, dst = src.at[way], dst.at[way]
+            copies.append(send(src, dst, peer))
         return copies
-
-    def z_scatter(a, step):
-        own = (lambda way, h: gacc[0, h]) if step == 0 else (lambda way, h: gacc[way, h])
-        return scatter_step(own, zs_out.at[a], zs_in.at[a], step, z_right, z_left)
 
     def to_y_ring(a):
         for h in range(2):
@@ -336,19 +328,19 @@
             total = total + jnp.where(owner == target * 4 + yh * 2 + c, part, 0.0)
         return total
 
-    def x_scatter(a, step):
-        distance = 2 - step
-        targets = ((x + distance) % X, (x + X - distance) % X)
-        return scatter_step(
-            lambda way, h: destined(a, targets[way], h),
-            xs_out.at[a], xs_in.at[a], step, x_right, x_left,
-        )
+    def x_scatter(a):
+        copies = []
+        for n, (distance, peer) in enumerate(((2, far_x_id), (1, x_right), (3, x_left))):
+            for h in range(2):
+                xs_out[a, n, h] = destined(a, (x + distance) % X, h).astype(BF)
+            copies.append(send(xs_out.at[a, n], xs_in.at[a, n], peer))
+        return copies
 
     def store(a):
         for h, ref in enumerate((gk_ref, gv_ref)):
             total = destined(a, x, h)
-            for way in range(2):
-                total = total + xs_in[a, way, 1, h].astype(F32)
+            for n in range(3):
+                total = total + xs_in[a, n, h].astype(F32)
             ref[0, :, head_lanes(yl, a)] = total[0]
             ref[0, :, head_lanes(other, a)] = total[1]
 
@@ -367,29 +359,39 @@
 
     opposite = [(z + 4) % Z]
     p, r = [None, None], [None, None]
+    own, far = 0, 1
 
     def pass_on(step):
         for a in range(2):
             arrive(p[a])
             p[a] = prompt_gather(a, step)
 
-    def pass_on_resp(step):
-        for h in range(2):
-            arrive(r[h])
-            r[h] = resp_gather(step, h)
-
+    def pass_on_resp(which, step):
+        arrive(r[which])
+        r[which] = resp_gather(yl if which == own else other, step)
+
+    def mine_at(slots):
+        return [(i, yl) for i in slots]
+
+    def theirs_at(slots):
+        return [(i, other) for i in slots]
+
+    present(own_resp)
+    turn_values()
+    r[own] = resp_gather(yl, 0)
+    y_far = [send(far_block, resp.at[z, yl], y_id)]
+    send_queries(1)
     arrive(x0)
-    x1 = gather_step(lambda i, h: xbuf.at[i, c, h], x, X, 1, x_right, x_left)
+    x1 = gather_step(lambda i: xbuf.at[i, c], x, X, 1, x_right, x_left)
     cores += [core_send((x + 1) % X), core_send((x + X - 1) % X)]
-    present(own_resp)
-    arrive([y_resp[0]])
-    r[0] = resp_gather(0, 0)
-    arrive([y_resp[1]])
-    turn_values()
-    r[1] = resp_gather(0, 1)
+    present(own_prompt + [own_q, own_do])
+    pass_on_resp(own, 1)
+    arrive([y_q[0]])
+    absorb(0, mine_at([z] + pair(1)), [])
     arrive(x1)
     cores += [core_send((x + 2) % X)]
-    present(own_prompt + [own_q, own_do])
+    arrive(y_far)
+    r[far] = resp_gather(other, 0)
     arrive(cores)
     theirs = owner_ref[prompt_ref[x * 4 + (1 - yh) * 2 + c]]
     mine = owner_ref[prompt_ref[dp]]
@@ -404,9 +406,11 @@
         for a in range(2):
             chosen_out[n, a] = piece(owner, half, a)
         ring.append(send(chosen_out.at[n], chosen_in.at[n], peer))
-    arrive([y_q[0]])
-    absorb(0, [z], [])
-    pass_on_resp(1)
+    pass_on_resp(own, 2)
+    absorb(0, mine_at(pair(2)) + theirs_at([z]), [])
+    arrive([y_q[1]])
+    absorb(1, mine_at([z] + pair(1)), [])
+    pass_on_resp(far, 1)
     arrive(ring)
     here = (mine // 2) % 2 == yh
     for a in range(2):
@@ -414,39 +418,38 @@
             prompt[a, z, kv, yl] = jnp.where(here, piece(mine, yl, a)[kv], chosen_in[1, a, kv])
             prompt[a, z, kv, other] = jnp.where(here, chosen_in[0, a, kv], chosen_in[2, a, kv])
         p[a] = prompt_gather(a, 0)
+    pass_on_resp(own, 3)
     y_do = [
         send(do_ref.at[0, :, group_lanes(other, a)], do_far.at[:, a * 1024 : a * 1024 + 1024], y_id)
         for a in range(2)
     ]
-    absorb(0, pair(1), [])
-    arrive([y_q[1]])
-    absorb(1, [z] + pair(1), [])
+    absorb(1, mine_at(pair(2)) + theirs_at([z]), [])
+    absorb(0, mine_at(pair(3)) + theirs_at(pair(1)), [])
     pass_on(1)
-    pass_on_resp(2)
-    absorb(0, pair(2), [])
+    pass_on_resp(far, 2)
+    absorb(1, mine_at(pair(3)) + theirs_at(pair(1)), [])
+    arrive(r[own])
     pass_on(2)
-    absorb(1, pair(2), [])
-    pass_on_resp(3)
+    absorb(0, mine_at(opposite) + theirs_at(pair(2)), [])
+    pass_on_resp(far, 3)
+    absorb(1, mine_at(opposite) + theirs_at(pair(2)), [])
     pass_on(3)
-    absorb(0, pair(3), [])
-    absorb(1, pair(3), [])
+    absorb(0, theirs_at(pair(3)), [z] + pair(1) + pair(2))
     drain()
-    for h in range(2):
-        arrive(r[h])
-    absorb(0, opposite, [z] + pair(1) + pair(2))
+    absorb(1, theirs_at(pair(3)), [z] + pair(1) + pair(2))
+    arrive(r[far])
     arrive([y_do[0]])
     arrive(p[0])
-    absorb(0, [], pair(3) + opposite)
+    absorb(0, theirs_at(opposite), pair(3) + opposite)
     results = [finish(0)]
     gradients(0, opposite)
     s0 = z_scatter(0, 0)
-    absorb(1, opposite, [z] + pair(1) + pair(2))
     gradients(0, pair(3))
     arrive(s0)
     s0 = z_scatter(0, 1)
     arrive([y_do[1]])
     arrive(p[1])
-    absorb(1, [], pair(3) + opposite)
+    absorb(1, theirs_at(opposite), pair(3) + opposite)
     results += [finish(1)]
     own_result = fetch(out_near, out_ref.at[0, :, mine_q])
     gradients(1, opposite)
@@ -474,30 +477,24 @@
     t0 = to_core(0)
     gradients(1, [z])
     arrive(t0)
-    t0 = x_scatter(0, 0)
+    t0 = x_scatter(0)
     arrive(s1)
     t1 = to_y_ring(1)
-    arrive(t0)
-    t0 = x_scatter(0, 1)
+    drain()
     arrive(t1)
     t1 = to_core(1)
-    drain()
-    arrive(t1)
-    t1 = x_scatter(1, 0)
     arrive(t0)
     store(0)
-    arrive(t1)
-    t1 = x_scatter(1, 1)
     arrive(results)
     present([own_result])
+    arrive(t1)
+    t1 = x_scatter(1)
     drain()
     arrive(t1)
     store(1)
 
 
-COPIES = 128
-
-
+COPIES = 96
 PIECES = 4
 
 
@@ -543,9 +540,9 @@
             pltpu.VMEM((ROWS, HALF_Q), BF),
             pltpu.VMEM((ROWS, HALF_Q), BF),
             pltpu.VMEM((ROWS, HALF_Q), BF),
-            pltpu.VMEM((Z, 2, ROWS, HALF_KV), BF),
-            pltpu.VMEM((Z, 2, 128, 2 * ROWS), BF),
-            pltpu.VMEM((2, ROWS, HALF_KV), BF),
+            pltpu.VMEM((Z, 2, 2, 2, 128, 128), BF),
+            pltpu.VMEM((2, 2, 128, 128), BF),
+            pltpu.VMEM((ROWS, 512), BF),
             pltpu.VMEM((X, 2, 2, PROWS, 512), BF),
             pltpu.VMEM((3, 2, 2, PROWS, 128), BF),
             pltpu.VMEM((3, 2, 2, PROWS, 128), BF),
@@ -561,8 +558,8 @@
             pltpu.VMEM((2, 2, PROWS, 128), BF),
             pltpu.VMEM((2, 2) + block, BF),
             pltpu.VMEM((2, 2) + block, BF),
-            pltpu.VMEM((2, 2, 2) + block, BF),
-            pltpu.VMEM((2, 2, 2) + block, BF),
+            pltpu.VMEM((2, 3) + block, BF),
+            pltpu.VMEM((2, 3) + block, BF),
             pltpu.SMEM((16,), jnp.int32),
             pltpu.SMEM((16,), jnp.int32),
             pltpu.SMEM((16,), jnp.int32),

time: 101 us -> 94 us (0.931)
  Pallas kernels: 100 us -> 93.1 us
    pallas_call x1, Pallas kernels: 98 us -> 91 us  [on_device(): pl.pallas_call(kernel, out_shape=(jax.ShapeDtypeStruct((1, ROWS, 4096), B...]
where the time goes in v7:
time: 94 us; the launch traced here: 93.9 us
  Pallas kernels  93.1 us (99%)
    pallas_call x1, Pallas kernels, on_device(): pl.pallas_call(kernel, out_shape=(jax.ShapeDtypeStruct((1, ROWS, 4096), B...  91 us
    pallas_call x1, Pallas kernels, on_device(): pl.pallas_call(copy_out, out_shape=tuple((jax.ShapeDtypeStruct(r.shape, r...  2.1 us

profile of v7, /device:TPU:1, one launch (start us, length us, event | category | flops | bytes accessed | tf_op | source)
XLA Modules:
  0.0 93.9 jit_solution(16811694282016723892)
XLA Ops:
  0.6 91.0 %shard_map.121 = (bf16[1,128,4096]{2,1,0:T(8,128)(2,1)}, f32[1,64,512]{2,1,0:T(8,128)}, f32[1,64,512]{2,1,0:T(8,128)}) custom-call(bf16[1,128,4096]{2,1,0:T(8,128)(2,1)} %q_ref.1, bf16[1,128,512]{2,1,0:T(8,128)(2,1)} %rk_ref.1, bf16[1,128,512]{2,1,0:T(8,128)(2,1)} %rv_ref.1, bf16[1,64,512]{2,1,0:T(8,128)(2,1)} %pk_ref.1, bf16[1,64,512]{2,1,0:T(8,128)(2,1)} %pv_ref.1, ...), custom_call_target="tpu_custom_call" | custom-call | flops 10000000000 | bytes 8388608 | tf_op jit(solution)/shard_map/pallas_call | solution.py:527
  91.6 2.1 %shard_map.122 = (bf16[1,128,4096]{2,1,0:T(8,128)(2,1)}, f32[1,64,512]{2,1,0:T(8,128)}, f32[1,64,512]{2,1,0:T(8,128)}) custom-call(bf16[1,128,4096]{2,1,0:T(8,128)(2,1)} %get-tuple-element.6.refs_0_, f32[1,64,512]{2,1,0:T(8,128)} %get-tuple-element.7.refs_1_, f32[1,64,512]{2,1,0:T(8,128)} %get-tuple-element.8.refs_2_), custom_call_target="tpu_custom_call" | custom-call | tf_op jit(solution)/shard_map/pallas_call | solution.py:578

commit v8 on v7

--- a/solution.py
+++ b/solution.py
@@ -107,13 +107,14 @@
 
     started = []
 
-    def send(src, dst, peer):
+    def send(src, dst, peer, begin=True):
         index = len(started)
         copy = pltpu.make_async_remote_copy(
             src_ref=src, dst_ref=dst, send_sem=send_sem.at[index], recv_sem=recv_sem.at[index],
             device_id=peer, device_id_type=MESH,
         )
-        copy.start()
+        if begin:
+            copy.start()
         started.append(copy)
         return copy
 
@@ -132,24 +133,29 @@
         near, far = q_ref.at[0, :, group_lanes(other, a)], q_far.at[:, a * 1024 : a * 1024 + 1024]
         y_q[a] = send(near, far, y_id)
 
+    own_keys = [
+        send(rk_ref.at[0, :, head_lanes(yl, a)], resp.at[z, yl, 0, a], peer)
+        for peer in (z_right, z_left)
+        for a in range(2)
+    ]
     send_queries(0)
     cores = [
         send(ref.at[0], xbuf.at[x, c, kv], core_id) for kv, ref in enumerate((pk_ref, pv_ref))
     ]
 
-    def gather_step(slot, pos, n, step, right, left):
+    def gather_step(slot, pos, n, step, right, left, begin=True):
         copies = []
         for way, peer in enumerate((right, left)):
             at = slot((pos + n - step) % n if way == 0 else (pos + step) % n)
             at = at.at[way] if step == n // 2 - 1 else at
-            copies.append(send(at, at, peer))
+            copies.append(send(at, at, peer, begin))
         return copies
 
-    def resp_gather(y, step):
-        return gather_step(lambda i: resp.at[i, y], z, Z, step, z_right, z_left)
-
-    def prompt_gather(a, step):
-        return gather_step(lambda i: prompt.at[a, i], z, Z, step, z_right, z_left)
+    def resp_gather(y, step, begin=True):
+        return gather_step(lambda i: resp.at[i, y], z, Z, step, z_right, z_left, begin)
+
+    def prompt_gather(a, step, begin=True):
+        return gather_step(lambda i: prompt.at[a, i], z, Z, step, z_right, z_left, begin)
 
     def core_send(i):
         return send(xbuf.at[i, c], xbuf.at[i, c], core_id)
@@ -178,7 +184,7 @@
     def prompt_rows(slots, kv, a):
         return [prompt[a, i, kv].reshape(2 * PROWS, 128) for i in slots]
 
-    def absorb(a, resp_slots, prompt_slots):
+    def absorb(a, resp_slots, prompt_slots, between=None):
         bounds = []
         for i, y in resp_slots:
             bounds += [limit - half_ref[2 * (y * Z + i) + e] * 64 for e in range(2)]
@@ -231,6 +237,8 @@
             for j in range(4):
                 m_ref[first + j] = peaks[j]
                 acc_ref[first + j] = mixes[j]
+            if between is not None:
+                pl.when(t == 0)(between)
             return carry
 
         lax.fori_loop(0, 2, body, 0)
@@ -361,14 +369,23 @@
     p, r = [None, None], [None, None]
     own, far = 0, 1
 
-    def pass_on(step):
-        for a in range(2):
-            arrive(p[a])
-            p[a] = prompt_gather(a, step)
-
-    def pass_on_resp(which, step):
-        arrive(r[which])
-        r[which] = resp_gather(yl if which == own else other, step)
+    def exchange(held, which, following, now):
+        previous, held[which] = held[which], following
+
+        def act():
+            arrive(previous)
+            for copy in following:
+                copy.start()
+
+        if now:
+            act()
+        return act
+
+    def pass_on(a, step, now=True):
+        return exchange(p, a, prompt_gather(a, step, False), now)
+
+    def pass_on_resp(which, step, now=True):
+        return exchange(r, which, resp_gather(yl if which == own else other, step, False), now)
 
     def mine_at(slots):
         return [(i, yl) for i in slots]
@@ -378,7 +395,9 @@
 
     present(own_resp)
     turn_values()
-    r[own] = resp_gather(yl, 0)
+    r[own] = own_keys + [
+        send(resp.at[z, yl, 1], resp.at[z, yl, 1], peer) for peer in (z_right, z_left)
+    ]
     y_far = [send(far_block, resp.at[z, yl], y_id)]
     send_queries(1)
     arrive(x0)
@@ -386,8 +405,6 @@
     cores += [core_send((x + 1) % X), core_send((x + X - 1) % X)]
     present(own_prompt + [own_q, own_do])
     pass_on_resp(own, 1)
-    arrive([y_q[0]])
-    absorb(0, mine_at([z] + pair(1)), [])
     arrive(x1)
     cores += [core_send((x + 2) % X)]
     arrive(y_far)
@@ -407,9 +424,9 @@
             chosen_out[n, a] = piece(owner, half, a)
         ring.append(send(chosen_out.at[n], chosen_in.at[n], peer))
     pass_on_resp(own, 2)
+    arrive([y_q[0]])
+    absorb(0, mine_at([z] + pair(1)), [])
     absorb(0, mine_at(pair(2)) + theirs_at([z]), [])
-    arrive([y_q[1]])
-    absorb(1, mine_at([z] + pair(1)), [])
     pass_on_resp(far, 1)
     arrive(ring)
     here = (mine // 2) % 2 == yh
@@ -418,68 +435,70 @@
             prompt[a, z, kv, yl] = jnp.where(here, piece(mine, yl, a)[kv], chosen_in[1, a, kv])
             prompt[a, z, kv, other] = jnp.where(here, chosen_in[0, a, kv], chosen_in[2, a, kv])
         p[a] = prompt_gather(a, 0)
-    pass_on_resp(own, 3)
     y_do = [
         send(do_ref.at[0, :, group_lanes(other, a)], do_far.at[:, a * 1024 : a * 1024 + 1024], y_id)
         for a in range(2)
     ]
+    arrive([y_q[1]])
+    absorb(1, mine_at([z] + pair(1)), [])
+    pass_on_resp(own, 3)
     absorb(1, mine_at(pair(2)) + theirs_at([z]), [])
-    absorb(0, mine_at(pair(3)) + theirs_at(pair(1)), [])
-    pass_on(1)
-    pass_on_resp(far, 2)
-    absorb(1, mine_at(pair(3)) + theirs_at(pair(1)), [])
+    pass_on(0, 1)
+    pass_on(1, 1)
+    absorb(0, mine_at(pair(3)) + theirs_at(pair(1)), [], pass_on_resp(far, 2, False))
+    absorb(1, mine_at(pair(3)) + theirs_at(pair(1)), [], pass_on(0, 2, False))
+    pass_on(1, 2)
     arrive(r[own])
-    pass_on(2)
-    absorb(0, mine_at(opposite) + theirs_at(pair(2)), [])
-    pass_on_resp(far, 3)
-    absorb(1, mine_at(opposite) + theirs_at(pair(2)), [])
-    pass_on(3)
-    absorb(0, theirs_at(pair(3)), [z] + pair(1) + pair(2))
+    near = [z] + pair(1)
+    absorb(0, mine_at(opposite) + theirs_at(pair(2)), near, pass_on_resp(far, 3, False))
+    pass_on(0, 3)
+    absorb(1, mine_at(opposite) + theirs_at(pair(2)), near, pass_on(1, 3, False))
     drain()
-    absorb(1, theirs_at(pair(3)), [z] + pair(1) + pair(2))
     arrive(r[far])
+    absorb(0, theirs_at(pair(3) + opposite), pair(2))
+    absorb(1, theirs_at(pair(3) + opposite), pair(2))
     arrive([y_do[0]])
     arrive(p[0])
-    absorb(0, theirs_at(opposite), pair(3) + opposite)
+    absorb(0, [], pair(3) + opposite)
     results = [finish(0)]
     gradients(0, opposite)
     s0 = z_scatter(0, 0)
-    gradients(0, pair(3))
-    arrive(s0)
-    s0 = z_scatter(0, 1)
     arrive([y_do[1]])
     arrive(p[1])
-    absorb(1, theirs_at(opposite), pair(3) + opposite)
+    absorb(1, [], pair(3) + opposite)
     results += [finish(1)]
     own_result = fetch(out_near, out_ref.at[0, :, mine_q])
     gradients(1, opposite)
     s1 = z_scatter(1, 0)
+    gradients(0, pair(3))
+    arrive(s0)
+    s0 = z_scatter(0, 1)
+    gradients(1, pair(3))
+    arrive(s1)
+    s1 = z_scatter(1, 1)
     gradients(0, pair(2))
     arrive(s0)
     s0 = z_scatter(0, 2)
-    gradients(1, pair(3))
+    gradients(1, pair(2))
     arrive(s1)
-    s1 = z_scatter(1, 1)
+    s1 = z_scatter(1, 2)
     gradients(0, pair(1))
     arrive(s0)
     s0 = z_scatter(0, 3)
-    gradients(1, pair(2))
-    arrive(s1)
-    s1 = z_scatter(1, 2)
-    gradients(0, [z])
-    arrive(s0)
-
-    t0 = to_y_ring(0)
     gradients(1, pair(1))
     arrive(s1)
     s1 = z_scatter(1, 3)
+    gradients(0, [z])
+    arrive(s0)
+
+    t0 = to_y_ring(0)
+    gradients(1, [z])
     arrive(t0)
     t0 = to_core(0)
-    gradients(1, [z])
+    arrive(s1)
+    t1 = to_y_ring(1)
     arrive(t0)
     t0 = x_scatter(0)
-    arrive(s1)
-    t1 = to_y_ring(1)
     drain()
     arrive(t1)
     t1 = to_core(1)

time: 94 us -> 91.7 us (0.976)
  Pallas kernels: 93.1 us -> 90.7 us
    pallas_call x1, Pallas kernels: 91 us -> 88.6 us  [on_device(): pl.pallas_call(kernel, out_shape=(jax.ShapeDtypeStruct((1, ROWS, 4096), B...]
where the time goes in v8:
time: 91.7 us; the launch traced here: 91.5 us
  Pallas kernels  90.7 us (99%)
    pallas_call x1, Pallas kernels, on_device(): pl.pallas_call(kernel, out_shape=(jax.ShapeDtypeStruct((1, ROWS, 4096), B...  88.6 us
    pallas_call x1, Pallas kernels, on_device(): pl.pallas_call(copy_out, out_shape=tuple((jax.ShapeDtypeStruct(r.shape, r...  2.1 us

profile of v8, /device:TPU:1, one launch (start us, length us, event | category | flops | bytes accessed | tf_op | source)
XLA Modules:
  0.0 91.5 jit_solution(16081898481826303839)
XLA Ops:
  0.6 88.6 %shard_map.121 = (bf16[1,128,4096]{2,1,0:T(8,128)(2,1)}, f32[1,64,512]{2,1,0:T(8,128)}, f32[1,64,512]{2,1,0:T(8,128)}) custom-call(bf16[1,128,4096]{2,1,0:T(8,128)(2,1)} %q_ref.1, bf16[1,128,512]{2,1,0:T(8,128)(2,1)} %rk_ref.1, bf16[1,128,512]{2,1,0:T(8,128)(2,1)} %rv_ref.1, bf16[1,64,512]{2,1,0:T(8,128)(2,1)} %pk_ref.1, bf16[1,64,512]{2,1,0:T(8,128)(2,1)} %pv_ref.1, ...), custom_call_target="tpu_custom_call" | custom-call | flops 10000000000 | bytes 8388608 | tf_op jit(solution)/shard_map/pallas_call | solution.py:546
  89.3 2.1 %shard_map.122 = (bf16[1,128,4096]{2,1,0:T(8,128)(2,1)}, f32[1,64,512]{2,1,0:T(8,128)}, f32[1,64,512]{2,1,0:T(8,128)}) custom-call(bf16[1,128,4096]{2,1,0:T(8,128)(2,1)} %get-tuple-element.6.refs_0_, f32[1,64,512]{2,1,0:T(8,128)} %get-tuple-element.7.refs_1_, f32[1,64,512]{2,1,0:T(8,128)} %get-tuple-element.8.refs_2_), custom_call_target="tpu_custom_call" | custom-call | tf_op jit(solution)/shard_map/pallas_call | solution.py:597

commit v9 on v8

--- a/solution.py
+++ b/solution.py
@@ -354,8 +354,8 @@
 
     drained = []
 
-    def drain():
-        for copy in started[len(drained) :]:
+    def drain(but=0):
+        for copy in started[len(drained) : len(started) - but]:
             copy.wait_send()
             drained.append(copy)
 
@@ -405,8 +405,15 @@
     cores += [core_send((x + 1) % X), core_send((x + X - 1) % X)]
     present(own_prompt + [own_q, own_do])
     pass_on_resp(own, 1)
-    arrive(x1)
-    cores += [core_send((x + 2) % X)]
+    arrive([y_q[0]])
+    last_core = [send(xbuf.at[(x + 2) % X, c], xbuf.at[(x + 2) % X, c], core_id, False)]
+    cores += last_core
+
+    def feed_core():
+        arrive(x1)
+        last_core[0].start()
+
+    absorb(0, mine_at([z] + pair(1)), [], feed_core)
     arrive(y_far)
     r[far] = resp_gather(other, 0)
     arrive(cores)
@@ -424,8 +431,6 @@
             chosen_out[n, a] = piece(owner, half, a)
         ring.append(send(chosen_out.at[n], chosen_in.at[n], peer))
     pass_on_resp(own, 2)
-    arrive([y_q[0]])
-    absorb(0, mine_at([z] + pair(1)), [])
     absorb(0, mine_at(pair(2)) + theirs_at([z]), [])
     pass_on_resp(far, 1)
     arrive(ring)
@@ -434,7 +439,7 @@
         for kv in range(2):
             prompt[a, z, kv, yl] = jnp.where(here, piece(mine, yl, a)[kv], chosen_in[1, a, kv])
             prompt[a, z, kv, other] = jnp.where(here, chosen_in[0, a, kv], chosen_in[2, a, kv])
-        p[a] = prompt_gather(a, 0)
+        p[a] = prompt_gather(a, 0, a == 0)
     y_do = [
         send(do_ref.at[0, :, group_lanes(other, a)], do_far.at[:, a * 1024 : a * 1024 + 1024], y_id)
         for a in range(2)
@@ -444,25 +449,31 @@
     pass_on_resp(own, 3)
     absorb(1, mine_at(pair(2)) + theirs_at([z]), [])
     pass_on(0, 1)
+    for copy in p[1]:
+        copy.start()
+    absorb(0, mine_at(pair(3)) + theirs_at(pair(1)), [], pass_on_resp(far, 2, False))
+    pass_on(0, 2)
     pass_on(1, 1)
-    absorb(0, mine_at(pair(3)) + theirs_at(pair(1)), [], pass_on_resp(far, 2, False))
-    absorb(1, mine_at(pair(3)) + theirs_at(pair(1)), [], pass_on(0, 2, False))
-    pass_on(1, 2)
+    absorb(1, mine_at(pair(3)) + theirs_at(pair(1)), [])
     arrive(r[own])
     near = [z] + pair(1)
     absorb(0, mine_at(opposite) + theirs_at(pair(2)), near, pass_on_resp(far, 3, False))
     pass_on(0, 3)
-    absorb(1, mine_at(opposite) + theirs_at(pair(2)), near, pass_on(1, 3, False))
+    pass_on(1, 2)
+    absorb(1, mine_at(opposite) + theirs_at(pair(2)), near)
     drain()
     arrive(r[far])
-    absorb(0, theirs_at(pair(3) + opposite), pair(2))
-    absorb(1, theirs_at(pair(3) + opposite), pair(2))
+    absorb(0, theirs_at(pair(3) + opposite), pair(2), pass_on(1, 3, False))
     arrive([y_do[0]])
     arrive(p[0])
     absorb(0, [], pair(3) + opposite)
     results = [finish(0)]
     gradients(0, opposite)
     s0 = z_scatter(0, 0)
+    absorb(1, theirs_at(pair(3) + opposite), pair(2))
+    gradients(0, pair(3))
+    arrive(s0)
+    s0 = z_scatter(0, 1)
     arrive([y_do[1]])
     arrive(p[1])
     absorb(1, [], pair(3) + opposite)
@@ -470,44 +481,41 @@
     own_result = fetch(out_near, out_ref.at[0, :, mine_q])
     gradients(1, opposite)
     s1 = z_scatter(1, 0)
-    gradients(0, pair(3))
+    gradients(0, pair(2))
     arrive(s0)
-    s0 = z_scatter(0, 1)
+    s0 = z_scatter(0, 2)
     gradients(1, pair(3))
     arrive(s1)
     s1 = z_scatter(1, 1)
-    gradients(0, pair(2))
+    gradients(0, pair(1))
     arrive(s0)
-    s0 = z_scatter(0, 2)
+    s0 = z_scatter(0, 3)
     gradients(1, pair(2))
     arrive(s1)
     s1 = z_scatter(1, 2)
-    gradients(0, pair(1))
+    gradients(0, [z])
     arrive(s0)
-    s0 = z_scatter(0, 3)
+
+    t0 = to_y_ring(0)
     gradients(1, pair(1))
     arrive(s1)
     s1 = z_scatter(1, 3)
-    gradients(0, [z])
-    arrive(s0)
-
-    t0 = to_y_ring(0)
+    arrive(t0)
+    t0 = to_core(0)
     gradients(1, [z])
     arrive(t0)
-    t0 = to_core(0)
+    t0 = x_scatter(0)
     arrive(s1)
     t1 = to_y_ring(1)
-    arrive(t0)
-    t0 = x_scatter(0)
-    drain()
+    drain(6)
     arrive(t1)
     t1 = to_core(1)
+    arrive(t1)
+    t1 = x_scatter(1)
     arrive(t0)
     store(0)
     arrive(results)
     present([own_result])
-    arrive(t1)
-    t1 = x_scatter(1)
     drain()
     arrive(t1)
     store(1)

time: 91.7 us -> 91.2 us (level)
  no operation moved by 1% of the time
where the time goes in v9:
time: 91.2 us; the launch traced here: 91.1 us
  Pallas kernels  90.3 us (99%)
    pallas_call x1, Pallas kernels, on_device(): pl.pallas_call(kernel, out_shape=(jax.ShapeDtypeStruct((1, ROWS, 4096), B...  88.2 us
    pallas_call x1, Pallas kernels, on_device(): pl.pallas_call(copy_out, out_shape=tuple((jax.ShapeDtypeStruct(r.shape, r...  2.1 us

profile of v9, /device:TPU:1, one launch (start us, length us, event | category | flops | bytes accessed | tf_op | source)
XLA Modules:
  0.0 91.1 jit_solution(9429674923692995887)
XLA Ops:
  0.6 88.2 %shard_map.121 = (bf16[1,128,4096]{2,1,0:T(8,128)(2,1)}, f32[1,64,512]{2,1,0:T(8,128)}, f32[1,64,512]{2,1,0:T(8,128)}) custom-call(bf16[1,128,4096]{2,1,0:T(8,128)(2,1)} %q_ref.1, bf16[1,128,512]{2,1,0:T(8,128)(2,1)} %rk_ref.1, bf16[1,128,512]{2,1,0:T(8,128)(2,1)} %rv_ref.1, bf16[1,64,512]{2,1,0:T(8,128)(2,1)} %pk_ref.1, bf16[1,64,512]{2,1,0:T(8,128)(2,1)} %pv_ref.1, ...), custom_call_target="tpu_custom_call" | custom-call | flops 10000000000 | bytes 8388608 | tf_op jit(solution)/shard_map/pallas_call | solution.py:554
  88.9 2.1 %shard_map.122 = (bf16[1,128,4096]{2,1,0:T(8,128)(2,1)}, f32[1,64,512]{2,1,0:T(8,128)}, f32[1,64,512]{2,1,0:T(8,128)}) custom-call(bf16[1,128,4096]{2,1,0:T(8,128)(2,1)} %get-tuple-element.6.refs_0_, f32[1,64,512]{2,1,0:T(8,128)} %get-tuple-element.7.refs_1_, f32[1,64,512]{2,1,0:T(8,128)} %get-tuple-element.8.refs_2_), custom_call_target="tpu_custom_call" | custom-call | tf_op jit(solution)/shard_map/pallas_call | solution.py:605

commit v10 on v9

--- a/solution.py
+++ b/solution.py
@@ -38,7 +38,7 @@
 def kernel(
     q_ref, rk_ref, rv_ref, pk_ref, pv_ref, do_ref, owner_hbm, prompt_hbm, length_hbm, half_hbm,
     out_ref, gk_ref, gv_ref,
-    q_near, q_far, do_near, do_far, out_near, out_far,
+    q_near, q_far, do_near, do_far, out_near, out_far, q_turned, do_turned,
     resp, far_block, values_in, xbuf, chosen_out, chosen_in, prompt, v_turned,
     m_ref, acc_ref, lse_ref, delta_ref, gacc,
     zs_out, zs_in, share_out, share, core_in, xs_out, xs_in,
@@ -164,6 +164,15 @@
         columns = pl.ds(pl.multiple_of(h * 128, 128), 128)
         return jnp.concatenate([near[:, columns], far[:, columns]], axis=0)
 
+    def prepare(source, part, a, turned):
+        def body(g, carry):
+            h = a * GROUP + g
+            tile = source[:, pl.ds(pl.multiple_of(h * 128, 128), 128)]
+            turned[h, :, part * ROWS : (part + 1) * ROWS] = tile.T
+            return carry
+
+        lax.fori_loop(0, GROUP, body, 0, unroll=4)
+
     def turn_values():
         for half, to in ((yl, resp.at[z, yl]), (other, far_block)):
             for a in range(2):
@@ -198,7 +207,7 @@
 
         def score(query):
             pieces, tops = [], []
-            scores = nt(keys, query) * SCORE_SCALE
+            scores = nn(keys, query) * SCORE_SCALE
             for n, bound in enumerate(bounds):
                 piece = scores[64 * n : 64 * n + 64]
                 if bound is not None:
@@ -229,9 +238,9 @@
                 peaks.append(peak)
                 mixes.append(old_mixed[j] * jnp.exp2(old[j] - peak) + nn(values, weights))
 
-            ready = score(head_of(q_near, q_far, first))
+            ready = score(q_turned[first])
             for j in range(4):
-                following = score(head_of(q_near, q_far, first + j + 1)) if j < 3 else None
+                following = score(q_turned[first + j + 1]) if j < 3 else None
                 weigh(j, *ready)
                 ready = following
             for j in range(4):
@@ -248,20 +257,17 @@
             first = a * GROUP + t * 4
             heads = pl.ds(first, 4)
             peak, mixed = m_ref[heads], acc_ref[heads]
-            outs, sums, deltas = [], [], []
+            outs, logs, deltas = [], [], []
             for j in range(4):
                 total = mixed[j, 128:129]
-                result = (mixed[j, :128] / total).T
-                sums.append(peak[j] + jnp.log(total) * LOG2E)
-                product = result * head_of(do_near, do_far, first + j).astype(F32)
-                high = product.astype(BF)
-                low = (product - high.astype(F32)).astype(BF)
-                halves = jnp.concatenate([high, low], axis=1)
-                deltas.append(nt(jnp.ones((16, 256), BF), halves)[:1])
-                outs.append(result.astype(BF))
+                result = mixed[j, :128] / total
+                logs.append(peak[j] + jnp.log(total) * LOG2E)
+                cotangent = do_turned[first + j].astype(F32)
+                deltas.append(jnp.sum(cotangent * result, axis=0, keepdims=True))
+                outs.append(result.T.astype(BF))
             for j in range(4):
                 h = first + j
-                lse_ref[h] = sums[j]
+                lse_ref[h] = logs[j]
                 delta_ref[h] = deltas[j]
                 columns = pl.ds(pl.multiple_of(h * 128, 128), 128)
                 out_near[:, columns] = outs[j][:ROWS]
@@ -280,9 +286,9 @@
         queries = [head_of(q_near, q_far, h) for h in heads]
         cotangents = [head_of(do_near, do_far, h) for h in heads]
         all_probs, all_slopes = [], []
-        for h, query, cotangent in zip(heads, queries, cotangents):
-            probs = jnp.exp2(nt(keys, query) * SCORE_SCALE - lse_ref[h])
-            slopes = probs * (nt(values, cotangent) - delta_ref[h])
+        for h in heads:
+            probs = jnp.exp2(nn(keys, q_turned[h]) * SCORE_SCALE - lse_ref[h])
+            slopes = probs * (nn(values, do_turned[h]) - delta_ref[h])
             all_probs.append(probs.astype(BF))
             all_slopes.append(slopes.astype(BF))
         queries = jnp.concatenate(queries, axis=0)
@@ -400,12 +406,16 @@
     ]
     y_far = [send(far_block, resp.at[z, yl], y_id)]
     send_queries(1)
+    present([own_q, own_do])
+    for a in range(2):
+        prepare(q_near, 0, a, q_turned)
     arrive(x0)
     x1 = gather_step(lambda i: xbuf.at[i, c], x, X, 1, x_right, x_left)
     cores += [core_send((x + 1) % X), core_send((x + X - 1) % X)]
-    present(own_prompt + [own_q, own_do])
+    present(own_prompt)
     pass_on_resp(own, 1)
     arrive([y_q[0]])
+    prepare(q_far, 1, 0, q_turned)
     last_core = [send(xbuf.at[(x + 2) % X, c], xbuf.at[(x + 2) % X, c], core_id, False)]
     cores += last_core
 
@@ -416,6 +426,8 @@
     absorb(0, mine_at([z] + pair(1)), [], feed_core)
     arrive(y_far)
     r[far] = resp_gather(other, 0)
+    for a in range(2):
+        prepare(do_near, 0, a, do_turned)
     arrive(cores)
     theirs = owner_ref[prompt_ref[x * 4 + (1 - yh) * 2 + c]]
     mine = owner_ref[prompt_ref[dp]]
@@ -445,6 +457,7 @@
         for a in range(2)
     ]
     arrive([y_q[1]])
+    prepare(q_far, 1, 1, q_turned)
     absorb(1, mine_at([z] + pair(1)), [])
     pass_on_resp(own, 3)
     absorb(1, mine_at(pair(2)) + theirs_at([z]), [])
@@ -465,6 +478,7 @@
     arrive(r[far])
     absorb(0, theirs_at(pair(3) + opposite), pair(2), pass_on(1, 3, False))
     arrive([y_do[0]])
+    prepare(do_far, 1, 0, do_turned)
     arrive(p[0])
     absorb(0, [], pair(3) + opposite)
     results = [finish(0)]
@@ -475,6 +489,7 @@
     arrive(s0)
     s0 = z_scatter(0, 1)
     arrive([y_do[1]])
+    prepare(do_far, 1, 1, do_turned)
     arrive(p[1])
     absorb(1, [], pair(3) + opposite)
     results += [finish(1)]
@@ -567,6 +582,8 @@
             pltpu.VMEM((ROWS, HALF_Q), BF),
             pltpu.VMEM((ROWS, HALF_Q), BF),
             pltpu.VMEM((ROWS, HALF_Q), BF),
+            pltpu.VMEM((16, 128, 256), BF),
+            pltpu.VMEM((16, 128, 256), BF),
             pltpu.VMEM((Z, 2, 2, 2, 128, 128), BF),
             pltpu.VMEM((2, 2, 128, 128), BF),
             pltpu.VMEM((ROWS, 512), BF),

time: 91.2 us -> 91.4 us (level)
  no operation moved by 1% of the time
where the time goes in v10:
time: 91.4 us; the launch traced here: 91.2 us
  Pallas kernels  90.4 us (99%)
    pallas_call x1, Pallas kernels, on_device(): pl.pallas_call(kernel, out_shape=(jax.ShapeDtypeStruct((1, ROWS, 4096), B...  88.3 us
    pallas_call x1, Pallas kernels, on_device(): pl.pallas_call(copy_out, out_shape=tuple((jax.ShapeDtypeStruct(r.shape, r...  2.1 us

profile of v10, /device:TPU:1, one launch (start us, length us, event | category | flops | bytes accessed | tf_op | source)
XLA Modules:
  0.0 91.2 jit_solution(11140764168782938183)
XLA Ops:
  0.6 88.3 %shard_map.121 = (bf16[1,128,4096]{2,1,0:T(8,128)(2,1)}, f32[1,64,512]{2,1,0:T(8,128)}, f32[1,64,512]{2,1,0:T(8,128)}) custom-call(bf16[1,128,4096]{2,1,0:T(8,128)(2,1)} %q_ref.1, bf16[1,128,512]{2,1,0:T(8,128)(2,1)} %rk_ref.1, bf16[1,128,512]{2,1,0:T(8,128)(2,1)} %rv_ref.1, bf16[1,64,512]{2,1,0:T(8,128)(2,1)} %pk_ref.1, bf16[1,64,512]{2,1,0:T(8,128)(2,1)} %pv_ref.1, ...), custom_call_target="tpu_custom_call" | custom-call | flops 10000000000 | bytes 8388608 | tf_op jit(solution)/shard_map/pallas_call | solution.py:569
  89.0 2.1 %shard_map.122 = (bf16[1,128,4096]{2,1,0:T(8,128)(2,1)}, f32[1,64,512]{2,1,0:T(8,128)}, f32[1,64,512]{2,1,0:T(8,128)}) custom-call(bf16[1,128,4096]{2,1,0:T(8,128)(2,1)} %get-tuple-element.6.refs_0_, f32[1,64,512]{2,1,0:T(8,128)} %get-tuple-element.7.refs_1_, f32[1,64,512]{2,1,0:T(8,128)} %get-tuple-element.8.refs_2_), custom_call_target="tpu_custom_call" | custom-call | tf_op jit(solution)/shard_map/pallas_call | solution.py:622

commit v11 on v10

--- a/solution.py
+++ b/solution.py
@@ -52,6 +52,7 @@
     other = 1 - yl
     y_id = (dp, other * Z + z)
     z_right, z_left = (dp, yl * Z + (z + 1) % Z), (dp, yl * Z + (z + Z - 1) % Z)
+    z_right2, z_left2 = (dp, yl * Z + (z + 2) % Z), (dp, yl * Z + (z + Z - 2) % Z)
     x_right = (((x + 1) % X) * 4 + yh * 2 + c, blk)
     x_left = (((x + X - 1) % X) * 4 + yh * 2 + c, blk)
     core_id = (x * 4 + yh * 2 + (1 - c), blk)
@@ -100,7 +101,7 @@
     own_do = fetch(do_ref.at[0, :, mine_q], do_near)
 
     barrier = pltpu.get_barrier_semaphore()
-    peers = (y_id, z_right, z_left, x_right, x_left, core_id, yh_id, diagonal_id, far_x_id)
+    peers = (y_id, z_right, z_left, x_right, x_left, core_id, yh_id, diagonal_id, far_x_id, z_right2, z_left2)
     for peer in peers:
         pl.semaphore_signal(barrier, inc=1, device_id=peer, device_id_type=MESH)
     pl.semaphore_wait(barrier, len(peers))
@@ -154,8 +155,18 @@
     def resp_gather(y, step, begin=True):
         return gather_step(lambda i: resp.at[i, y], z, Z, step, z_right, z_left, begin)
 
-    def prompt_gather(a, step, begin=True):
-        return gather_step(lambda i: prompt.at[a, i], z, Z, step, z_right, z_left, begin)
+    def prompt_first(a):
+        at = prompt.at[a, z]
+        return [send(at, at, peer) for peer in (z_right2, z_left2, z_right, z_left)]
+
+    def prompt_second(a, begin):
+        copies = []
+        for way, (distance, near, far) in enumerate(
+            ((Z - 2, z_right, z_right2), (2, z_left, z_left2))
+        ):
+            at = prompt.at[a, (z + distance) % Z]
+            copies += [send(at.at[way], at.at[way], far, begin), send(at, at, near, begin)]
+        return copies
 
     def core_send(i):
         return send(xbuf.at[i, c], xbuf.at[i, c], core_id)
@@ -279,7 +290,7 @@
             out_far.at[:, a * 1024 : a * 1024 + 1024], out_ref.at[0, :, group_lanes(yl, a)], y_id
         )
 
-    def gradients(a, slots):
+    def gradients(a, slots, place=0):
         keys = jnp.concatenate(prompt_rows(slots, 0, a), axis=0)
         values = jnp.concatenate(prompt_rows(slots, 1, a), axis=0)
         heads = range(a * GROUP, a * GROUP + GROUP)
@@ -296,22 +307,30 @@
         key_part = nn(jnp.concatenate(all_slopes, axis=1), queries) * SCALE
         value_part = nn(jnp.concatenate(all_probs, axis=1), cotangents)
         for n in range(len(slots)):
-            gacc[n, 0] = key_part[n * 128 : n * 128 + 128].reshape(2, PROWS, 128)
-            gacc[n, 1] = value_part[n * 128 : n * 128 + 128].reshape(2, PROWS, 128)
-
-    def z_scatter(a, step):
+            gacc[place + n, 0] = key_part[n * 128 : n * 128 + 128].reshape(2, PROWS, 128)
+            gacc[place + n, 1] = value_part[n * 128 : n * 128 + 128].reshape(2, PROWS, 128)
+
+    def z_first(a):
         copies = []
-        for way, peer in enumerate((z_right, z_left)):
-            n = 0 if step == 0 else way
-            for h in (way,) if step == 0 else (0, 1):
-                part = gacc[n, h]
-                if step > 1 or (step == 1 and h == way):
-                    part = part + zs_in[a, way, step - 1, h].astype(F32)
-                zs_out[a, way, step, h] = part.astype(BF)
-            src, dst = zs_out.at[a, way, step], zs_in.at[a, way, step]
-            if step == 0:
-                src, dst = src.at[way], dst.at[way]
-            copies.append(send(src, dst, peer))
+        for way, (near, far) in enumerate(((z_right, z_right2), (z_left, z_left2))):
+            zs_out[a, way, 1, way] = gacc[0, way].astype(BF)
+            copies.append(send(zs_out.at[a, way, 1, way], zs_in.at[a, way, 1, way], far))
+            for h in range(2):
+                zs_out[a, way, 0, h] = gacc[1 + way, h].astype(BF)
+            copies.append(send(zs_out.at[a, way, 0], zs_in.at[a, way, 0], near))
+        return copies
+
+    def z_second(a):
+        copies = []
+        for way, (near, far) in enumerate(((z_right, z_right2), (z_left, z_left2))):
+            for h in range(2):
+                part = gacc[3 + way, h] + zs_in[a, way, 0, h].astype(F32)
+                if h == way:
+                    part = part + zs_in[a, way, 1, h].astype(F32)
+                zs_out[a, way, 2, h] = part.astype(BF)
+                zs_out[a, way, 3, h] = gacc[5 + way, h].astype(BF)
+            copies.append(send(zs_out.at[a, way, 2], zs_in.at[a, way, 2], far))
+            copies.append(send(zs_out.at[a, way, 3], zs_in.at[a, way, 3], near))
         return copies
 
     def to_y_ring(a):
@@ -319,6 +338,7 @@
             for n, where in enumerate((yl, other)):
                 total = gacc[0, h, where]
                 for way in range(2):
+                    total = total + zs_in[a, way, 2, h, where].astype(F32)
                     total = total + zs_in[a, way, 3, h, where].astype(F32)
                 (share.at[a, 0, 0] if n == 0 else share_out.at[a])[h] = total.astype(BF)
         return [
@@ -387,8 +407,8 @@
             act()
         return act
 
-    def pass_on(a, step, now=True):
-        return exchange(p, a, prompt_gather(a, step, False), now)
+    def pass_on(a, now=True):
+        return exchange(p, a, prompt_second(a, False), now)
 
     def pass_on_resp(which, step, now=True):
         return exchange(r, which, resp_gather(yl if which == own else other, step, False), now)
@@ -451,7 +471,7 @@
         for kv in range(2):
             prompt[a, z, kv, yl] = jnp.where(here, piece(mine, yl, a)[kv], chosen_in[1, a, kv])
             prompt[a, z, kv, other] = jnp.where(here, chosen_in[0, a, kv], chosen_in[2, a, kv])
-        p[a] = prompt_gather(a, 0, a == 0)
+        p[a] = prompt_first(a)
     y_do = [
         send(do_ref.at[0, :, group_lanes(other, a)], do_far.at[:, a * 1024 : a * 1024 + 1024], y_id)
         for a in range(2)
@@ -461,67 +481,47 @@
     absorb(1, mine_at([z] + pair(1)), [])
     pass_on_resp(own, 3)
     absorb(1, mine_at(pair(2)) + theirs_at([z]), [])
-    pass_on(0, 1)
-    for copy in p[1]:
-        copy.start()
     absorb(0, mine_at(pair(3)) + theirs_at(pair(1)), [], pass_on_resp(far, 2, False))
-    pass_on(0, 2)
-    pass_on(1, 1)
-    absorb(1, mine_at(pair(3)) + theirs_at(pair(1)), [])
+    pass_on(0)
+    absorb(1, mine_at(pair(3)) + theirs_at(pair(1)), [], pass_on(1, False))
     arrive(r[own])
-    near = [z] + pair(1)
+    near = [z] + pair(1) + pair(2)
     absorb(0, mine_at(opposite) + theirs_at(pair(2)), near, pass_on_resp(far, 3, False))
-    pass_on(0, 3)
-    pass_on(1, 2)
     absorb(1, mine_at(opposite) + theirs_at(pair(2)), near)
     drain()
     arrive(r[far])
-    absorb(0, theirs_at(pair(3) + opposite), pair(2), pass_on(1, 3, False))
     arrive([y_do[0]])
     prepare(do_far, 1, 0, do_turned)
     arrive(p[0])
-    absorb(0, [], pair(3) + opposite)
+    absorb(0, theirs_at(pair(3) + opposite), pair(3) + opposite)
     results = [finish(0)]
-    gradients(0, opposite)
-    s0 = z_scatter(0, 0)
-    absorb(1, theirs_at(pair(3) + opposite), pair(2))
-    gradients(0, pair(3))
-    arrive(s0)
-    s0 = z_scatter(0, 1)
+    gradients(0, opposite + pair(3))
+    s0 = z_first(0)
     arrive([y_do[1]])
     prepare(do_far, 1, 1, do_turned)
     arrive(p[1])
-    absorb(1, [], pair(3) + opposite)
+    absorb(1, theirs_at(pair(3) + opposite), pair(3) + opposite)
     results += [finish(1)]
     own_result = fetch(out_near, out_ref.at[0, :, mine_q])
-    gradients(1, opposite)
-    s1 = z_scatter(1, 0)
-    gradients(0, pair(2))
+    gradients(1, opposite + pair(3))
+    s1 = z_first(1)
+    gradients(0, pair(2) + pair(1), 3)
     arrive(s0)
-    s0 = z_scatter(0, 2)
-    gradients(1, pair(3))
+    s0 = z_second(0)
+    gradients(1, pair(2) + pair(1), 3)
     arrive(s1)
-    s1 = z_scatter(1, 1)
-    gradients(0, pair(1))
-    arrive(s0)
-    s0 = z_scatter(0, 3)
-    gradients(1, pair(2))
-    arrive(s1)
-    s1 = z_scatter(1, 2)
+    s1 = z_second(1)
     gradients(0, [z])
     arrive(s0)
 
     t0 = to_y_ring(0)
-    gradients(1, pair(1))
-    arrive(s1)
-    s1 = z_scatter(1, 3)
+    gradients(1, [z])
     arrive(t0)
     t0 = to_core(0)
-    gradients(1, [z])
+    arrive(s1)
+    t1 = to_y_ring(1)
     arrive(t0)
     t0 = x_scatter(0)
-    arrive(s1)
-    t1 = to_y_ring(1)
     drain(6)
     arrive(t1)
     t1 = to_core(1)
@@ -596,7 +596,7 @@
             pltpu.VMEM((16, 144, 256), F32),
             pltpu.VMEM((16, 1, 256), F32),
             pltpu.VMEM((16, 1, 256), F32),
-            pltpu.VMEM((2,) + block, F32),
+            pltpu.VMEM((7,) + block, F32),
             pltpu.VMEM((2, 2, 4) + block, BF),
             pltpu.VMEM((2, 2, 4) + block, BF),
             pltpu.VMEM((2, 2, PROWS, 128), BF),

time: 91.4 us -> 92.9 us (1.016)
  Pallas kernels: 90.4 us -> 92 us
    pallas_call x1, Pallas kernels: 88.3 us -> 89.9 us  [on_device(): pl.pallas_call(kernel, out_shape=(jax.ShapeDtypeStruct((1, ROWS, 4096), B...]
where the time goes in v11:
time: 92.9 us; the launch traced here: 92.8 us
  Pallas kernels  92 us (99%)
    pallas_call x1, Pallas kernels, on_device(): pl.pallas_call(kernel, out_shape=(jax.ShapeDtypeStruct((1, ROWS, 4096), B...  89.9 us
    pallas_call x1, Pallas kernels, on_device(): pl.pallas_call(copy_out, out_shape=tuple((jax.ShapeDtypeStruct(r.shape, r...  2.1 us

profile of v11, /device:TPU:1, one launch (start us, length us, event | category | flops | bytes accessed | tf_op | source)
XLA Modules:
  0.0 92.8 jit_solution(12270510703367997066)
XLA Ops:
  0.6 89.9 %shard_map.121 = (bf16[1,128,4096]{2,1,0:T(8,128)(2,1)}, f32[1,64,512]{2,1,0:T(8,128)}, f32[1,64,512]{2,1,0:T(8,128)}) custom-call(bf16[1,128,4096]{2,1,0:T(8,128)(2,1)} %q_ref.1, bf16[1,128,512]{2,1,0:T(8,128)(2,1)} %rk_ref.1, bf16[1,128,512]{2,1,0:T(8,128)(2,1)} %rv_ref.1, bf16[1,64,512]{2,1,0:T(8,128)(2,1)} %pk_ref.1, bf16[1,64,512]{2,1,0:T(8,128)(2,1)} %pv_ref.1, ...), custom_call_target="tpu_custom_call" | custom-call | flops 10000000000 | bytes 8388608 | tf_op jit(solution)/shard_map/pallas_call | solution.py:569
  90.5 2.1 %shard_map.122 = (bf16[1,128,4096]{2,1,0:T(8,128)(2,1)}, f32[1,64,512]{2,1,0:T(8,128)}, f32[1,64,512]{2,1,0:T(8,128)}) custom-call(bf16[1,128,4096]{2,1,0:T(8,128)(2,1)} %get-tuple-element.6.refs_0_, f32[1,64,512]{2,1,0:T(8,128)} %get-tuple-element.7.refs_1_, f32[1,64,512]{2,1,0:T(8,128)} %get-tuple-element.8.refs_2_), custom_call_target="tpu_custom_call" | custom-call | tf_op jit(solution)/shard_map/pallas_call | solution.py:622

commit v12 on v11

--- a/solution.py
+++ b/solution.py
@@ -155,18 +155,8 @@
     def resp_gather(y, step, begin=True):
         return gather_step(lambda i: resp.at[i, y], z, Z, step, z_right, z_left, begin)
 
-    def prompt_first(a):
-        at = prompt.at[a, z]
-        return [send(at, at, peer) for peer in (z_right2, z_left2, z_right, z_left)]
-
-    def prompt_second(a, begin):
-        copies = []
-        for way, (distance, near, far) in enumerate(
-            ((Z - 2, z_right, z_right2), (2, z_left, z_left2))
-        ):
-            at = prompt.at[a, (z + distance) % Z]
-            copies += [send(at.at[way], at.at[way], far, begin), send(at, at, near, begin)]
-        return copies
+    def prompt_gather(a, step, begin=True):
+        return gather_step(lambda i: prompt.at[a, i], z, Z, step, z_right, z_left, begin)
 
     def core_send(i):
         return send(xbuf.at[i, c], xbuf.at[i, c], core_id)
@@ -407,8 +397,8 @@
             act()
         return act
 
-    def pass_on(a, now=True):
-        return exchange(p, a, prompt_second(a, False), now)
+    def pass_on(a, step, now=True):
+        return exchange(p, a, prompt_gather(a, step, False), now)
 
     def pass_on_resp(which, step, now=True):
         return exchange(r, which, resp_gather(yl if which == own else other, step, False), now)
@@ -471,7 +461,7 @@
         for kv in range(2):
             prompt[a, z, kv, yl] = jnp.where(here, piece(mine, yl, a)[kv], chosen_in[1, a, kv])
             prompt[a, z, kv, other] = jnp.where(here, chosen_in[0, a, kv], chosen_in[2, a, kv])
-        p[a] = prompt_first(a)
+        p[a] = prompt_gather(a, 0, a == 0)
     y_do = [
         send(do_ref.at[0, :, group_lanes(other, a)], do_far.at[:, a * 1024 : a * 1024 + 1024], y_id)
         for a in range(2)
@@ -481,26 +471,34 @@
     absorb(1, mine_at([z] + pair(1)), [])
     pass_on_resp(own, 3)
     absorb(1, mine_at(pair(2)) + theirs_at([z]), [])
+    pass_on(0, 1)
+    for copy in p[1]:
+        copy.start()
     absorb(0, mine_at(pair(3)) + theirs_at(pair(1)), [], pass_on_resp(far, 2, False))
-    pass_on(0)
-    absorb(1, mine_at(pair(3)) + theirs_at(pair(1)), [], pass_on(1, False))
+    pass_on(0, 2)
+    pass_on(1, 1)
+    absorb(1, mine_at(pair(3)) + theirs_at(pair(1)), [])
     arrive(r[own])
-    near = [z] + pair(1) + pair(2)
+    near = [z] + pair(1)
     absorb(0, mine_at(opposite) + theirs_at(pair(2)), near, pass_on_resp(far, 3, False))
+    pass_on(0, 3)
+    pass_on(1, 2)
     absorb(1, mine_at(opposite) + theirs_at(pair(2)), near)
     drain()
     arrive(r[far])
+    absorb(0, theirs_at(pair(3) + opposite), pair(2), pass_on(1, 3, False))
     arrive([y_do[0]])
     prepare(do_far, 1, 0, do_turned)
     arrive(p[0])
-    absorb(0, theirs_at(pair(3) + opposite), pair(3) + opposite)
+    absorb(0, [], pair(3) + opposite)
     results = [finish(0)]
     gradients(0, opposite + pair(3))
     s0 = z_first(0)
+    absorb(1, theirs_at(pair(3) + opposite), pair(2))
     arrive([y_do[1]])
     prepare(do_far, 1, 1, do_turned)
     arrive(p[1])
-    absorb(1, theirs_at(pair(3) + opposite), pair(3) + opposite)
+    absorb(1, [], pair(3) + opposite)
     results += [finish(1)]
     own_result = fetch(out_near, out_ref.at[0, :, mine_q])
     gradients(1, opposite + pair(3))

time: 92.9 us -> 90 us (0.969)
  Pallas kernels: 92 us -> 89.1 us
    pallas_call x1, Pallas kernels: 89.9 us -> 87 us  [on_device(): pl.pallas_call(kernel, out_shape=(jax.ShapeDtypeStruct((1, ROWS, 4096), B...]
where the time goes in v12:
time: 90 us; the launch traced here: 89.9 us
  Pallas kernels  89.1 us (99%)
    pallas_call x1, Pallas kernels, on_device(): pl.pallas_call(kernel, out_shape=(jax.ShapeDtypeStruct((1, ROWS, 4096), B...  87 us
    pallas_call x1, Pallas kernels, on_device(): pl.pallas_call(copy_out, out_shape=tuple((jax.ShapeDtypeStruct(r.shape, r...  2.1 us

profile of v12, /device:TPU:1, one launch (start us, length us, event | category | flops | bytes accessed | tf_op | source)
XLA Modules:
  0.0 89.9 jit_solution(15816200580224811807)
XLA Ops:
  0.6 87.0 %shard_map.121 = (bf16[1,128,4096]{2,1,0:T(8,128)(2,1)}, f32[1,64,512]{2,1,0:T(8,128)}, f32[1,64,512]{2,1,0:T(8,128)}) custom-call(bf16[1,128,4096]{2,1,0:T(8,128)(2,1)} %q_ref.1, bf16[1,128,512]{2,1,0:T(8,128)(2,1)} %rk_ref.1, bf16[1,128,512]{2,1,0:T(8,128)(2,1)} %rv_ref.1, bf16[1,64,512]{2,1,0:T(8,128)(2,1)} %pk_ref.1, bf16[1,64,512]{2,1,0:T(8,128)(2,1)} %pv_ref.1, ...), custom_call_target="tpu_custom_call" | custom-call | flops 10000000000 | bytes 8388608 | tf_op jit(solution)/shard_map/pallas_call | solution.py:567
  87.7 2.1 %shard_map.122 = (bf16[1,128,4096]{2,1,0:T(8,128)(2,1)}, f32[1,64,512]{2,1,0:T(8,128)}, f32[1,64,512]{2,1,0:T(8,128)}) custom-call(bf16[1,128,4096]{2,1,0:T(8,128)(2,1)} %get-tuple-element.6.refs_0_, f32[1,64,512]{2,1,0:T(8,128)} %get-tuple-element.7.refs_1_, f32[1,64,512]{2,1,0:T(8,128)} %get-tuple-element.8.refs_2_), custom_call_target="tpu_custom_call" | custom-call | tf_op jit(solution)/shard_map/pallas_call | solution.py:620
